TPU v7x, 512 devices: a whole 4x8x8 slice. The times are simulated.
512 devices in a mesh: fsdp: 32 (over z, x_hi, core), tensor: 16 (over x_lo, y).
Axes of the slice: x: 4 (x_hi: 2, x_lo: 2; x = x_hi * 2 + x_lo), y: 8, z: 8, core: 2. Of those that a mesh axis runs over, the one named last changes fastest.
Arguments:
- tokens: bfloat16 [352, 8192], P('fsdp', 'tensor'), may hold values from -6 to 6
- cotangent: bfloat16 [352, 8192], P('fsdp', 'tensor'), may hold values from -3 to 3
- gate_weight: bfloat16 [8192, 14336], P('fsdp', 'tensor'), may hold values from -0.0625 to 0.0625
- up_weight: bfloat16 [8192, 14336], P('fsdp', 'tensor'), may hold values from -0.0625 to 0.0625
- down_weight: bfloat16 [14336, 8192], P('tensor', 'fsdp'), may hold values from -0.046875 to 0.046875
Outputs:
- grad_tokens: bfloat16 [352, 8192], P('fsdp', 'tensor')
- grad_gate: bfloat16 [8192, 14336], P('fsdp', 'tensor')
- grad_up: bfloat16 [8192, 14336], P('fsdp', 'tensor')
- grad_down: bfloat16 [14336, 8192], P('tensor', 'fsdp')
All inputs are finite; a program needn't handle non-finite values.
Results may differ from a plain program's by a relative error of at most 0.0049.
Values may be sent and summed in bfloat16 or wider, within the bound.
No kernel may reach another device: no remote copies, remote signals or barrier semaphores. Data moves between devices by JAX's collectives and lax.ppermute only.
A program may use at most 64 MiB of HBM per device.

v0:
```python
import jax
import jax.numpy as jnp
from jax import lax
from jax.sharding import PartitionSpec as P


def activations(gate, up, back):
    logistic = jax.nn.sigmoid(gate)
    hidden = (gate * logistic * up).astype(jnp.bfloat16)
    grad_gate_act = (back * up * logistic * (1.0 + gate * (1.0 - logistic))).astype(jnp.bfloat16)
    grad_up_act = (back * gate * logistic).astype(jnp.bfloat16)
    return (hidden, grad_gate_act, grad_up_act)


def per_device(tokens, cotangent, gate_weight, up_weight, down_weight):
    full_rows = (
        lax.all_gather(tokens, "tensor", axis=1, tiled=True),
        lax.all_gather(cotangent, "tensor", axis=1, tiled=True),
    )
    tok_cols, back_cols = (
        lax.all_to_all(full_rows[0], "fsdp", split_axis=1, concat_axis=0, tiled=True),
        lax.all_to_all(full_rows[1], "fsdp", split_axis=1, concat_axis=0, tiled=True),
    )
    contract_cols = (((1,), (1,)), ((), ()))
    contract_rows = (((0,), (0,)), ((), ()))
    gate_part = jnp.dot(tok_cols, gate_weight, preferred_element_type=jnp.float32)
    up_part = jnp.dot(tok_cols, up_weight, preferred_element_type=jnp.float32)
    back_part = lax.dot_general(
        back_cols, down_weight, contract_cols, preferred_element_type=jnp.float32
    )
    gate, up, back = lax.psum((gate_part, up_part, back_part), "fsdp")
    hidden, grad_gate_act, grad_up_act = activations(gate, up, back)
    grad_down = lax.dot_general(
        hidden, back_cols, contract_rows, preferred_element_type=jnp.float32
    ).astype(jnp.bfloat16)
    grad_gate = lax.dot_general(
        tok_cols, grad_gate_act, contract_rows, preferred_element_type=jnp.float32
    ).astype(jnp.bfloat16)
    grad_up = lax.dot_general(
        tok_cols, grad_up_act, contract_rows, preferred_element_type=jnp.float32
    ).astype(jnp.bfloat16)
    partial_grad = lax.dot_general(
        grad_gate_act, gate_weight, contract_cols, preferred_element_type=jnp.float32
    )
    partial_grad = partial_grad + lax.dot_general(
        grad_up_act, up_weight, contract_cols, preferred_element_type=jnp.float32
    )
    owned_rows = lax.all_to_all(partial_grad, "fsdp", split_axis=0, concat_axis=1, tiled=True)
    grad_tokens = lax.psum_scatter(owned_rows, "tensor", scatter_dimension=1, tiled=True).astype(
        jnp.bfloat16
    )
    return (grad_tokens, grad_gate, grad_up, grad_down)


def solution(mesh):
    return jax.shard_map(
        per_device,
        mesh=mesh,
        in_specs=(
            P("fsdp", "tensor"),
            P("fsdp", "tensor"),
            P("fsdp", "tensor"),
            P("fsdp", "tensor"),
            P("tensor", "fsdp"),
        ),
        out_specs=(
            P("fsdp", "tensor"),
            P("fsdp", "tensor"),
            P("fsdp", "tensor"),
            P("tensor", "fsdp"),
        ),
        check_vma=False,
    )
```

profile of v0, /device:TPU:6, one launch (start us, length us, event | category | flops | bytes accessed | tf_op | source)
XLA Modules:
  0.0 500.2 jit_solution(6802551115889351062)
XLA Ops:
  7.2 35.0 %all_gather.7 = bf16[11,8192]{1,0:T(8,128)(2,1)S(1)} all-gather(bf16[11,512]{1,0:T(8,128)(2,1)} %param.5), channel_id=1, replica_groups=mesh['fsdp'=32,'tensor'=16] {'tensor'}, dimensions={1}, use_global_device_ids=true | all-gather | bytes 191488 | tf_op jit(solution)/shard_map/all_gather | solution.py:17
  42.3 0.8 copy.17
  43.1 13.4 %all-to-all-start.1 = ((bf16[11,32,256]{2,0,1:T(8,128)(2,1)}), bf16[11,32,256]{2,0,1:T(8,128)(2,1)S(1)}, u32[]{:S(2)}, u32[]{:S(2)}) async-start(bf16[11,32,256]{2,0,1:T(8,128)(2,1)} %copy.17), calls=%async_computation.1 | async-start | bytes 524288 | tf_op jit(solution)/shard_map/all_to_all | solution.py:21
  56.6 31.0 %all_gather.6 = bf16[11,8192]{1,0:T(8,128)(2,1)S(1)} all-gather(bf16[11,512]{1,0:T(8,128)(2,1)S(1)} %copy-done.4), channel_id=1, replica_groups=mesh['fsdp'=32,'tensor'=16] {'tensor'}, dimensions={1}, use_global_device_ids=true | all-gather | bytes 191488 | tf_op jit(solution)/shard_map/all_gather | solution.py:18
  87.6 0.8 copy.16
  88.5 9.9 %all-to-all-start = ((bf16[11,32,256]{2,0,1:T(8,128)(2,1)}), bf16[11,32,256]{2,0,1:T(8,128)(2,1)S(1)}, u32[]{:S(2)}, u32[]{:S(2)}) async-start(bf16[11,32,256]{2,0,1:T(8,128)(2,1)} %copy.16), calls=%async_computation | async-start | bytes 524288 | tf_op jit(solution)/shard_map/all_to_all | solution.py:22
  98.5 11.9 %all-to-all-done = bf16[11,32,256]{2,0,1:T(8,128)(2,1)S(1)} async-done(((bf16[11,32,256]{2,0,1:T(8,128)(2,1)}), bf16[11,32,256]{2,0,1:T(8,128)(2,1)S(1)}, u32[]{:S(2)}, u32[]{:S(2)}) %all-to-all-start) | async-done | bytes 180256 | tf_op jit(solution)/shard_map/all_to_all | solution.py:22
  110.6 1.4 fusion.5
  112.0 1.4 fusion.4
  113.4 1.5 fusion.3
  114.9 273.9 %all-reduce.3.cloned.1.call-done = (f32[352,896]{1,0:T(8,128)}, f32[352,896]{1,0:T(8,128)}, f32[352,896]{1,0:T(8,128)}) async-done(((f32[352,896]{1,0:T(8,128)}, f32[352,896]{1,0:T(8,128)}, f32[352,896]{1,0:T(8,128)}), (f32[352,896]{1,0:T(8,128)}, f32[352,896]{1,0:T(8,128)}, f32[352,896]{1,0:T(8,128)})) %all-reduce.3.cloned.1.call-update) | async-done | bytes 3784720 | tf_op jit(solution)/shard_map/psum | solution.py:31
  388.9 2.7 multiply_convert_fusion.1
  391.5 0.4 fusion.6
  391.9 0.4 convolution_add_fusion
  392.4 30.6 %all_to_all.57 = f32[32,11,256]{2,1,0:T(8,128)S(1)} all-to-all(f32[32,11,256]{2,1,0:T(8,128)S(1)} %all_to_all.50), channel_id=1, replica_groups=mesh['fsdp'=32,'tensor'=16] {'fsdp'}, dimensions={0} | all-to-all | bytes 720896 | tf_op jit(solution)/shard_map/all_to_all | solution.py:48
  422.9 0.2 copy.18
  423.2 1.1 copy.23
  424.3 0.4 fusion
  424.8 1.0 copy.19
  425.7 0.4 fusion.1
  426.2 1.0 copy.20
  427.2 2.6 convolution_convert_fusion
  429.8 62.2 %reduce-scatter.2.cloned.1.call-done = f32[11,512]{1,0:T(8,128)} async-done(((f32[11,8192]{1,0:T(8,128)}), f32[11,512]{1,0:T(8,128)}) %reduce-scatter.2.cloned.1.call-update) | async-done | bytes 22544 | tf_op jit(solution)/shard_map/reduce_scatter | solution.py:49
  492.0 1.4 convert_element_type.29
  (23 shorter events, 0.5 us)
Async XLA Ops:
  7.2 103.4 %copy-start = (bf16[256,896]{1,0:T(8,128)(2,1)S(1)}, bf16[256,896]{1,0:T(8,128)(2,1)}, u32[]{:S(2)}) copy-start(bf16[256,896]{1,0:T(8,128)(2,1)} %param.7) | copy-start | bytes 1376260
  7.2 49.4 %copy-start.4 = (bf16[11,512]{1,0:T(8,128)(2,1)S(1)}, bf16[11,512]{1,0:T(8,128)(2,1)}, u32[]{:S(2)}) copy-start(bf16[11,512]{1,0:T(8,128)(2,1)} %param.6) | copy-start | bytes 33796
  43.1 45.4 %all-to-all-start.1 = ((bf16[11,32,256]{2,0,1:T(8,128)(2,1)}), bf16[11,32,256]{2,0,1:T(8,128)(2,1)S(1)}, u32[]{:S(2)}, u32[]{:S(2)}) async-start(bf16[11,32,256]{2,0,1:T(8,128)(2,1)} %copy.17), calls=%async_computation.1 | async-start | bytes 524288 | tf_op jit(solution)/shard_map/all_to_all | solution.py:21
  88.5 22.0 %all-to-all-start = ((bf16[11,32,256]{2,0,1:T(8,128)(2,1)}), bf16[11,32,256]{2,0,1:T(8,128)(2,1)S(1)}, u32[]{:S(2)}, u32[]{:S(2)}) async-start(bf16[11,32,256]{2,0,1:T(8,128)(2,1)} %copy.16), calls=%async_computation | async-start | bytes 524288 | tf_op jit(solution)/shard_map/all_to_all | solution.py:22
  98.4 290.5 %all-reduce.3.cloned.1.call-start = ((), (), s32[]{:S(2)}) async-start(), calls=%async_computation.5 | async-start | bytes 7569408 | tf_op jit(solution)/shard_map/psum | solution.py:31
  98.5 13.5 %copy-start.1 = (bf16[256,896]{1,0:T(8,128)(2,1)S(1)}, bf16[256,896]{1,0:T(8,128)(2,1)}, u32[]{:S(2)}) copy-start(bf16[256,896]{1,0:T(8,128)(2,1)} %param.8) | copy-start | bytes 1376260
  112.0 1.4 copy-start.3
  114.9 377.1 %reduce-scatter.2.cloned.1.call-start = ((), (), s32[]{:S(2)}) async-start(), calls=%async_computation.4 | async-start | bytes 557056 | tf_op jit(solution)/shard_map/reduce_scatter | solution.py:49
  425.7 1.4 copy-start.2
Sparse Core Ops, SparseCore 0:
  115.0 273.8 all-reduce.2
  424.4 67.5 reduce-scatter.1
where the time goes:
time: 501 us; the launch traced here: 500 us
  waiting for transfers between devices  348 us (69%)
  blocking collectives  96.6 us (19%)
  starting transfers between devices  23.4 us (5%)
  between operations  14.2 us (3%)
  matrix products  8.56 us (2%)
  local copies, waits for them, and re-layouts  5.3 us (1%)
    psum x1, waiting for transfers between devices, per_device(): gate, up, back = lax.psum((gate_part, up_part, back_part), 'fsdp')  274 us
    reduce_scatter x1, waiting for transfers between devices, per_device(): lax.psum_scatter(owned_rows, 'tensor', scatter_dimension=1, tiled=True)  62.2 us
    all_gather x1, blocking collectives, per_device(): lax.all_gather(tokens, 'tensor', axis=1, tiled=True)  35 us
    all_gather x1, blocking collectives, per_device(): lax.all_gather(cotangent, 'tensor', axis=1, tiled=True)  31 us
    all_to_all x1, blocking collectives, per_device(): lax.all_to_all(partial_grad, 'fsdp', split_axis=0, concat_axis=1, tiled=T...  30.6 us
    all_to_all x1, starting transfers between devices, per_device(): lax.all_to_all(full_rows[0], 'fsdp', split_axis=1, concat_axis=0, tiled=T...  13.4 us
    all_to_all x1, waiting for transfers between devices, per_device(): lax.all_to_all(full_rows[1], 'fsdp', split_axis=1, concat_axis=0, tiled=T...  11.9 us
  transfers between devices with their start and end apart: 4, of which 3 were waited for; matrix products, arithmetic and copies ran while one was open for 1% of the time, Pallas kernels for 0%

commit v1 on v0

v1 whole, which is shorter than its diff:
```python
import functools

import jax
import jax.numpy as jnp
from jax import lax
from jax.experimental import pallas as pl
from jax.experimental.pallas import tpu as pltpu
from jax.sharding import Mesh
from jax.sharding import PartitionSpec as P

F32, BF16 = jnp.float32, jnp.bfloat16
ALL = ("z", "xh", "core", "xl", "y")
FSDP = ("z", "xh", "core")
TENSOR = ("xl", "y")
CHIPS = ("z", "xh")

ROWS, HALF = 11, 176
UP, ACROSS, PER = 11, 7, 5
VMEM = pl.BlockSpec(memory_space=pltpu.VMEM)
SMEM = pl.BlockSpec(memory_space=pltpu.SMEM)
PARAMS = pltpu.CompilerParams(vmem_limit_bytes=40 * 1024 * 1024)


def call(kernel, out_shape, inputs, scratch=(), specs=None, flops=0):
    moved = sum(x.size * x.dtype.itemsize for x in inputs)
    moved += sum(s.size * s.dtype.itemsize for s in jax.tree.leaves(out_shape))
    return pl.pallas_call(
        kernel,
        out_shape=out_shape,
        in_specs=specs or [VMEM] * len(inputs),
        out_specs=jax.tree.map(lambda _: VMEM, out_shape),
        scratch_shapes=list(scratch),
        compiler_params=PARAMS,
        cost_estimate=pl.CostEstimate(flops=flops, bytes_accessed=moved, transcendentals=0),
    )(*inputs)


def shape(*dims, dtype=BF16):
    return jax.ShapeDtypeStruct(dims, dtype)


def tile(ref_or_value, j):
    return ref_or_value[:, j * 128 : (j + 1) * 128]


def pack_kernel(core, tok, cot, out, wide):
    odd = core[0] == 1
    for base, ref in ((0, tok), (4, cot)):
        rows = ref[...].astype(F32)
        for j in range(4):
            piece = jnp.where(odd, tile(rows, (j + 2) % 4), tile(rows, j))
            wide[pl.ds(base + j, ROWS, stride=8), :] = piece
    out[...] = wide[...].astype(BF16)


def put_tiles(out, m, value):
    for i in range(UP):
        for j in range(ACROSS):
            dest, slot = divmod(i * ACROSS + j, PER)
            row = (m * PER + slot) * 16
            out[dest, row : row + 16, :] = value[i * 16 : (i + 1) * 16, j * 128 : (j + 1) * 128]


def get_tiles(ref, m, out, first):
    for i in range(UP):
        for j in range(ACROSS):
            source, slot = divmod(i * ACROSS + j, PER)
            row = (m * PER + slot) * 16
            out[first + i * 16 : first + (i + 1) * 16, j * 128 : (j + 1) * 128] = ref[source, row : row + 16, :]


def forward_kernel(
    rows, gate_own, gate_oth, up_own, up_oth, down_own, down_oth, parts, x_own, x_oth, wide
):
    for t in range(16):
        wide[t * 88 : (t + 1) * 88, :] = rows[t].astype(F32)
    for j, (ref, at) in enumerate(
        ((x_own, 0), (x_own, 1), (x_oth, 0), (x_oth, 1), (x_own, 2), (x_own, 3), (x_oth, 2), (x_oth, 3))
    ):
        ref[:, at * 128 : (at + 1) * 128] = wide[pl.ds(j, HALF, stride=8), :].astype(BF16)
    by_cols = (((1,), (0,)), ((), ()))
    by_rows = (((1,), (1,)), ((), ()))
    for m, (own, oth, cols, dims) in enumerate(
        (
            (gate_own, gate_oth, slice(0, 256), by_cols),
            (up_own, up_oth, slice(0, 256), by_cols),
            (down_own, down_oth, slice(256, 512), by_rows),
        )
    ):
        total = lax.dot_general(x_own[:, cols], own[...], dims, preferred_element_type=F32)
        total = total + lax.dot_general(x_oth[:, cols], oth[...], dims, preferred_element_type=F32)
        put_tiles(parts, m, total.astype(BF16))
        parts[15, (m * PER + 2) * 16 : (m + 1) * PER * 16, :] = jnp.zeros((48, 128), BF16)


def activation_kernel(parts, grads, hiddens):
    size = PER * 16
    total = parts[0].astype(F32)
    for i in range(1, 16):
        total = total + parts[i].astype(F32)
    gate, up, back = total[:size], total[size : 2 * size], total[2 * size :]
    logistic = jax.nn.sigmoid(gate)
    hidden = (gate * logistic * up).astype(BF16)
    grad_gate_act = (back * up * logistic * (1.0 + gate * (1.0 - logistic))).astype(BF16)
    grad_up_act = (back * gate * logistic).astype(BF16)
    for i in range(16):
        grads[i, :size, :] = grad_gate_act
        grads[i, size:, :] = grad_up_act
        hiddens[i] = hidden


def token_grad_kernel(grads, gate_own, gate_oth, up_own, up_oth, out, gate_act, up_act, total, wide):
    get_tiles(grads, 0, gate_act, 0)
    get_tiles(grads, 1, up_act, 0)
    dims = (((1,), (1,)), ((), ()))
    for at, gate_weight, up_weight in ((0, gate_own, up_own), (256, gate_oth, up_oth)):
        part = lax.dot_general(gate_act[...], gate_weight[...], dims, preferred_element_type=F32)
        part = part + lax.dot_general(up_act[...], up_weight[...], dims, preferred_element_type=F32)
        total[:, at : at + 256] = part
    for t in range(16):
        for j in range(4):
            wide[j * ROWS : (j + 1) * ROWS, :] = total[t * ROWS : (t + 1) * ROWS, j * 128 : (j + 1) * 128]
        out[t] = wide[...].astype(BF16)


def token_sum_kernel(core, parts, out, total):
    odd = core[0] == 1
    acc = parts[0].astype(F32)
    for t in range(1, 16):
        acc = acc + parts[t].astype(F32)
    total[...] = acc
    for j in range(4):
        here = total[j * ROWS : (j + 1) * ROWS, :]
        there = total[(j + 2) % 4 * ROWS : ((j + 2) % 4 + 1) * ROWS, :]
        out[:, j * 128 : (j + 1) * 128] = jnp.where(odd, there, here).astype(BF16)


def weight_grad_kernel(
    x_own, x_got, grads, grads_got, hiddens, hiddens_got, grad_gate, grad_up, grad_down, x_all, act
):
    contract_rows = (((0,), (0,)), ((), ()))
    x_all[:HALF, :] = x_own[...]
    x_all[HALF:, :] = x_got[...]
    for m, (mine, got, out) in enumerate(((grads, grads_got, grad_gate), (grads, grads_got, grad_up))):
        get_tiles(mine, m, act, 0)
        get_tiles(got, m, act, HALF)
        out[...] = lax.dot_general(
            x_all[:, :256], act[...], contract_rows, preferred_element_type=F32
        ).astype(BF16)
    get_tiles(hiddens, 0, act, 0)
    get_tiles(hiddens_got, 0, act, HALF)
    grad_down[...] = lax.dot_general(
        act[...], x_all[:, 256:], contract_rows, preferred_element_type=F32
    ).astype(BF16)


def swap_cores(x):
    return lax.ppermute(x, "core", [(0, 1), (1, 0)])


def per_device(tokens, cotangent, gate_weight, up_weight, down_weight):
    core = jnp.reshape(lax.axis_index("core"), (1,)).astype(jnp.int32)
    there = [(f * 16 + t, (2 * t + f % 2) * 16 + f // 2) for f in range(32) for t in range(16)]
    home = [(b, a) for a, b in there]

    packed = call(
        pack_kernel,
        shape(88, 128),
        (core, tokens, cotangent),
        [pltpu.VMEM((88, 128), F32)],
        specs=[SMEM, VMEM, VMEM],
    )
    packed = lax.ppermute(packed, ALL, there)
    gate_oth, up_oth, down_oth = swap_cores(gate_weight), swap_cores(up_weight), swap_cores(down_weight)
    rows = lax.all_to_all(jnp.broadcast_to(packed[None], (16, 88, 128)), TENSOR, 0, 0, tiled=True)

    parts, x_own, x_oth = call(
        forward_kernel,
        (shape(16, 3 * PER * 16, 128), shape(HALF, 512), shape(HALF, 512)),
        (rows, gate_weight, gate_oth, up_weight, up_oth, down_weight, down_oth),
        [pltpu.VMEM((16 * 88, 128), F32)],
        flops=6 * HALF * 512 * 896,
    )
    parts = lax.all_to_all(parts, CHIPS, 0, 0, tiled=True)
    x_got = swap_cores(x_oth)

    grads, hiddens = call(
        activation_kernel,
        (shape(16, 2 * PER * 16, 128), shape(16, PER * 16, 128)),
        (parts,),
    )
    grads = lax.all_to_all(grads, CHIPS, 0, 0, tiled=True)
    hiddens = lax.all_to_all(hiddens, CHIPS, 0, 0, tiled=True)

    token_parts = call(
        token_grad_kernel,
        shape(16, 4 * ROWS, 128),
        (grads, gate_weight, gate_oth, up_weight, up_oth),
        [
            pltpu.VMEM((HALF, 896), BF16),
            pltpu.VMEM((HALF, 896), BF16),
            pltpu.VMEM((HALF, 512), F32),
            pltpu.VMEM((4 * ROWS, 128), F32),
        ],
        flops=4 * HALF * 512 * 896,
    )
    token_parts = lax.all_to_all(token_parts, TENSOR, 0, 0, tiled=True)
    grads_got, hiddens_got = swap_cores(grads), swap_cores(hiddens)

    grad_tokens = call(
        token_sum_kernel,
        shape(ROWS, 512),
        (core, token_parts),
        [pltpu.VMEM((4 * ROWS, 128), F32)],
        specs=[SMEM, VMEM],
    )
    grad_tokens = lax.ppermute(grad_tokens, ALL, home)

    grad_gate, grad_up, grad_down = call(
        weight_grad_kernel,
        (shape(256, 896), shape(256, 896), shape(896, 256)),
        (x_own, x_got, grads, grads_got, hiddens, hiddens_got),
        [pltpu.VMEM((2 * HALF, 512), BF16), pltpu.VMEM((2 * HALF, 896), BF16)],
        flops=6 * 2 * HALF * 256 * 896,
    )
    return (grad_tokens, grad_gate, grad_up, grad_down)


def solution(mesh):
    chips = Mesh(mesh.devices.reshape(8, 2, 2, 2, 8), ALL)
    rows, cols = P(FSDP, TENSOR), P(TENSOR, FSDP)
    return jax.shard_map(
        per_device,
        mesh=chips,
        in_specs=(rows, rows, rows, rows, cols),
        out_specs=(rows, rows, rows, cols),
        check_vma=False,
    )
```

time: 501 us -> 149 us (0.30)
  waiting for transfers between devices: 348 us -> 21.3 us
  blocking collectives: 96.6 us -> 59.6 us
  starting transfers between devices: 23.4 us -> 57.1 us
  between operations: 14.2 us -> 0.82 us
  matrix products: 8.56 us -> 0 us
  Pallas kernels: 0 us -> 5.16 us
    psum x1 -> x0, waiting for transfers between devices: 274 us -> none  [per_device(): gate, up, back = lax.psum((gate_part, up_part, back_part), 'fsdp')]
    all_gather x2 -> x0, blocking collectives: 66 us -> none  [the longest x1 35 us: per_device(): lax.all_gather(tokens, 'tensor', axis=1, tiled=True)]
    reduce_scatter x1 -> x0, waiting for transfers between devices: 62.2 us -> none  [per_device(): lax.psum_scatter(owned_rows, 'tensor', scatter_dimension=1, tiled=True)]
    ppermute x0 -> x8, starting transfers between devices: none -> 30.9 us  [the longest x6 12.6 us: swap_cores(): return lax.ppermute(x, 'core', [(0, 1), (1, 0)])]
    all_to_all x1 -> x2, blocking collectives: 30.6 us -> 59.6 us  [the longest x1 36.4 us: per_device(): parts = lax.all_to_all(parts, CHIPS, 0, 0, tiled=True)]
    ppermute x0 -> x8, waiting for transfers between devices: none -> 9.75 us  [the longest x1 6.2 us: per_device(): grad_tokens = lax.ppermute(grad_tokens, ALL, home)]
    dot_general x8 -> x0, matrix products: 8.56 us -> none  [the longest x1 2.64 us: per_device(): lax.dot_general(hidden, back_cols, contract_rows, preferred_element_type=...]
    pallas_call x0 -> x6, Pallas kernels: none -> 5.16 us  [call(): pl.pallas_call(kernel, out_shape=out_shape, in_specs=specs or [VMEM] * le...]
  transfers between devices with their start and end apart: 4 -> 11, of which waited for: 3 -> 6; matrix products, arithmetic and copies ran while one was open for 1% -> 0% of each run, Pallas kernels for 0% -> 1%
where the time goes in v1:
time: 149 us; the launch traced here: 148 us
  blocking collectives  59.6 us (40%)
  starting transfers between devices  57.1 us (38%)
  waiting for transfers between devices  21.3 us (14%)
  Pallas kernels  5.16 us (3%)
  local copies, waits for them, and re-layouts  3.86 us (3%)
    all_to_all x1, blocking collectives, per_device(): parts = lax.all_to_all(parts, CHIPS, 0, 0, tiled=True)  36.4 us
    all_to_all x1, blocking collectives, per_device(): grads = lax.all_to_all(grads, CHIPS, 0, 0, tiled=True)  23.3 us
    ppermute x6, starting transfers between devices, swap_cores(): return lax.ppermute(x, 'core', [(0, 1), (1, 0)])  12.6 us
    ppermute x1, starting transfers between devices, per_device(): packed = lax.ppermute(packed, ALL, there)  12 us
    all_to_all x1, starting transfers between devices, per_device(): token_parts = lax.all_to_all(token_parts, TENSOR, 0, 0, tiled=True)  10.9 us
    all_to_all x1, starting transfers between devices, per_device(): lax.all_to_all(jnp.broadcast_to(packed[None], (16, 88, 128)), TENSOR, 0,...  8.95 us
    all_to_all x1, waiting for transfers between devices, per_device(): hiddens = lax.all_to_all(hiddens, CHIPS, 0, 0, tiled=True)  6.56 us
    ppermute x1, starting transfers between devices, per_device(): grad_tokens = lax.ppermute(grad_tokens, ALL, home)  6.35 us
  transfers between devices with their start and end apart: 11, of which 6 were waited for; matrix products, arithmetic and copies ran while one was open for 0% of the time, Pallas kernels for 1%

profile of v1, /device:TPU:6, one launch (start us, length us, event | category | flops | bytes accessed | tf_op | source)
XLA Modules:
  0.0 147.9 jit_solution(5317709017155287840)
XLA Ops:
  2.1 12.0 %collective-permute-start = (bf16[88,128]{1,0:T(8,128)(2,1)S(1)}, bf16[88,128]{1,0:T(8,128)(2,1)S(1)}, u32[]{:S(2)}, u32[]{:S(2)}) collective-permute-start(bf16[88,128]{1,0:T(8,128)(2,1)S(1)} %shard_map.84), channel_id=1, source_target_pairs={{0,0},{1,32},{2,64},{3,96},{4,128},{5,160},{6,192},{7,224},{8,256}... | collective-permute-start | bytes 67592 | tf_op jit(solution)/shard_map/ppermute | solution.py:173
  14.1 1.8 %collective-permute-done = bf16[88,128]{1,0:T(8,128)(2,1)S(1)} collective-permute-done((bf16[88,128]{1,0:T(8,128)(2,1)S(1)}, bf16[88,128]{1,0:T(8,128)(2,1)S(1)}, u32[]{:S(2)}, u32[]{:S(2)}) %collective-permute-start) | collective-permute-done | bytes 22560 | tf_op jit(solution)/shard_map/ppermute | solution.py:173
  16.7 8.9 %all-to-all-start = ((bf16[16,88,128]{2,1,0:T(8,128)(2,1)}), bf16[16,88,128]{2,1,0:T(8,128)(2,1)S(1)}, u32[]{:S(2)}, u32[]{:S(2)}) async-start(bf16[16,88,128]{2,1,0:T(8,128)(2,1)} %broadcast_in_dim.2), calls=%async_computation | async-start | bytes 720896 | tf_op jit(solution)/shard_map/all_to_all | solution.py:175
  25.6 1.9 %collective-permute-start.3 = (bf16[896,256]{1,0:T(8,128)(2,1)}, bf16[896,256]{1,0:T(8,128)(2,1)S(1)}, u32[]{:S(2)}, u32[]{:S(2)}) collective-permute-start(bf16[896,256]{1,0:T(8,128)(2,1)} %down_own.1), channel_id=1, source_target_pairs={{0,16},{16,0},{1,17},{17,1},{2,18},{18,2},{3,19},{19,3},{4,20},{20... | collective-permute-start | bytes 1376264 | tf_op jit(solution)/shard_map/ppermute | solution.py:158
  27.5 2.4 %collective-permute-start.1 = (bf16[256,896]{1,0:T(8,128)(2,1)S(1)}, bf16[256,896]{1,0:T(8,128)(2,1)S(1)}, u32[]{:S(2)}, u32[]{:S(2)}) collective-permute-start(bf16[256,896]{1,0:T(8,128)(2,1)S(1)} %copy-done), channel_id=1, source_target_pairs={{0,16},{16,0},{1,17},{17,1},{2,18},{18,2},{3,19},{19,3},{4,20},{20... | collective-permute-start | bytes 1376264 | tf_op jit(solution)/shard_map/ppermute | solution.py:158
  30.0 1.9 %collective-permute-start.2 = (bf16[256,896]{1,0:T(8,128)(2,1)S(1)}, bf16[256,896]{1,0:T(8,128)(2,1)S(1)}, u32[]{:S(2)}, u32[]{:S(2)}) collective-permute-start(bf16[256,896]{1,0:T(8,128)(2,1)S(1)} %copy-done.1), channel_id=1, source_target_pairs={{0,16},{16,0},{1,17},{17,1},{2,18},{18,2},{3,19},{19,3},{4,20},{20... | collective-permute-start | bytes 1376264 | tf_op jit(solution)/shard_map/ppermute | solution.py:158
  31.9 1.8 %collective-permute-done.2.up_oth = bf16[256,896]{1,0:T(8,128)(2,1)S(1)} collective-permute-done((bf16[256,896]{1,0:T(8,128)(2,1)S(1)}, bf16[256,896]{1,0:T(8,128)(2,1)S(1)}, u32[]{:S(2)}, u32[]{:S(2)}) %collective-permute-start.2) | collective-permute-done | bytes 458784 | tf_op jit(solution)/shard_map/ppermute | solution.py:158
  33.7 1.7 %all-to-all-done.rows = bf16[16,88,128]{2,1,0:T(8,128)(2,1)S(1)} async-done(((bf16[16,88,128]{2,1,0:T(8,128)(2,1)}), bf16[16,88,128]{2,1,0:T(8,128)(2,1)S(1)}, u32[]{:S(2)}, u32[]{:S(2)}) %all-to-all-start) | async-done | bytes 360480 | tf_op jit(solution)/shard_map/all_to_all | solution.py:175
  35.4 1.0 copy-done.2
  36.4 0.9 shard_map.85
  37.3 36.4 %all_to_all.25.parts = bf16[16,240,128]{2,1,0:T(8,128)(2,1)S(1)} all-to-all(bf16[16,240,128]{2,1,0:T(8,128)(2,1)S(1)} %get-tuple-element.12), channel_id=1, replica_groups=mesh['z'=8,'xh'=2,'core'=2,'xl'=2,'y'=8] {'z','xh'}, dimensions={0} | all-to-all | bytes 1966080 | tf_op jit(solution)/shard_map/all_to_all | solution.py:184
  73.7 0.8 shard_map.86
  74.5 23.3 %all_to_all.26.grads = bf16[16,160,128]{2,1,0:T(8,128)(2,1)S(1)} all-to-all(bf16[16,160,128]{2,1,0:T(8,128)(2,1)S(1)} %get-tuple-element.13), channel_id=1, replica_groups=mesh['z'=8,'xh'=2,'core'=2,'xl'=2,'y'=8] {'z','xh'}, dimensions={0} | all-to-all | bytes 1310720 | tf_op jit(solution)/shard_map/all_to_all | solution.py:192
  97.8 6.3 %all-to-all-start.4 = ((bf16[16,80,128]{2,1,0:T(8,128)(2,1)}), bf16[16,80,128]{2,1,0:T(8,128)(2,1)S(1)}, u32[]{:S(2)}, u32[]{:S(2)}) async-start(bf16[16,80,128]{2,1,0:T(8,128)(2,1)} %get-tuple-element.16), calls=%async_computation.4 | async-start | bytes 655360 | tf_op jit(solution)/shard_map/all_to_all | solution.py:193
  104.1 1.9 %collective-permute-start.6 = (bf16[16,160,128]{2,1,0:T(8,128)(2,1)S(1)}, bf16[16,160,128]{2,1,0:T(8,128)(2,1)S(1)}, u32[]{:S(2)}, u32[]{:S(2)}) collective-permute-start(bf16[16,160,128]{2,1,0:T(8,128)(2,1)S(1)} %all_to_all.26.grads), channel_id=1, source_target_pairs={{0,16},{16,0},{1,17},{17,1},{2,18},{18,2},{3,19},{19,3},{4,20},{20... | collective-permute-start | bytes 1966088 | tf_op jit(solution)/shard_map/ppermute | solution.py:158
  106.0 1.5 %shard_map.87 = bf16[16,44,128]{2,1,0:T(8,128)(2,1)} custom-call(bf16[16,160,128]{2,1,0:T(8,128)(2,1)S(1)} %all_to_all.26.grads, bf16[256,896]{1,0:T(8,128)(2,1)S(1)} %copy-done, bf16[256,896]{1,0:T(8,128)(2,1)S(1)} %collective-permute-done.1.gate_oth, bf16[256,896]{1,0:T(8,128)(2,1)S(1)} %copy-done.1, bf16[256,896]{1,0:T(8,128)(2,1)S(1)} %collective-permute-done.2.up_oth), custom_call_target="tpu_custom_call" | custom-call | flops 322961408 | bytes 2670592 | tf_op jit(solution)/shard_map/pallas_call | solution.py:27
  107.5 6.6 %all-to-all-done.4.hiddens = bf16[16,80,128]{2,1,0:T(8,128)(2,1)S(1)} async-done(((bf16[16,80,128]{2,1,0:T(8,128)(2,1)}), bf16[16,80,128]{2,1,0:T(8,128)(2,1)S(1)}, u32[]{:S(2)}, u32[]{:S(2)}) %all-to-all-start.4) | async-done | bytes 327712 | tf_op jit(solution)/shard_map/all_to_all | solution.py:193
  114.1 10.9 %all-to-all-start.3 = ((bf16[16,44,128]{2,1,0:T(8,128)(2,1)}), bf16[16,44,128]{2,1,0:T(8,128)(2,1)S(1)}, u32[]{:S(2)}, u32[]{:S(2)}) async-start(bf16[16,44,128]{2,1,0:T(8,128)(2,1)} %shard_map.87), calls=%async_computation.3 | async-start | bytes 393216 | tf_op jit(solution)/shard_map/all_to_all | solution.py:207
  125.0 2.1 %collective-permute-start.7 = (bf16[16,80,128]{2,1,0:T(8,128)(2,1)S(1)}, bf16[16,80,128]{2,1,0:T(8,128)(2,1)S(1)}, u32[]{:S(2)}, u32[]{:S(2)}) collective-permute-start(bf16[16,80,128]{2,1,0:T(8,128)(2,1)S(1)} %all-to-all-done.4.hiddens), channel_id=1, source_target_pairs={{0,16},{16,0},{1,17},{17,1},{2,18},{18,2},{3,19},{19,3},{4,20},{20... | collective-permute-start | bytes 983048 | tf_op jit(solution)/shard_map/ppermute | solution.py:158
  127.1 2.4 %collective-permute-start.5 = (bf16[176,512]{1,0:T(8,128)(2,1)S(1)}, bf16[176,512]{1,0:T(8,128)(2,1)S(1)}, u32[]{:S(2)}, u32[]{:S(2)}) collective-permute-start(bf16[176,512]{1,0:T(8,128)(2,1)S(1)} %copy-done.8), channel_id=1, source_target_pairs={{0,16},{16,0},{1,17},{17,1},{2,18},{18,2},{3,19},{19,3},{4,20},{20... | collective-permute-start | bytes 540680 | tf_op jit(solution)/shard_map/ppermute | solution.py:158
  129.5 3.3 %all-to-all-done.3.parts = bf16[16,44,128]{2,1,0:T(8,128)(2,1)S(1)} async-done(((bf16[16,44,128]{2,1,0:T(8,128)(2,1)}), bf16[16,44,128]{2,1,0:T(8,128)(2,1)S(1)}, u32[]{:S(2)}, u32[]{:S(2)}) %all-to-all-start.3) | async-done | bytes 180256 | tf_op jit(solution)/shard_map/all_to_all | solution.py:207
  132.8 6.3 %collective-permute-start.4 = (bf16[11,512]{1,0:T(8,128)(2,1)S(1)}, bf16[11,512]{1,0:T(8,128)(2,1)S(1)}, u32[]{:S(2)}, u32[]{:S(2)}) collective-permute-start(bf16[11,512]{1,0:T(8,128)(2,1)S(1)} %shard_map.88), channel_id=1, source_target_pairs={{0,0},{32,1},{64,2},{96,3},{128,4},{160,5},{192,6},{224,7},{256,8}... | collective-permute-start | bytes 33800 | tf_op jit(solution)/shard_map/ppermute | solution.py:217
  139.2 6.2 %collective-permute-done.4 = bf16[11,512]{1,0:T(8,128)(2,1)S(1)} collective-permute-done((bf16[11,512]{1,0:T(8,128)(2,1)S(1)}, bf16[11,512]{1,0:T(8,128)(2,1)S(1)}, u32[]{:S(2)}, u32[]{:S(2)}) %collective-permute-start.4) | collective-permute-done | bytes 11296 | tf_op jit(solution)/shard_map/ppermute | solution.py:217
  145.4 1.9 %shard_map.89 = (bf16[256,896]{1,0:T(8,128)(2,1)}, bf16[256,896]{1,0:T(8,128)(2,1)}, bf16[896,256]{1,0:T(8,128)(2,1)}) custom-call(bf16[176,512]{1,0:T(8,128)(2,1)S(1)} %copy-done.4, bf16[176,512]{1,0:T(8,128)(2,1)S(1)} %collective-permute-done.5.x_got, bf16[16,160,128]{2,1,0:T(8,128)(2,1)S(1)} %all_to_all.26.grads, ...), custom_call_target="tpu_custom_call" | custom-call | flops 484442112 | bytes 3702784 | tf_op jit(solution)/shard_map/pallas_call | solution.py:27
  (26 shorter events, 2.9 us)
Async XLA Ops:
  0.6 0.7 copy-start.5
  1.4 0.7 copy-start.6
  2.1 25.4 %copy-start = (bf16[256,896]{1,0:T(8,128)(2,1)S(1)}, bf16[256,896]{1,0:T(8,128)(2,1)}, u32[]{:S(2)}) copy-start(bf16[256,896]{1,0:T(8,128)(2,1)} %gate_own.3) | copy-start | bytes 1376260
  2.1 27.9 %copy-start.1 = (bf16[256,896]{1,0:T(8,128)(2,1)S(1)}, bf16[256,896]{1,0:T(8,128)(2,1)}, u32[]{:S(2)}) copy-start(bf16[256,896]{1,0:T(8,128)(2,1)} %up_own.3) | copy-start | bytes 1376260
  2.1 13.8 %collective-permute-start = (bf16[88,128]{1,0:T(8,128)(2,1)S(1)}, bf16[88,128]{1,0:T(8,128)(2,1)S(1)}, u32[]{:S(2)}, u32[]{:S(2)}) collective-permute-start(bf16[88,128]{1,0:T(8,128)(2,1)S(1)} %shard_map.84), channel_id=1, source_target_pairs={{0,0},{1,32},{2,64},{3,96},{4,128},{5,160},{6,192},{7,224},{8,256}... | collective-permute-start | bytes 67592 | tf_op jit(solution)/shard_map/ppermute | solution.py:173
  16.7 18.7 %all-to-all-start = ((bf16[16,88,128]{2,1,0:T(8,128)(2,1)}), bf16[16,88,128]{2,1,0:T(8,128)(2,1)S(1)}, u32[]{:S(2)}, u32[]{:S(2)}) async-start(bf16[16,88,128]{2,1,0:T(8,128)(2,1)} %broadcast_in_dim.2), calls=%async_computation | async-start | bytes 720896 | tf_op jit(solution)/shard_map/all_to_all | solution.py:175
  25.6 6.3 %collective-permute-start.3 = (bf16[896,256]{1,0:T(8,128)(2,1)}, bf16[896,256]{1,0:T(8,128)(2,1)S(1)}, u32[]{:S(2)}, u32[]{:S(2)}) collective-permute-start(bf16[896,256]{1,0:T(8,128)(2,1)} %down_own.1), channel_id=1, source_target_pairs={{0,16},{16,0},{1,17},{17,1},{2,18},{18,2},{3,19},{19,3},{4,20},{20... | collective-permute-start | bytes 1376264 | tf_op jit(solution)/shard_map/ppermute | solution.py:158
  27.5 4.4 %collective-permute-start.1 = (bf16[256,896]{1,0:T(8,128)(2,1)S(1)}, bf16[256,896]{1,0:T(8,128)(2,1)S(1)}, u32[]{:S(2)}, u32[]{:S(2)}) collective-permute-start(bf16[256,896]{1,0:T(8,128)(2,1)S(1)} %copy-done), channel_id=1, source_target_pairs={{0,16},{16,0},{1,17},{17,1},{2,18},{18,2},{3,19},{19,3},{4,20},{20... | collective-permute-start | bytes 1376264 | tf_op jit(solution)/shard_map/ppermute | solution.py:158
  30.0 3.7 %collective-permute-start.2 = (bf16[256,896]{1,0:T(8,128)(2,1)S(1)}, bf16[256,896]{1,0:T(8,128)(2,1)S(1)}, u32[]{:S(2)}, u32[]{:S(2)}) collective-permute-start(bf16[256,896]{1,0:T(8,128)(2,1)S(1)} %copy-done.1), channel_id=1, source_target_pairs={{0,16},{16,0},{1,17},{17,1},{2,18},{18,2},{3,19},{19,3},{4,20},{20... | collective-permute-start | bytes 1376264 | tf_op jit(solution)/shard_map/ppermute | solution.py:158
  35.4 1.0 copy-start.2
  37.3 36.4 %copy-start.3 = (bf16[176,512]{1,0:T(8,128)(2,1)}, bf16[176,512]{1,0:T(8,128)(2,1)S(1)}, u32[]{:S(2)}) copy-start(bf16[176,512]{1,0:T(8,128)(2,1)S(1)} %get-tuple-element.14.x_own) | copy-start | bytes 540676
  37.3 36.4 %copy-start.7 = (bf16[176,512]{1,0:T(8,128)(2,1)}, bf16[176,512]{1,0:T(8,128)(2,1)S(1)}, u32[]{:S(2)}) copy-start(bf16[176,512]{1,0:T(8,128)(2,1)S(1)} %get-tuple-element.15) | copy-start | bytes 540676
  97.8 16.3 %all-to-all-start.4 = ((bf16[16,80,128]{2,1,0:T(8,128)(2,1)}), bf16[16,80,128]{2,1,0:T(8,128)(2,1)S(1)}, u32[]{:S(2)}, u32[]{:S(2)}) async-start(bf16[16,80,128]{2,1,0:T(8,128)(2,1)} %get-tuple-element.16), calls=%async_computation.4 | async-start | bytes 655360 | tf_op jit(solution)/shard_map/all_to_all | solution.py:193
  104.1 41.3 %collective-permute-start.6 = (bf16[16,160,128]{2,1,0:T(8,128)(2,1)S(1)}, bf16[16,160,128]{2,1,0:T(8,128)(2,1)S(1)}, u32[]{:S(2)}, u32[]{:S(2)}) collective-permute-start(bf16[16,160,128]{2,1,0:T(8,128)(2,1)S(1)} %all_to_all.26.grads), channel_id=1, source_target_pairs={{0,16},{16,0},{1,17},{17,1},{2,18},{18,2},{3,19},{19,3},{4,20},{20... | collective-permute-start | bytes 1966088 | tf_op jit(solution)/shard_map/ppermute | solution.py:158
  107.5 19.6 %copy-start.8 = (bf16[176,512]{1,0:T(8,128)(2,1)S(1)}, bf16[176,512]{1,0:T(8,128)(2,1)}, u32[]{:S(2)}) copy-start(bf16[176,512]{1,0:T(8,128)(2,1)} %copy-done.7) | copy-start | bytes 540676
  114.1 18.7 %all-to-all-start.3 = ((bf16[16,44,128]{2,1,0:T(8,128)(2,1)}), bf16[16,44,128]{2,1,0:T(8,128)(2,1)S(1)}, u32[]{:S(2)}, u32[]{:S(2)}) async-start(bf16[16,44,128]{2,1,0:T(8,128)(2,1)} %shard_map.87), calls=%async_computation.3 | async-start | bytes 393216 | tf_op jit(solution)/shard_map/all_to_all | solution.py:207
  125.0 20.4 %copy-start.4 = (bf16[176,512]{1,0:T(8,128)(2,1)S(1)}, bf16[176,512]{1,0:T(8,128)(2,1)}, u32[]{:S(2)}) copy-start(bf16[176,512]{1,0:T(8,128)(2,1)} %copy-done.3) | copy-start | bytes 540676
  125.0 20.4 %collective-permute-start.7 = (bf16[16,80,128]{2,1,0:T(8,128)(2,1)S(1)}, bf16[16,80,128]{2,1,0:T(8,128)(2,1)S(1)}, u32[]{:S(2)}, u32[]{:S(2)}) collective-permute-start(bf16[16,80,128]{2,1,0:T(8,128)(2,1)S(1)} %all-to-all-done.4.hiddens), channel_id=1, source_target_pairs={{0,16},{16,0},{1,17},{17,1},{2,18},{18,2},{3,19},{19,3},{4,20},{20... | collective-permute-start | bytes 983048 | tf_op jit(solution)/shard_map/ppermute | solution.py:158
  127.1 18.3 %collective-permute-start.5 = (bf16[176,512]{1,0:T(8,128)(2,1)S(1)}, bf16[176,512]{1,0:T(8,128)(2,1)S(1)}, u32[]{:S(2)}, u32[]{:S(2)}) collective-permute-start(bf16[176,512]{1,0:T(8,128)(2,1)S(1)} %copy-done.8), channel_id=1, source_target_pairs={{0,16},{16,0},{1,17},{17,1},{2,18},{18,2},{3,19},{19,3},{4,20},{20... | collective-permute-start | bytes 540680 | tf_op jit(solution)/shard_map/ppermute | solution.py:158
  132.8 12.6 %collective-permute-start.4 = (bf16[11,512]{1,0:T(8,128)(2,1)S(1)}, bf16[11,512]{1,0:T(8,128)(2,1)S(1)}, u32[]{:S(2)}, u32[]{:S(2)}) collective-permute-start(bf16[11,512]{1,0:T(8,128)(2,1)S(1)} %shard_map.88), channel_id=1, source_target_pairs={{0,0},{32,1},{64,2},{96,3},{128,4},{160,5},{192,6},{224,7},{256,8}... | collective-permute-start | bytes 33800 | tf_op jit(solution)/shard_map/ppermute | solution.py:217

commit v2 on v1

v2 whole, which is shorter than its diff:
```python
import functools

import jax
import jax.numpy as jnp
from jax import lax
from jax.experimental import pallas as pl
from jax.experimental.pallas import tpu as pltpu
from jax.sharding import Mesh
from jax.sharding import PartitionSpec as P

F32, BF16 = jnp.float32, jnp.bfloat16
ALL = ("z", "xh", "core", "xl", "y")
FSDP = ("z", "xh", "core")
TENSOR = ("xl", "y")

ROWS, QUARTER, PADDED = 11, 88, 96
UP, ACROSS, PER = 5, 7, 5
SIZE = PER * 16
VMEM = pl.BlockSpec(memory_space=pltpu.VMEM)
ANY = pl.BlockSpec(memory_space=pl.ANY)
SMEM = pl.BlockSpec(memory_space=pltpu.SMEM)
PARAMS = pltpu.CompilerParams(vmem_limit_bytes=24 * 1024 * 1024)


def call(kernel, out_shape, inputs, scratch=(), specs=None, flops=0, deps=()):
    moved = sum(x.size * x.dtype.itemsize for x in inputs)
    moved += sum(s.size * s.dtype.itemsize for s in jax.tree.leaves(out_shape))
    n = len(inputs)

    def body(*refs):
        kernel(*refs[:n], *refs[n + len(deps) :])

    return pl.pallas_call(
        body,
        out_shape=out_shape,
        in_specs=(specs or [VMEM] * n) + [VMEM] * len(deps),
        out_specs=jax.tree.map(lambda _: VMEM, out_shape),
        scratch_shapes=list(scratch),
        compiler_params=PARAMS,
        cost_estimate=pl.CostEstimate(flops=flops, bytes_accessed=moved, transcendentals=0),
    )(*inputs, *deps)


def shape(*dims, dtype=BF16):
    return jax.ShapeDtypeStruct(dims, dtype)


def tile(ref_or_value, j):
    return ref_or_value[:, j * 128 : (j + 1) * 128]


def pack_kernel(core, tok, cot, out, wide):
    odd = core[0] == 1
    for base, ref in ((0, tok), (4, cot)):
        rows = ref[...].astype(F32)
        for j in range(4):
            piece = jnp.where(odd, tile(rows, (j + 2) % 4), tile(rows, j))
            wide[pl.ds(base + j, ROWS, stride=8), :] = piece
    out[...] = wide[...].astype(BF16)


def put_tiles(out, m, value):
    def put(slot, rows):
        row = m * SIZE + slot % PER * 16
        out[slot // PER, row : row + 16, :] = rows.astype(BF16)

    blank = jnp.zeros((8, 128), F32)
    for i in range(UP):
        for j in range(ACROSS):
            put(i * ACROSS + j, tile(value[i * 16 : (i + 1) * 16], j))
    last = [tile(value[UP * 16 : QUARTER], j) for j in range(ACROSS)] + [blank] * 3
    for j in range(0, 10, 2):
        put(UP * ACROSS + j // 2, jnp.concatenate([last[j], last[j + 1]], axis=0))


def get_tiles(ref, m, out, first):
    def get(slot):
        row = m * SIZE + slot % PER * 16
        return ref[slot // PER, row : row + 16, :]

    blank = jnp.zeros((8, 128), F32)
    for i in range(UP):
        for j in range(ACROSS):
            out[first + i * 16 : first + (i + 1) * 16, j * 128 : (j + 1) * 128] = get(i * ACROSS + j)
    for j in range(ACROSS):
        pair = get(UP * ACROSS + j // 2).astype(F32)
        half = pair[8:] if j % 2 else pair[:8]
        rows = jnp.concatenate([half, blank], axis=0).astype(BF16)
        out[first + UP * 16 : first + PADDED, j * 128 : (j + 1) * 128] = rows


def weights_kernel(gate_weight, up_weight, down_weight, out, down, sems):
    copies = [
        pltpu.make_async_copy(down_weight, down, sems.at[0]),
        pltpu.make_async_copy(gate_weight, out.at[:256], sems.at[1]),
        pltpu.make_async_copy(up_weight, out.at[256:512], sems.at[2]),
    ]
    for copy in copies:
        copy.start()
    for copy in copies:
        copy.wait()
    out[512:, :] = down[...].T


def spread_kernel(packed, out):
    for t in range(16):
        out[t] = packed[...]


def forward_kernel(rows, w0, w1, w2, w3, parts, x0, x1, x23, wide):
    for t in range(16):
        wide[t * 88 : (t + 1) * 88, :] = rows[t].astype(F32)
    blank = jnp.zeros((PADDED - QUARTER, 128), F32)
    for far in range(2):
        for j in range(8):
            piece = jnp.concatenate([wide[pl.ds(far * 704 + j, QUARTER, stride=8), :], blank], axis=0)
            at = (j // 4 * 2 + j % 2) * 128
            k = 2 * far + j % 4 // 2
            ref, first = ((x0, 0), (x1, 0), (x23, 0), (x23, PADDED))[k]
            ref[first : first + PADDED, at : at + 128] = piece.astype(BF16)
    blocks = (x0[...], x1[...], x23[:PADDED], x23[PADDED:])
    for m in range(3):
        cols = slice(256, 512) if m == 2 else slice(0, 256)
        total = jnp.zeros((PADDED, 896), F32)
        for x, w in zip(blocks, (w0, w1, w2, w3)):
            total = total + jnp.dot(x[:, cols], w[m * 256 : (m + 1) * 256, :], preferred_element_type=F32)
        put_tiles(parts, m, total)


def activation_kernel(parts, acts):
    total = parts[0].astype(F32)
    for i in range(1, 8):
        total = total + parts[i].astype(F32)
    gate, up, back = total[:SIZE], total[SIZE : 2 * SIZE], total[2 * SIZE :]
    logistic = jax.nn.sigmoid(gate)
    hidden = (gate * logistic * up).astype(BF16)
    grad_gate_act = (back * up * logistic * (1.0 + gate * (1.0 - logistic))).astype(BF16)
    grad_up_act = (back * gate * logistic).astype(BF16)
    for i in range(8):
        acts[i, :SIZE, :] = grad_gate_act
        acts[i, SIZE : 2 * SIZE, :] = grad_up_act
        acts[i, 2 * SIZE :, :] = hidden


def token_grad_kernel(acts, w0, w1, w2, w3, out, gate_act, up_act, total, wide):
    get_tiles(acts, 0, gate_act, 0)
    get_tiles(acts, 1, up_act, 0)
    dims = (((1,), (1,)), ((), ()))
    for k, w in enumerate((w0, w1, w2, w3)):
        part = lax.dot_general(gate_act[...], w[:256, :], dims, preferred_element_type=F32)
        part = part + lax.dot_general(up_act[...], w[256:512, :], dims, preferred_element_type=F32)
        total[:, k * 256 : (k + 1) * 256] = part
    for far in range(2):
        for i in range(8):
            for j in range(4):
                at = far * 512 + j * 128
                wide[j * ROWS : (j + 1) * ROWS, :] = total[i * ROWS : (i + 1) * ROWS, at : at + 128]
            out[far * 8 + i] = wide[...].astype(BF16)


def token_sum_kernel(core, parts, out, total):
    odd = core[0] == 1
    acc = parts[0].astype(F32)
    for t in range(1, 16):
        acc = acc + parts[t].astype(F32)
    total[...] = acc
    for j in range(4):
        here = total[j * ROWS : (j + 1) * ROWS, :]
        there = total[(j + 2) % 4 * ROWS : ((j + 2) % 4 + 1) * ROWS, :]
        out[:, j * 128 : (j + 1) * 128] = jnp.where(odd, there, here).astype(BF16)


def weight_grad_kernel(x0, x2, x13, acts0, acts1, acts2, acts3, grad_gate, grad_up, grad_down, x, act):
    contract_rows = (((0,), (0,)), ((), ()))
    x[:PADDED, :] = x0[...]
    x[PADDED : 2 * PADDED, :] = x13[:PADDED, :]
    x[2 * PADDED : 3 * PADDED, :] = x2[:PADDED, :]
    x[3 * PADDED :, :] = x13[PADDED:, :]
    for m in range(3):
        for k, acts in enumerate((acts0, acts1, acts2, acts3)):
            get_tiles(acts, m, act, k * PADDED)
        if m < 2:
            out, left, right = (grad_gate, grad_up)[m], x[:, :256], act[...]
        else:
            out, left, right = grad_down, act[...], x[:, 256:]
        out[...] = lax.dot_general(left, right, contract_rows, preferred_element_type=F32).astype(BF16)


def copy_kernel(x, out):
    out[...] = x[...]


def after(x, *deps):
    return call(copy_kernel, shape(*x.shape, dtype=x.dtype), (x,), deps=deps)


def swap(axis, x):
    return lax.ppermute(x, axis, [(0, 1), (1, 0)])


def place(z, xh, core, xl, y):
    return (((z * 2 + xh) * 2 + core) * 2 + xl) * 8 + y


def per_device(tokens, cotangent, gate_weight, up_weight, down_weight):
    core = jnp.reshape(lax.axis_index("core"), (1,)).astype(jnp.int32)
    there = [
        (place(z, xh, c, xl, y), place(4 * xl + y // 2, xh, c, y % 2 ^ xh, z))
        for z in range(8)
        for xh in range(2)
        for c in range(2)
        for xl in range(2)
        for y in range(8)
    ]
    home = [(b, a) for a, b in there]

    w0 = call(
        weights_kernel,
        shape(768, 896),
        (gate_weight, up_weight, down_weight),
        [pltpu.VMEM((896, 256), BF16), pltpu.SemaphoreType.DMA((3,))],
        specs=[ANY] * 3,
    )
    w2 = swap("xh", w0)
    packed = call(
        pack_kernel,
        shape(88, 128),
        (core, tokens, cotangent),
        [pltpu.VMEM((88, 128), F32)],
        specs=[SMEM, VMEM, VMEM],
    )
    packed = lax.ppermute(packed, ALL, there)
    w1 = swap("core", after(w0, packed))
    rows = lax.all_to_all(call(spread_kernel, shape(16, 88, 128), (packed,)), TENSOR, 0, 0, tiled=True)
    w2 = after(w2, rows)
    w3 = swap("core", w2)

    parts, x0, x1, x23 = call(
        forward_kernel,
        (shape(8, 3 * SIZE, 128), shape(PADDED, 512), shape(PADDED, 512), shape(2 * PADDED, 512)),
        (rows, w0, w1, w2, w3),
        [pltpu.VMEM((16 * 88, 128), F32)],
        flops=6 * PADDED * 1024 * 896,
    )
    parts = lax.all_to_all(parts, "z", 0, 0, tiled=True)
    x2 = swap("xh", after(x23, parts))
    x13 = swap("core", jnp.concatenate([x1, x2[PADDED:]], axis=0))

    acts0 = lax.all_to_all(call(activation_kernel, shape(8, 3 * SIZE, 128), (parts,)), "z", 0, 0, tiled=True)
    acts2 = swap("xh", acts0)

    token_parts = call(
        token_grad_kernel,
        shape(16, 4 * ROWS, 128),
        (acts0, w0, w1, w2, w3),
        [
            pltpu.VMEM((PADDED, 896), BF16),
            pltpu.VMEM((PADDED, 896), BF16),
            pltpu.VMEM((PADDED, 1024), F32),
            pltpu.VMEM((4 * ROWS, 128), F32),
        ],
        flops=4 * PADDED * 1024 * 896,
        deps=(x13,),
    )
    token_parts = lax.all_to_all(token_parts, TENSOR, 0, 0, tiled=True)
    acts0, acts2 = after(acts0, token_parts), after(acts2, token_parts)
    acts1, acts3 = swap("core", acts0), swap("core", acts2)

    grad_tokens = call(
        token_sum_kernel,
        shape(ROWS, 512),
        (core, token_parts),
        [pltpu.VMEM((4 * ROWS, 128), F32)],
        specs=[SMEM, VMEM],
    )
    grad_tokens = lax.ppermute(grad_tokens, ALL, home)

    grad_gate, grad_up, grad_down = call(
        weight_grad_kernel,
        (shape(256, 896), shape(256, 896), shape(896, 256)),
        (x0, x2, x13, acts0, acts1, acts2, acts3),
        [pltpu.VMEM((4 * PADDED, 512), BF16), pltpu.VMEM((4 * PADDED, 896), BF16)],
        flops=6 * 4 * PADDED * 256 * 896,
    )
    return (grad_tokens, grad_gate, grad_up, grad_down)


def solution(mesh):
    chips = Mesh(mesh.devices.reshape(8, 2, 2, 2, 8), ALL)
    rows, cols = P(FSDP, TENSOR), P(TENSOR, FSDP)
    return jax.shard_map(
        per_device,
        mesh=chips,
        in_specs=(rows, rows, rows, rows, cols),
        out_specs=(rows, rows, rows, cols),
        check_vma=False,
    )
```

time: 149 us -> 155 us (1.040)
  the two profiles are of different devices: /device:TPU:6 before, /device:TPU:264 now
where the time goes in v2:
time: 155 us; the launch traced here: 154 us
  starting transfers between devices  59.9 us (39%)
  waiting for transfers between devices  38.6 us (25%)
  blocking collectives  32.6 us (21%)
  Pallas kernels  10.7 us (7%)
  local copies, waits for them, and re-layouts  10 us (6%)
  other arithmetic  1.65 us (1%)
    ppermute x8, starting transfers between devices, swap(): return lax.ppermute(x, axis, [(0, 1), (1, 0)])  37.5 us
    all_to_all x1, blocking collectives, per_device(): parts = lax.all_to_all(parts, 'z', 0, 0, tiled=True)  18.8 us
    all_to_all x1, blocking collectives, per_device(): token_parts = lax.all_to_all(token_parts, TENSOR, 0, 0, tiled=True)  13.8 us
    all_to_all x1, waiting for transfers between devices, per_device(): lax.all_to_all(call(spread_kernel, shape(16, 88, 128), (packed,)), TENSOR...  12.7 us
    ppermute x1, waiting for transfers between devices, per_device(): grad_tokens = lax.ppermute(grad_tokens, ALL, home)  11.7 us
    pallas_call x13, Pallas kernels, call(): pl.pallas_call(body, out_shape=out_shape, in_specs=(specs or [VMEM] * n)...  10.7 us
    unnamed x31, local copies, waits for them, and re-layouts  10 us
    all_to_all x1, starting transfers between devices, per_device(): lax.all_to_all(call(activation_kernel, shape(8, 3 * SIZE, 128), (parts,))...  8.77 us
  transfers between devices with their start and end apart: 12, of which 5 were waited for; matrix products, arithmetic and copies ran while one was open for 1% of the time, Pallas kernels for 3%

profile of v2, /device:TPU:264, one launch (start us, length us, event | category | flops | bytes accessed | tf_op | source)
XLA Modules:
  0.0 154.3 jit_solution(9888846952165143551)
XLA Ops:
  4.7 4.9 %collective-permute-start.2 = (bf16[768,896]{1,0:T(8,128)(2,1)S(1)}, bf16[768,896]{1,0:T(8,128)(2,1)S(1)}, u32[]{:S(2)}, u32[]{:S(2)}) collective-permute-start(bf16[768,896]{1,0:T(8,128)(2,1)S(1)} %shard_map.86.refs_0_.refs_1_), channel_id=1, source_target_pairs={{0,32},{32,0},{1,33},{33,1},{2,34},{34,2},{3,35},{35,3},{4,36},{36... | collective-permute-start | bytes 4128776 | tf_op jit(solution)/shard_map/ppermute | solution.py:198
  9.7 3.1 %collective-permute-start = (bf16[88,128]{1,0:T(8,128)(2,1)S(1)}, bf16[88,128]{1,0:T(8,128)(2,1)S(1)}, u32[]{:S(2)}, u32[]{:S(2)}) collective-permute-start(bf16[88,128]{1,0:T(8,128)(2,1)S(1)} %shard_map.84), channel_id=1, source_target_pairs={{0,0},{1,8},{2,64},{3,72},{4,128},{5,136},{6,192},{7,200},{8,256},... | collective-permute-start | bytes 67592 | tf_op jit(solution)/shard_map/ppermute | solution.py:232
  12.8 7.5 %collective-permute-done.refs_0_.refs_1_ = bf16[88,128]{1,0:T(8,128)(2,1)S(1)} collective-permute-done((bf16[88,128]{1,0:T(8,128)(2,1)S(1)}, bf16[88,128]{1,0:T(8,128)(2,1)S(1)}, u32[]{:S(2)}, u32[]{:S(2)}) %collective-permute-start) | collective-permute-done | bytes 22560 | tf_op jit(solution)/shard_map/ppermute | solution.py:232
  21.1 7.6 %all-to-all-start = ((bf16[16,88,128]{2,1,0:T(8,128)(2,1)}), bf16[16,88,128]{2,1,0:T(8,128)(2,1)S(1)}, u32[]{:S(2)}, u32[]{:S(2)}) async-start(bf16[16,88,128]{2,1,0:T(8,128)(2,1)} %shard_map.85), calls=%async_computation | async-start | bytes 720896 | tf_op jit(solution)/shard_map/all_to_all | solution.py:234
  29.9 1.9 %collective-permute-start.1 = (bf16[768,896]{1,0:T(8,128)(2,1)}, bf16[768,896]{1,0:T(8,128)(2,1)}, u32[]{:S(2)}, u32[]{:S(2)}) collective-permute-start(bf16[768,896]{1,0:T(8,128)(2,1)} %shard_map.87), channel_id=1, source_target_pairs={{0,16},{16,0},{1,17},{17,1},{2,18},{18,2},{3,19},{19,3},{4,20},{20... | collective-permute-start | bytes 4128776 | tf_op jit(solution)/shard_map/ppermute | solution.py:198
  31.8 12.7 %all-to-all-done.refs_1_.refs_0_ = bf16[16,88,128]{2,1,0:T(8,128)(2,1)S(1)} async-done(((bf16[16,88,128]{2,1,0:T(8,128)(2,1)}), bf16[16,88,128]{2,1,0:T(8,128)(2,1)S(1)}, u32[]{:S(2)}, u32[]{:S(2)}) %all-to-all-start) | async-done | bytes 360480 | tf_op jit(solution)/shard_map/all_to_all | solution.py:234
  45.5 1.3 copy-done.6
  47.0 1.9 %collective-permute-start.3 = (bf16[768,896]{1,0:T(8,128)(2,1)S(1)}, bf16[768,896]{1,0:T(8,128)(2,1)S(1)}, u32[]{:S(2)}, u32[]{:S(2)}) collective-permute-start(bf16[768,896]{1,0:T(8,128)(2,1)S(1)} %shard_map.88.refs_3_), channel_id=1, source_target_pairs={{0,16},{16,0},{1,17},{17,1},{2,18},{18,2},{3,19},{19,3},{4,20},{20... | collective-permute-start | bytes 4128776 | tf_op jit(solution)/shard_map/ppermute | solution.py:198
  48.9 3.1 %collective-permute-done.3.refs_4_ = bf16[768,896]{1,0:T(8,128)(2,1)S(1)} collective-permute-done((bf16[768,896]{1,0:T(8,128)(2,1)S(1)}, bf16[768,896]{1,0:T(8,128)(2,1)S(1)}, u32[]{:S(2)}, u32[]{:S(2)}) %collective-permute-start.3) | collective-permute-done | bytes 1376288 | tf_op jit(solution)/shard_map/ppermute | solution.py:198
  52.0 2.9 %shard_map.89 = (bf16[8,240,128]{2,1,0:T(8,128)(2,1)S(1)}, bf16[96,512]{1,0:T(8,128)(2,1)S(1)}, bf16[96,512]{1,0:T(8,128)(2,1)S(1)}, bf16[192,512]{1,0:T(8,128)(2,1)S(1)}) custom-call(bf16[16,88,128]{2,1,0:T(8,128)(2,1)S(1)} %all-to-all-done.refs_1_.refs_0_, bf16[768,896]{1,0:T(8,128)(2,1)S(1)} %shard_map.86.refs_0_.refs_1_, ...), custom_call_target="tpu_custom_call" | custom-call | flops 528482304 | bytes 6750208 | tf_op jit(solution)/shard_map/pallas_call | solution.py:33
  54.9 18.8 %all_to_all.20.refs_0_.refs_1_ = bf16[8,240,128]{2,1,0:T(8,128)(2,1)S(1)} all-to-all(bf16[8,240,128]{2,1,0:T(8,128)(2,1)S(1)} %get-tuple-element.11), channel_id=1, replica_groups=mesh['z'=8,'xh'=2,'core'=2,'xl'=2,'y'=8] {'z'}, dimensions={0} | all-to-all | bytes 983040 | tf_op jit(solution)/shard_map/all_to_all | solution.py:245
  75.3 8.8 %all-to-all-start.2 = ((bf16[8,240,128]{2,1,0:T(8,128)(2,1)}), bf16[8,240,128]{2,1,0:T(8,128)(2,1)S(1)}, u32[]{:S(2)}, u32[]{:S(2)}) async-start(bf16[8,240,128]{2,1,0:T(8,128)(2,1)} %copy-done.4), calls=%async_computation.2 | async-start | bytes 983040 | tf_op jit(solution)/shard_map/all_to_all | solution.py:249
  85.2 17.0 %collective-permute-start.4 = (bf16[192,512]{1,0:T(8,128)(2,1)S(1)}, bf16[192,512]{1,0:T(8,128)(2,1)S(1)}, u32[]{:S(2)}, u32[]{:S(2)}) collective-permute-start(bf16[192,512]{1,0:T(8,128)(2,1)S(1)} %shard_map.91), channel_id=1, source_target_pairs={{0,32},{32,0},{1,33},{33,1},{2,34},{34,2},{3,35},{35,3},{4,36},{36... | collective-permute-start | bytes 589832 | tf_op jit(solution)/shard_map/ppermute | solution.py:198
  102.1 3.6 %collective-permute-done.4.refs_1_ = bf16[192,512]{1,0:T(8,128)(2,1)S(1)} collective-permute-done((bf16[192,512]{1,0:T(8,128)(2,1)S(1)}, bf16[192,512]{1,0:T(8,128)(2,1)S(1)}, u32[]{:S(2)}, u32[]{:S(2)}) %collective-permute-start.4) | collective-permute-done | bytes 196640 | tf_op jit(solution)/shard_map/ppermute | solution.py:198
  105.8 1.7 %pad_maximum_fusion = bf16[192,512]{1,0:T(8,128)(2,1)} fusion(bf16[96,512]{1,0:T(8,128)(2,1)S(1)} %slice.4, bf16[96,512]{1,0:T(8,128)(2,1)} %copy-done.12), kind=kLoop, calls=%fused_computation | loop fusion | flops 393216 | bytes 393216 | tf_op jit(solution)/shard_map/concatenate | solution.py:247
  107.5 1.9 %collective-permute-start.5 = (bf16[192,512]{1,0:T(8,128)(2,1)}, bf16[192,512]{1,0:T(8,128)(2,1)S(1)}, u32[]{:S(2)}, u32[]{:S(2)}) collective-permute-start(bf16[192,512]{1,0:T(8,128)(2,1)} %pad_maximum_fusion), channel_id=1, source_target_pairs={{0,16},{16,0},{1,17},{17,1},{2,18},{18,2},{3,19},{19,3},{4,20},{20... | collective-permute-start | bytes 589832 | tf_op jit(solution)/shard_map/ppermute | solution.py:198
  109.4 5.4 %collective-permute-start.8 = (bf16[8,240,128]{2,1,0:T(8,128)(2,1)S(1)}, bf16[8,240,128]{2,1,0:T(8,128)(2,1)S(1)}, u32[]{:S(2)}, u32[]{:S(2)}) collective-permute-start(bf16[8,240,128]{2,1,0:T(8,128)(2,1)S(1)} %all-to-all-done.2.refs_0_), channel_id=1, source_target_pairs={{0,32},{32,0},{1,33},{33,1},{2,34},{34,2},{3,35},{35,3},{4,36},{36... | collective-permute-start | bytes 1474568 | tf_op jit(solution)/shard_map/ppermute | solution.py:198
  116.2 2.6 %shard_map.92 = bf16[16,44,128]{2,1,0:T(8,128)(2,1)S(1)} custom-call(bf16[8,240,128]{2,1,0:T(8,128)(2,1)S(1)} %all-to-all-done.2.refs_0_, bf16[768,896]{1,0:T(8,128)(2,1)S(1)} %shard_map.86.refs_0_.refs_1_, bf16[768,896]{1,0:T(8,128)(2,1)} %collective-permute-done.1.refs_2_, bf16[768,896]{1,0:T(8,128)(2,1)S(1)} %shard_map.88.refs_3_, ...), custom_call_target="tpu_custom_call" | custom-call | flops 352321536 | bytes 6176768 | tf_op jit(solution)/shard_map/pallas_call | solution.py:33
  118.8 13.8 %all_to_all.21.refs_1_ = bf16[16,44,128]{2,1,0:T(8,128)(2,1)S(1)} all-to-all(bf16[16,44,128]{2,1,0:T(8,128)(2,1)S(1)} %shard_map.92), channel_id=1, replica_groups=mesh['z'=8,'xh'=2,'core'=2,'xl'=2,'y'=8] {'xl','y'}, dimensions={0} | all-to-all | bytes 360448 | tf_op jit(solution)/shard_map/all_to_all | solution.py:265
  132.7 2.1 %collective-permute-start.7 = (bf16[8,240,128]{2,1,0:T(8,128)(2,1)S(1)}, bf16[8,240,128]{2,1,0:T(8,128)(2,1)S(1)}, u32[]{:S(2)}, u32[]{:S(2)}) collective-permute-start(bf16[8,240,128]{2,1,0:T(8,128)(2,1)S(1)} %shard_map.94.refs_3_), channel_id=1, source_target_pairs={{0,16},{16,0},{1,17},{17,1},{2,18},{18,2},{3,19},{19,3},{4,20},{20... | collective-permute-start | bytes 1474568 | tf_op jit(solution)/shard_map/ppermute | solution.py:198
  134.8 2.4 %collective-permute-start.9 = (bf16[8,240,128]{2,1,0:T(8,128)(2,1)S(1)}, bf16[8,240,128]{2,1,0:T(8,128)(2,1)S(1)}, u32[]{:S(2)}, u32[]{:S(2)}) collective-permute-start(bf16[8,240,128]{2,1,0:T(8,128)(2,1)S(1)} %shard_map.95.refs_5_), channel_id=1, source_target_pairs={{0,16},{16,0},{1,17},{17,1},{2,18},{18,2},{3,19},{19,3},{4,20},{20... | collective-permute-start | bytes 1474568 | tf_op jit(solution)/shard_map/ppermute | solution.py:198
  137.2 2.9 %collective-permute-start.6 = (bf16[11,512]{1,0:T(8,128)(2,1)S(1)}, bf16[11,512]{1,0:T(8,128)(2,1)S(1)}, u32[]{:S(2)}, u32[]{:S(2)}) collective-permute-start(bf16[11,512]{1,0:T(8,128)(2,1)S(1)} %shard_map.93), channel_id=1, source_target_pairs={{0,0},{8,1},{64,2},{72,3},{128,4},{136,5},{192,6},{200,7},{256,8},... | collective-permute-start | bytes 33800 | tf_op jit(solution)/shard_map/ppermute | solution.py:276
  140.1 11.7 %collective-permute-done.6 = bf16[11,512]{1,0:T(8,128)(2,1)S(1)} collective-permute-done((bf16[11,512]{1,0:T(8,128)(2,1)S(1)}, bf16[11,512]{1,0:T(8,128)(2,1)S(1)}, u32[]{:S(2)}, u32[]{:S(2)}) %collective-permute-start.6) | collective-permute-done | bytes 11296 | tf_op jit(solution)/shard_map/ppermute | solution.py:276
  151.8 1.9 %shard_map.96 = (bf16[256,896]{1,0:T(8,128)(2,1)}, bf16[256,896]{1,0:T(8,128)(2,1)}, bf16[896,256]{1,0:T(8,128)(2,1)}) custom-call(bf16[96,512]{1,0:T(8,128)(2,1)S(1)} %get-tuple-element.14.refs_0_, bf16[192,512]{1,0:T(8,128)(2,1)S(1)} %copy-done.11, bf16[192,512]{1,0:T(8,128)(2,1)S(1)} %collective-permute-done.5.refs_5_.refs_2_, ...), custom_call_target="tpu_custom_call" | custom-call | flops 528482304 | bytes 3833856 | tf_op jit(solution)/shard_map/pallas_call | solution.py:33
  (48 shorter events, 12.0 us)
Async XLA Ops:
  0.6 1.0 copy-start.7
  1.7 1.0 copy-start.8
  3.7 6.0 %copy-start.13 = (bf16[11,512]{1,0:T(8,128)(2,1)S(1)}, bf16[11,512]{1,0:T(8,128)(2,1)}, u32[]{:S(2)}) copy-start(bf16[11,512]{1,0:T(8,128)(2,1)} %refs_1_.2) | copy-start | bytes 33796
  3.7 6.0 %copy-start.14 = (bf16[11,512]{1,0:T(8,128)(2,1)S(1)}, bf16[11,512]{1,0:T(8,128)(2,1)}, u32[]{:S(2)}) copy-start(bf16[11,512]{1,0:T(8,128)(2,1)} %refs_2_.2) | copy-start | bytes 33796
  4.7 39.8 %collective-permute-start.2 = (bf16[768,896]{1,0:T(8,128)(2,1)S(1)}, bf16[768,896]{1,0:T(8,128)(2,1)S(1)}, u32[]{:S(2)}, u32[]{:S(2)}) collective-permute-start(bf16[768,896]{1,0:T(8,128)(2,1)S(1)} %shard_map.86.refs_0_.refs_1_), channel_id=1, source_target_pairs={{0,32},{32,0},{1,33},{33,1},{2,34},{34,2},{3,35},{35,3},{4,36},{36... | collective-permute-start | bytes 4128776 | tf_op jit(solution)/shard_map/ppermute | solution.py:198
  9.7 10.6 %collective-permute-start = (bf16[88,128]{1,0:T(8,128)(2,1)S(1)}, bf16[88,128]{1,0:T(8,128)(2,1)S(1)}, u32[]{:S(2)}, u32[]{:S(2)}) collective-permute-start(bf16[88,128]{1,0:T(8,128)(2,1)S(1)} %shard_map.84), channel_id=1, source_target_pairs={{0,0},{1,8},{2,64},{3,72},{4,128},{5,136},{6,192},{7,200},{8,256},... | collective-permute-start | bytes 67592 | tf_op jit(solution)/shard_map/ppermute | solution.py:232
  21.1 23.4 %all-to-all-start = ((bf16[16,88,128]{2,1,0:T(8,128)(2,1)}), bf16[16,88,128]{2,1,0:T(8,128)(2,1)S(1)}, u32[]{:S(2)}, u32[]{:S(2)}) async-start(bf16[16,88,128]{2,1,0:T(8,128)(2,1)} %shard_map.85), calls=%async_computation | async-start | bytes 720896 | tf_op jit(solution)/shard_map/all_to_all | solution.py:234
  29.9 19.1 %collective-permute-start.1 = (bf16[768,896]{1,0:T(8,128)(2,1)}, bf16[768,896]{1,0:T(8,128)(2,1)}, u32[]{:S(2)}, u32[]{:S(2)}) collective-permute-start(bf16[768,896]{1,0:T(8,128)(2,1)} %shard_map.87), channel_id=1, source_target_pairs={{0,16},{16,0},{1,17},{17,1},{2,18},{18,2},{3,19},{19,3},{4,20},{20... | collective-permute-start | bytes 4128776 | tf_op jit(solution)/shard_map/ppermute | solution.py:198
  44.5 1.1 copy-start.5
  45.5 1.3 copy-start.6
  47.0 5.0 %collective-permute-start.3 = (bf16[768,896]{1,0:T(8,128)(2,1)S(1)}, bf16[768,896]{1,0:T(8,128)(2,1)S(1)}, u32[]{:S(2)}, u32[]{:S(2)}) collective-permute-start(bf16[768,896]{1,0:T(8,128)(2,1)S(1)} %shard_map.88.refs_3_), channel_id=1, source_target_pairs={{0,16},{16,0},{1,17},{17,1},{2,18},{18,2},{3,19},{19,3},{4,20},{20... | collective-permute-start | bytes 4128776 | tf_op jit(solution)/shard_map/ppermute | solution.py:198
  52.0 2.9 %copy-start = (bf16[768,896]{1,0:T(8,128)(2,1)}, bf16[768,896]{1,0:T(8,128)(2,1)S(1)}, u32[]{:S(2)}) copy-start(bf16[768,896]{1,0:T(8,128)(2,1)S(1)} %collective-permute-done.3.refs_4_) | copy-start | bytes 4128772
  54.9 20.4 %copy-start.12 = (bf16[96,512]{1,0:T(8,128)(2,1)}, bf16[96,512]{1,0:T(8,128)(2,1)S(1)}, u32[]{:S(2)}) copy-start(bf16[96,512]{1,0:T(8,128)(2,1)S(1)} %get-tuple-element.12) | copy-start | bytes 294916
  75.3 34.0 %all-to-all-start.2 = ((bf16[8,240,128]{2,1,0:T(8,128)(2,1)}), bf16[8,240,128]{2,1,0:T(8,128)(2,1)S(1)}, u32[]{:S(2)}, u32[]{:S(2)}) async-start(bf16[8,240,128]{2,1,0:T(8,128)(2,1)} %copy-done.4), calls=%async_computation.2 | async-start | bytes 983040 | tf_op jit(solution)/shard_map/all_to_all | solution.py:249
  84.1 1.0 copy-start.3
  85.2 20.6 %collective-permute-start.4 = (bf16[192,512]{1,0:T(8,128)(2,1)S(1)}, bf16[192,512]{1,0:T(8,128)(2,1)S(1)}, u32[]{:S(2)}, u32[]{:S(2)}) collective-permute-start(bf16[192,512]{1,0:T(8,128)(2,1)S(1)} %shard_map.91), channel_id=1, source_target_pairs={{0,32},{32,0},{1,33},{33,1},{2,34},{34,2},{3,35},{35,3},{4,36},{36... | collective-permute-start | bytes 589832 | tf_op jit(solution)/shard_map/ppermute | solution.py:198
  105.8 1.7 %copy-start.10 = (bf16[192,512]{1,0:T(8,128)(2,1)}, bf16[192,512]{1,0:T(8,128)(2,1)S(1)}, u32[]{:S(2)}) copy-start(bf16[192,512]{1,0:T(8,128)(2,1)S(1)} %collective-permute-done.4.refs_1_) | copy-start | bytes 589828
  107.5 7.4 %collective-permute-start.5 = (bf16[192,512]{1,0:T(8,128)(2,1)}, bf16[192,512]{1,0:T(8,128)(2,1)S(1)}, u32[]{:S(2)}, u32[]{:S(2)}) collective-permute-start(bf16[192,512]{1,0:T(8,128)(2,1)} %pad_maximum_fusion), channel_id=1, source_target_pairs={{0,16},{16,0},{1,17},{17,1},{2,18},{18,2},{3,19},{19,3},{4,20},{20... | collective-permute-start | bytes 589832 | tf_op jit(solution)/shard_map/ppermute | solution.py:198
  109.4 25.3 %collective-permute-start.8 = (bf16[8,240,128]{2,1,0:T(8,128)(2,1)S(1)}, bf16[8,240,128]{2,1,0:T(8,128)(2,1)S(1)}, u32[]{:S(2)}, u32[]{:S(2)}) collective-permute-start(bf16[8,240,128]{2,1,0:T(8,128)(2,1)S(1)} %all-to-all-done.2.refs_0_), channel_id=1, source_target_pairs={{0,32},{32,0},{1,33},{33,1},{2,34},{34,2},{3,35},{35,3},{4,36},{36... | collective-permute-start | bytes 1474568 | tf_op jit(solution)/shard_map/ppermute | solution.py:198
  114.8 1.3 copy-start.1
  132.6 19.1 %copy-start.11 = (bf16[192,512]{1,0:T(8,128)(2,1)S(1)}, bf16[192,512]{1,0:T(8,128)(2,1)}, u32[]{:S(2)}) copy-start(bf16[192,512]{1,0:T(8,128)(2,1)} %copy-done.10) | copy-start | bytes 589828
  132.7 19.1 %collective-permute-start.7 = (bf16[8,240,128]{2,1,0:T(8,128)(2,1)S(1)}, bf16[8,240,128]{2,1,0:T(8,128)(2,1)S(1)}, u32[]{:S(2)}, u32[]{:S(2)}) collective-permute-start(bf16[8,240,128]{2,1,0:T(8,128)(2,1)S(1)} %shard_map.94.refs_3_), channel_id=1, source_target_pairs={{0,16},{16,0},{1,17},{17,1},{2,18},{18,2},{3,19},{19,3},{4,20},{20... | collective-permute-start | bytes 1474568 | tf_op jit(solution)/shard_map/ppermute | solution.py:198
  134.8 17.0 %collective-permute-start.9 = (bf16[8,240,128]{2,1,0:T(8,128)(2,1)S(1)}, bf16[8,240,128]{2,1,0:T(8,128)(2,1)S(1)}, u32[]{:S(2)}, u32[]{:S(2)}) collective-permute-start(bf16[8,240,128]{2,1,0:T(8,128)(2,1)S(1)} %shard_map.95.refs_5_), channel_id=1, source_target_pairs={{0,16},{16,0},{1,17},{17,1},{2,18},{18,2},{3,19},{19,3},{4,20},{20... | collective-permute-start | bytes 1474568 | tf_op jit(solution)/shard_map/ppermute | solution.py:198
  137.2 14.5 %collective-permute-start.6 = (bf16[11,512]{1,0:T(8,128)(2,1)S(1)}, bf16[11,512]{1,0:T(8,128)(2,1)S(1)}, u32[]{:S(2)}, u32[]{:S(2)}) collective-permute-start(bf16[11,512]{1,0:T(8,128)(2,1)S(1)} %shard_map.93), channel_id=1, source_target_pairs={{0,0},{8,1},{64,2},{72,3},{128,4},{136,5},{192,6},{200,7},{256,8},... | collective-permute-start | bytes 33800 | tf_op jit(solution)/shard_map/ppermute | solution.py:276
  (3 other events, 2.6 us)

commit v3 on v2

v3 whole, which is shorter than its diff:
```python
import math

import jax
import jax.numpy as jnp
from jax import lax
from jax.experimental import pallas as pl
from jax.experimental.pallas import tpu as pltpu
from jax.sharding import Mesh
from jax.sharding import PartitionSpec as P

F32, BF16 = jnp.float32, jnp.bfloat16
ALL = ("z", "xh", "core", "xl", "y")
FSDP = ("z", "xh", "core")
TENSOR = ("xl", "y")

ROWS, QUARTER, PADDED = 11, 88, 96
UP, ACROSS, PER = 5, 7, 5
SIZE = PER * 16
VMEM = pl.BlockSpec(memory_space=pltpu.VMEM)
HBM = pl.BlockSpec(memory_space=pltpu.HBM)
SMEM = pl.BlockSpec(memory_space=pltpu.SMEM)
PARAMS = pltpu.CompilerParams(vmem_limit_bytes=20 * 1024 * 1024)


def call(kernel, out_shape, inputs, scratch=(), specs=None, flops=0, deps=(), outs=None):
    moved = sum(x.size * x.dtype.itemsize for x in inputs)
    moved += sum(math.prod(s.shape) * s.dtype.itemsize for s in out_shape)
    n, m = len(inputs), len(out_shape)

    def body(*refs):
        rest = refs[n + len(deps) :]
        rest[m][...] = jnp.zeros((8, 128), F32)
        kernel(*refs[:n], *rest[:m], *rest[m + 1 :])

    return pl.pallas_call(
        body,
        out_shape=(*out_shape, shape(8, 128, dtype=F32)),
        in_specs=list(specs or [VMEM] * n) + [VMEM] * len(deps),
        out_specs=list(outs or [VMEM] * m) + [VMEM],
        scratch_shapes=list(scratch),
        compiler_params=PARAMS,
        cost_estimate=pl.CostEstimate(flops=flops, bytes_accessed=moved, transcendentals=0),
    )(*inputs, *deps)


def shape(*dims, dtype=BF16):
    return jax.ShapeDtypeStruct(dims, dtype)


def tile(ref_or_value, j):
    return ref_or_value[:, j * 128 : (j + 1) * 128]


def fetch(sems, *pairs):
    copies = [pltpu.make_async_copy(source, to, sems.at[i]) for i, (source, to) in enumerate(pairs)]
    for copy in copies:
        copy.start()
    for copy in copies:
        copy.wait()


def pack_kernel(place, tok, cot, out, wide):
    odd = place[0] == 1
    for base, ref in ((0, tok), (4, cot)):
        rows = ref[...].astype(F32)
        for j in range(4):
            piece = jnp.where(odd, tile(rows, (j + 2) % 4), tile(rows, j))
            wide[pl.ds(base + j, ROWS, stride=8), :] = piece
    out[...] = wide[...].astype(BF16)


def put_tiles(out, m, value, half):
    def put(slot, rows):
        row = m * SIZE + slot % PER * 16
        out[slot // PER * 2 + half, row : row + 16, :] = rows.astype(BF16)

    blank = jnp.zeros((8, 128), F32)
    for i in range(UP):
        for j in range(ACROSS):
            put(i * ACROSS + j, tile(value[i * 16 : (i + 1) * 16], j))
    last = [tile(value[UP * 16 : QUARTER], j) for j in range(ACROSS)] + [blank] * 3
    for j in range(0, 10, 2):
        put(UP * ACROSS + j // 2, jnp.concatenate([last[j], last[j + 1]], axis=0))


def get_tiles(ref, m, out, first):
    def get(slot):
        row = m * SIZE + slot % PER * 16
        return ref[slot // PER, row : row + 16, :]

    blank = jnp.zeros((8, 128), F32)
    for i in range(UP):
        for j in range(ACROSS):
            out[first + i * 16 : first + (i + 1) * 16, j * 128 : (j + 1) * 128] = get(i * ACROSS + j)
    for j in range(ACROSS):
        pair = get(UP * ACROSS + j // 2).astype(F32)
        half = pair[8:] if j % 2 else pair[:8]
        rows = jnp.concatenate([half, blank], axis=0).astype(BF16)
        out[first + UP * 16 : first + PADDED, j * 128 : (j + 1) * 128] = rows


def weights_kernel(gate_weight, up_weight, out, sems):
    fetch(sems, (gate_weight, out.at[:256]), (up_weight, out.at[256:]))


def spread_kernel(packed, out):
    for t in range(16):
        out[t] = packed[...]


def forward_kernel(place, rows, gu0, gu1, down0, down1, out, x_own, x_oth, wide, parts, sems):
    for t in range(16):
        wide[t * 88 : (t + 1) * 88, :] = rows[t].astype(F32)
    blank = jnp.zeros((PADDED - QUARTER, 128), F32)
    for far in range(2):
        for j in range(8):
            piece = jnp.concatenate([wide[pl.ds(far * 704 + j, QUARTER, stride=8), :], blank], axis=0)
            at = (j // 4 * 2 + j % 2) * 128
            ref = (x_own, x_oth)[j % 4 // 2]
            ref[far * PADDED : (far + 1) * PADDED, at : at + 128] = piece.astype(BF16)
    by_cols = (((1,), (0,)), ((), ()))
    by_rows = (((1,), (1,)), ((), ()))
    copies = []
    for m in range(3):
        cols, dims = (slice(256, 512), by_rows) if m == 2 else (slice(0, 256), by_cols)
        own, oth = (down0[...], down1[...]) if m == 2 else (gu[m * 256 : (m + 1) * 256, :] for gu in (gu0, gu1))
        total = lax.dot_general(x_own[:, cols], own, dims, preferred_element_type=F32)
        total = total + lax.dot_general(x_oth[:, cols], oth, dims, preferred_element_type=F32)
        put_tiles(parts, m, total[:PADDED], place[1])
        put_tiles(parts, m, total[PADDED:], 1 - place[1])
        here = pl.ds(m * SIZE, SIZE)
        copies.append(pltpu.make_async_copy(parts.at[:, here], out.at[:, here], sems.at[m]))
        copies[m].start()
    for copy in copies:
        copy.wait()


def activation_kernel(parts, acts):
    total = parts[0].astype(F32)
    for i in range(1, 16):
        total = total + parts[i].astype(F32)
    gate, up, back = total[:SIZE], total[SIZE : 2 * SIZE], total[2 * SIZE :]
    logistic = jax.nn.sigmoid(gate)
    hidden = (gate * logistic * up).astype(BF16)
    grad_gate_act = (back * up * logistic * (1.0 + gate * (1.0 - logistic))).astype(BF16)
    grad_up_act = (back * gate * logistic).astype(BF16)
    for i in range(8):
        acts[i, :SIZE, :] = grad_gate_act
        acts[i, SIZE : 2 * SIZE, :] = grad_up_act
        acts[i, 2 * SIZE :, :] = hidden


def token_grad_kernel(acts, gu0, gu1, gu2, gu3, out, gate_act, up_act, wide):
    get_tiles(acts, 0, gate_act, 0)
    get_tiles(acts, 1, up_act, 0)
    dims = (((1,), (1,)), ((), ()))
    for k, gu in enumerate((gu0, gu1, gu2, gu3)):
        part = lax.dot_general(gate_act[...], gu[:256, :], dims, preferred_element_type=F32)
        part = part + lax.dot_general(up_act[...], gu[256:, :], dims, preferred_element_type=F32)
        for j in range(2):
            wide[k // 2, pl.ds(k % 2 * 2 + j, QUARTER, stride=4), :] = tile(part[:QUARTER], j)
    for far in range(2):
        for i in range(8):
            out[far * 8 + i] = wide[far, i * 4 * ROWS : (i + 1) * 4 * ROWS, :].astype(BF16)


def token_sum_kernel(place, parts, out, total):
    odd = place[0] == 1
    acc = parts[0].astype(F32)
    for t in range(1, 16):
        acc = acc + parts[t].astype(F32)
    total[...] = acc
    pieces = [total[pl.ds(j, ROWS, stride=4), :] for j in range(4)]
    for j in range(4):
        out[:, j * 128 : (j + 1) * 128] = jnp.where(odd, pieces[(j + 2) % 4], pieces[j]).astype(BF16)


def weight_grad_kernel(x_own, x_got, acts0, acts1, acts2, acts3, grad_gate, grad_up, grad_down, x, act):
    contract_rows = (((0,), (0,)), ((), ()))
    for k in range(4):
        rows = slice(k // 2 * PADDED, (k // 2 + 1) * PADDED)
        x[k * PADDED : (k + 1) * PADDED, :] = (x_got if k % 2 else x_own)[rows, :]
    for m in range(3):
        for k, acts in enumerate((acts0, acts1, acts2, acts3)):
            get_tiles(acts, m, act, k * PADDED)
        if m < 2:
            out, left, right = (grad_gate, grad_up)[m], x[:, :256], act[...]
        else:
            out, left, right = grad_down, act[...], x[:, 256:]
        out[...] = lax.dot_general(left, right, contract_rows, preferred_element_type=F32).astype(BF16)


def copy_kernel(x, out):
    out[...] = x[...]


def after(x, *deps, flops=0):
    return call(copy_kernel, (shape(*x.shape, dtype=x.dtype),), (x,), deps=deps, flops=flops)[0]


def swap(axis, x):
    return lax.ppermute(x, axis, [(0, 1), (1, 0)])


def place_of(z, xh, core, xl, y):
    return (((z * 2 + xh) * 2 + core) * 2 + xl) * 8 + y


def permutation(to):
    grid = [(z, xh, c, xl, y) for z in range(8) for xh in range(2) for c in range(2) for xl in range(2) for y in range(8)]
    return [(place_of(*at), place_of(*to(*at))) for at in grid]


def per_device(tokens, cotangent, gate_weight, up_weight, down_weight):
    place = jnp.stack([lax.axis_index("core"), lax.axis_index("xh")]).astype(jnp.int32)
    there = permutation(lambda z, xh, c, xl, y: (4 * xl + y // 2, y % 2, c, xh ^ y % 2, z))
    home = [(b, a) for a, b in permutation(lambda z, xh, c, xl, y: (4 * xl + y // 2, xh, c, xh ^ y % 2, z))]

    packed, ready = call(
        pack_kernel,
        (shape(88, 128),),
        (place, tokens, cotangent),
        [pltpu.VMEM((88, 128), F32)],
        specs=[SMEM, VMEM, VMEM],
    )
    packed = lax.ppermute(packed, ALL, there)
    spread, _ = call(spread_kernel, (shape(16, 88, 128),), (packed,), flops=10**11)
    rows = lax.all_to_all(spread, TENSOR, 0, 0, tiled=True)
    gu0, _ = call(
        weights_kernel,
        (shape(512, 896),),
        (gate_weight, up_weight),
        [pltpu.SemaphoreType.DMA((2,))],
        specs=[HBM, HBM],
        deps=(ready,),
    )
    gu1, down1 = swap("core", gu0), swap("core", down_weight)

    parts, x_own, x_oth, ready = call(
        forward_kernel,
        (pltpu.HBM((16, 3 * SIZE, 128), BF16), shape(2 * PADDED, 512), shape(2 * PADDED, 512)),
        (place, rows, gu0, gu1, down_weight, down1),
        [
            pltpu.VMEM((16 * 88, 128), F32),
            pltpu.VMEM((16, 3 * SIZE, 128), BF16),
            pltpu.SemaphoreType.DMA((3,)),
        ],
        specs=[SMEM] + [VMEM] * 5,
        outs=[HBM, VMEM, VMEM],
        flops=12 * PADDED * 512 * 896,
    )
    parts = lax.all_to_all(parts, ("z", "xh"), 0, 0, tiled=True)
    x_got = swap("core", after(x_oth, ready))
    gu2 = swap("xh", after(gu0, ready))

    acts0, ready = call(activation_kernel, (shape(8, 3 * SIZE, 128),), (parts,))
    acts0 = lax.all_to_all(acts0, "z", 0, 0, tiled=True)
    gu3 = swap("core", after(gu2, ready, x_got))
    acts2 = swap("xh", acts0)

    token_parts, ready = call(
        token_grad_kernel,
        (shape(16, 4 * ROWS, 128),),
        (acts0, gu0, gu1, gu2, gu3),
        [
            pltpu.VMEM((PADDED, 896), BF16),
            pltpu.VMEM((PADDED, 896), BF16),
            pltpu.VMEM((2, 4 * QUARTER, 128), F32),
        ],
        flops=4 * PADDED * 1024 * 896,
    )
    token_parts = lax.all_to_all(token_parts, TENSOR, 0, 0, tiled=True)
    acts1 = swap("core", after(acts0, ready))

    grad_tokens, _ = call(
        token_sum_kernel,
        (shape(ROWS, 512),),
        (place, token_parts),
        [pltpu.VMEM((4 * ROWS, 128), F32)],
        specs=[SMEM, VMEM],
    )
    grad_tokens = after(lax.ppermute(grad_tokens, ALL, home), flops=10**11)
    acts3 = swap("core", acts2)

    grad_gate, grad_up, grad_down, _ = call(
        weight_grad_kernel,
        (shape(256, 896), shape(256, 896), shape(896, 256)),
        (x_own, x_got, acts0, acts1, acts2, acts3),
        [pltpu.VMEM((4 * PADDED, 512), BF16), pltpu.VMEM((4 * PADDED, 896), BF16)],
        flops=6 * 4 * PADDED * 256 * 896,
    )
    return (grad_tokens, grad_gate, grad_up, grad_down)


def solution(mesh):
    chips = Mesh(mesh.devices.reshape(8, 2, 2, 2, 8), ALL)
    rows, cols = P(FSDP, TENSOR), P(TENSOR, FSDP)
    return jax.shard_map(
        per_device,
        mesh=chips,
        in_specs=(rows, rows, rows, rows, cols),
        out_specs=(rows, rows, rows, cols),
        check_vma=False,
    )
```

time: 155 us -> 136 us (0.88)
  the two profiles are of different devices: /device:TPU:264 before, /device:TPU:14 now
where the time goes in v3:
time: 136 us; the launch traced here: 135 us
  starting transfers between devices  54.3 us (40%)
  waiting for transfers between devices  43.1 us (32%)
  Pallas kernels  16.6 us (12%)
  blocking collectives  16 us (12%)
  local copies, waits for them, and re-layouts  4.06 us (3%)
    ppermute x8, starting transfers between devices, swap(): return lax.ppermute(x, axis, [(0, 1), (1, 0)])  18.9 us
    all_to_all x1, waiting for transfers between devices, per_device(): parts = lax.all_to_all(parts, ('z', 'xh'), 0, 0, tiled=True)  16.6 us
    pallas_call x13, Pallas kernels, call(): pl.pallas_call(body, out_shape=(*out_shape, shape(8, 128, dtype=F32)), in...  16.6 us
    all_to_all x1, blocking collectives, per_device(): token_parts = lax.all_to_all(token_parts, TENSOR, 0, 0, tiled=True)  16 us
    ppermute x1, starting transfers between devices, per_device(): packed = lax.ppermute(packed, ALL, there)  11.1 us
    all_to_all x1, starting transfers between devices, per_device(): parts = lax.all_to_all(parts, ('z', 'xh'), 0, 0, tiled=True)  9.65 us
    all_to_all x1, waiting for transfers between devices, per_device(): rows = lax.all_to_all(spread, TENSOR, 0, 0, tiled=True)  8.99 us
    all_to_all x1, starting transfers between devices, per_device(): rows = lax.all_to_all(spread, TENSOR, 0, 0, tiled=True)  8.85 us
  transfers between devices with their start and end apart: 13, of which 6 were waited for; matrix products, arithmetic and copies ran while one was open for 0% of the time, Pallas kernels for 9%

profile of v3, /device:TPU:14, one launch (start us, length us, event | category | flops | bytes accessed | tf_op | source)
XLA Modules:
  0.0 135.0 jit_solution(15304466026532197425)
XLA Ops:
  2.6 11.1 %collective-permute-start = (bf16[88,128]{1,0:T(8,128)(2,1)S(1)}, bf16[88,128]{1,0:T(8,128)(2,1)S(1)}, u32[]{:S(2)}, u32[]{:S(2)}) collective-permute-start(bf16[88,128]{1,0:T(8,128)(2,1)S(1)} %get-tuple-element.25), channel_id=1, source_target_pairs={{0,0},{1,40},{2,64},{3,104},{4,128},{5,168},{6,192},{7,232},{8,256... | collective-permute-start | bytes 67592 | tf_op jit(solution)/shard_map/ppermute | solution.py:226
  16.9 1.9 %collective-permute-start.1 = (bf16[512,896]{1,0:T(8,128)(2,1)S(1)}, bf16[512,896]{1,0:T(8,128)(2,1)S(1)}, u32[]{:S(2)}, u32[]{:S(2)}) collective-permute-start(bf16[512,896]{1,0:T(8,128)(2,1)S(1)} %get-tuple-element.28.refs_2_.refs_0_.refs_1_), channel_id=1, source_target_pairs={{0,16},{16,0},{1,17},{17,1},{2,18},{18,2},{3,19},{19,3},{4,20},{20... | collective-permute-start | bytes 2752520 | tf_op jit(solution)/shard_map/ppermute | solution.py:202
  19.6 8.9 %all-to-all-start = ((bf16[16,88,128]{2,1,0:T(8,128)(2,1)}), bf16[16,88,128]{2,1,0:T(8,128)(2,1)S(1)}, u32[]{:S(2)}, u32[]{:S(2)}) async-start(bf16[16,88,128]{2,1,0:T(8,128)(2,1)} %get-tuple-element.26), calls=%async_computation | async-start | bytes 720896 | tf_op jit(solution)/shard_map/all_to_all | solution.py:228
  28.5 1.9 %collective-permute-start.2 = (bf16[896,256]{1,0:T(8,128)(2,1)S(1)}, bf16[896,256]{1,0:T(8,128)(2,1)S(1)}, u32[]{:S(2)}, u32[]{:S(2)}) collective-permute-start(bf16[896,256]{1,0:T(8,128)(2,1)S(1)} %copy-done), channel_id=1, source_target_pairs={{0,16},{16,0},{1,17},{17,1},{2,18},{18,2},{3,19},{19,3},{4,20},{20... | collective-permute-start | bytes 1376264 | tf_op jit(solution)/shard_map/ppermute | solution.py:202
  30.4 1.8 %collective-permute-done.2.refs_5_ = bf16[896,256]{1,0:T(8,128)(2,1)S(1)} collective-permute-done((bf16[896,256]{1,0:T(8,128)(2,1)S(1)}, bf16[896,256]{1,0:T(8,128)(2,1)S(1)}, u32[]{:S(2)}, u32[]{:S(2)}) %collective-permute-start.2) | collective-permute-done | bytes 458784 | tf_op jit(solution)/shard_map/ppermute | solution.py:202
  32.2 9.0 %all-to-all-done.refs_1_ = bf16[16,88,128]{2,1,0:T(8,128)(2,1)S(1)} async-done(((bf16[16,88,128]{2,1,0:T(8,128)(2,1)}), bf16[16,88,128]{2,1,0:T(8,128)(2,1)S(1)}, u32[]{:S(2)}, u32[]{:S(2)}) %all-to-all-start) | async-done | bytes 360480 | tf_op jit(solution)/shard_map/all_to_all | solution.py:228
  41.2 2.3 %shard_map.87 = (bf16[16,240,128]{2,1,0:T(8,128)(2,1)}, bf16[192,512]{1,0:T(8,128)(2,1)S(1)}, bf16[192,512]{1,0:T(8,128)(2,1)S(1)}, f32[8,128]{1,0:T(8,128)S(1)}) custom-call(s32[2]{0:T(128)S(1)} %pad_add_fusion.refs_0_, bf16[16,88,128]{2,1,0:T(8,128)(2,1)S(1)} %all-to-all-done.refs_1_, bf16[512,896]{1,0:T(8,128)(2,1)S(1)} %get-tuple-element.28.refs_2_.refs_0_.refs_1_, ...), custom_call_target="tpu_custom_call" | custom-call | flops 528482304 | bytes 4489224 | tf_op jit(solution)/shard_map/pallas_call | solution.py:35
  44.2 9.7 %all-to-all-start.1 = ((bf16[16,240,128]{2,1,0:T(8,128)(2,1)}), bf16[16,240,128]{2,1,0:T(8,128)(2,1)S(1)}, u32[]{:S(2)}, u32[]{:S(2)}) async-start(bf16[16,240,128]{2,1,0:T(8,128)(2,1)} %get-tuple-element.29), calls=%async_computation.1 | async-start | bytes 1966080 | tf_op jit(solution)/shard_map/all_to_all | solution.py:252
  54.8 2.0 %collective-permute-start.3 = (bf16[512,896]{1,0:T(8,128)(2,1)}, bf16[512,896]{1,0:T(8,128)(2,1)}, u32[]{:S(2)}, u32[]{:S(2)}) collective-permute-start(bf16[512,896]{1,0:T(8,128)(2,1)} %get-tuple-element.32), channel_id=1, source_target_pairs={{0,32},{32,0},{1,33},{33,1},{2,34},{34,2},{3,35},{35,3},{4,36},{36... | collective-permute-start | bytes 2752520 | tf_op jit(solution)/shard_map/ppermute | solution.py:202
  57.5 1.9 %collective-permute-start.4 = (bf16[192,512]{1,0:T(8,128)(2,1)S(1)}, bf16[192,512]{1,0:T(8,128)(2,1)S(1)}, u32[]{:S(2)}, u32[]{:S(2)}) collective-permute-start(bf16[192,512]{1,0:T(8,128)(2,1)S(1)} %get-tuple-element.35), channel_id=1, source_target_pairs={{0,16},{16,0},{1,17},{17,1},{2,18},{18,2},{3,19},{19,3},{4,20},{20... | collective-permute-start | bytes 589832 | tf_op jit(solution)/shard_map/ppermute | solution.py:202
  59.4 16.6 %all-to-all-done.1.refs_0_ = bf16[16,240,128]{2,1,0:T(8,128)(2,1)S(1)} async-done(((bf16[16,240,128]{2,1,0:T(8,128)(2,1)}), bf16[16,240,128]{2,1,0:T(8,128)(2,1)S(1)}, u32[]{:S(2)}, u32[]{:S(2)}) %all-to-all-start.1) | async-done | bytes 983072 | tf_op jit(solution)/shard_map/all_to_all | solution.py:252
  77.0 3.8 %all-to-all-start.2 = ((bf16[8,240,128]{2,1,0:T(8,128)(2,1)}), bf16[8,240,128]{2,1,0:T(8,128)(2,1)S(1)}, u32[]{:S(2)}, u32[]{:S(2)}) async-start(bf16[8,240,128]{2,1,0:T(8,128)(2,1)} %get-tuple-element.30), calls=%async_computation.2 | async-start | bytes 983040 | tf_op jit(solution)/shard_map/all_to_all | solution.py:257
  80.8 5.7 %collective-permute-done.3.refs_0_.refs_3_ = bf16[512,896]{1,0:T(8,128)(2,1)} collective-permute-done((bf16[512,896]{1,0:T(8,128)(2,1)}, bf16[512,896]{1,0:T(8,128)(2,1)}, u32[]{:S(2)}, u32[]{:S(2)}) %collective-permute-start.3) | collective-permute-done | bytes 917536 | tf_op jit(solution)/shard_map/ppermute | solution.py:202
  86.4 2.2 %shard_map.91 = (bf16[512,896]{1,0:T(8,128)(2,1)}, f32[8,128]{1,0:T(8,128)}) custom-call(bf16[512,896]{1,0:T(8,128)(2,1)} %collective-permute-done.3.refs_0_.refs_3_, f32[8,128]{1,0:T(8,128)S(1)} %get-tuple-element.33.refs_1_, bf16[192,512]{1,0:T(8,128)(2,1)S(1)} %collective-permute-done.4.refs_2_.refs_1_), custom_call_target="tpu_custom_call" | custom-call | bytes 1835008 | tf_op jit(solution)/shard_map/pallas_call | solution.py:35
  88.6 1.9 %collective-permute-start.5 = (bf16[512,896]{1,0:T(8,128)(2,1)}, bf16[512,896]{1,0:T(8,128)(2,1)}, u32[]{:S(2)}, u32[]{:S(2)}) collective-permute-start(bf16[512,896]{1,0:T(8,128)(2,1)} %get-tuple-element.36), channel_id=1, source_target_pairs={{0,16},{16,0},{1,17},{17,1},{2,18},{18,2},{3,19},{19,3},{4,20},{20... | collective-permute-start | bytes 2752520 | tf_op jit(solution)/shard_map/ppermute | solution.py:202
  90.5 5.7 %all-to-all-done.2.refs_0_.refs_2_ = bf16[8,240,128]{2,1,0:T(8,128)(2,1)S(1)} async-done(((bf16[8,240,128]{2,1,0:T(8,128)(2,1)}), bf16[8,240,128]{2,1,0:T(8,128)(2,1)S(1)}, u32[]{:S(2)}, u32[]{:S(2)}) %all-to-all-start.2) | async-done | bytes 491552 | tf_op jit(solution)/shard_map/all_to_all | solution.py:257
  96.3 4.9 %collective-permute-start.8 = (bf16[8,240,128]{2,1,0:T(8,128)(2,1)S(1)}, bf16[8,240,128]{2,1,0:T(8,128)(2,1)S(1)}, u32[]{:S(2)}, u32[]{:S(2)}) collective-permute-start(bf16[8,240,128]{2,1,0:T(8,128)(2,1)S(1)} %all-to-all-done.2.refs_0_.refs_2_), channel_id=1, source_target_pairs={{0,32},{32,0},{1,33},{33,1},{2,34},{34,2},{3,35},{35,3},{4,36},{36... | collective-permute-start | bytes 1474568 | tf_op jit(solution)/shard_map/ppermute | solution.py:202
  101.2 2.7 %shard_map.92 = (bf16[16,44,128]{2,1,0:T(8,128)(2,1)S(1)}, f32[8,128]{1,0:T(8,128)S(1)}) custom-call(bf16[8,240,128]{2,1,0:T(8,128)(2,1)S(1)} %all-to-all-done.2.refs_0_.refs_2_, bf16[512,896]{1,0:T(8,128)(2,1)S(1)} %get-tuple-element.28.refs_2_.refs_0_.refs_1_, bf16[512,896]{1,0:T(8,128)(2,1)S(1)} %collective-permute-done.1.refs_3_.refs_2_, ...), custom_call_target="tpu_custom_call" | custom-call | flops 352321536 | bytes 4341760 | tf_op jit(solution)/shard_map/pallas_call | solution.py:35
  104.0 16.0 %all_to_all.20.refs_1_ = bf16[16,44,128]{2,1,0:T(8,128)(2,1)S(1)} all-to-all(bf16[16,44,128]{2,1,0:T(8,128)(2,1)S(1)} %get-tuple-element.37), channel_id=1, replica_groups=mesh['z'=8,'xh'=2,'core'=2,'xl'=2,'y'=8] {'xl','y'}, dimensions={0} | all-to-all | bytes 360448 | tf_op jit(solution)/shard_map/all_to_all | solution.py:272
  121.1 2.0 %collective-permute-start.6 = (bf16[11,512]{1,0:T(8,128)(2,1)S(1)}, bf16[11,512]{1,0:T(8,128)(2,1)S(1)}, u32[]{:S(2)}, u32[]{:S(2)}) collective-permute-start(bf16[11,512]{1,0:T(8,128)(2,1)S(1)} %get-tuple-element.38), channel_id=1, source_target_pairs={{0,0},{8,1},{64,2},{72,3},{128,4},{136,5},{192,6},{200,7},{256,8},... | collective-permute-start | bytes 33800 | tf_op jit(solution)/shard_map/ppermute | solution.py:282
  123.7 1.9 %collective-permute-start.7 = (bf16[8,240,128]{2,1,0:T(8,128)(2,1)S(1)}, bf16[8,240,128]{2,1,0:T(8,128)(2,1)S(1)}, u32[]{:S(2)}, u32[]{:S(2)}) collective-permute-start(bf16[8,240,128]{2,1,0:T(8,128)(2,1)S(1)} %get-tuple-element.42), channel_id=1, source_target_pairs={{0,16},{16,0},{1,17},{17,1},{2,18},{18,2},{3,19},{19,3},{4,20},{20... | collective-permute-start | bytes 1474568 | tf_op jit(solution)/shard_map/ppermute | solution.py:202
  125.7 2.4 %collective-permute-start.9 = (bf16[8,240,128]{2,1,0:T(8,128)(2,1)S(1)}, bf16[8,240,128]{2,1,0:T(8,128)(2,1)S(1)}, u32[]{:S(2)}, u32[]{:S(2)}) collective-permute-start(bf16[8,240,128]{2,1,0:T(8,128)(2,1)S(1)} %collective-permute-done.8.refs_4_), channel_id=1, source_target_pairs={{0,16},{16,0},{1,17},{17,1},{2,18},{18,2},{3,19},{19,3},{4,20},{20... | collective-permute-start | bytes 1474568 | tf_op jit(solution)/shard_map/ppermute | solution.py:202
  128.1 4.3 %collective-permute-done.6.refs_0_ = bf16[11,512]{1,0:T(8,128)(2,1)S(1)} collective-permute-done((bf16[11,512]{1,0:T(8,128)(2,1)S(1)}, bf16[11,512]{1,0:T(8,128)(2,1)S(1)}, u32[]{:S(2)}, u32[]{:S(2)}) %collective-permute-start.6) | collective-permute-done | bytes 11296 | tf_op jit(solution)/shard_map/ppermute | solution.py:282
  133.0 2.0 %shard_map.96 = (bf16[256,896]{1,0:T(8,128)(2,1)}, bf16[256,896]{1,0:T(8,128)(2,1)}, bf16[896,256]{1,0:T(8,128)(2,1)}, f32[8,128]{1,0:T(8,128)}) custom-call(bf16[192,512]{1,0:T(8,128)(2,1)S(1)} %get-tuple-element.40.refs_0_, bf16[192,512]{1,0:T(8,128)(2,1)S(1)} %collective-permute-done.4.refs_2_.refs_1_, ...), custom_call_target="tpu_custom_call" | custom-call | flops 528482304 | bytes 3735552 | tf_op jit(solution)/shard_map/pallas_call | solution.py:35
  (31 shorter events, 11.6 us)
Async XLA Ops:
  0.6 0.7 copy-start.5
  1.3 0.7 copy-start.6
  2.6 16.2 %collective-permute-start = (bf16[88,128]{1,0:T(8,128)(2,1)S(1)}, bf16[88,128]{1,0:T(8,128)(2,1)S(1)}, u32[]{:S(2)}, u32[]{:S(2)}) collective-permute-start(bf16[88,128]{1,0:T(8,128)(2,1)S(1)} %get-tuple-element.25), channel_id=1, source_target_pairs={{0,0},{1,40},{2,64},{3,104},{4,128},{5,168},{6,192},{7,232},{8,256... | collective-permute-start | bytes 67592 | tf_op jit(solution)/shard_map/ppermute | solution.py:226
  13.7 1.0 copy-start.1
  14.7 1.0 copy-start.2
  16.9 24.3 %collective-permute-start.1 = (bf16[512,896]{1,0:T(8,128)(2,1)S(1)}, bf16[512,896]{1,0:T(8,128)(2,1)S(1)}, u32[]{:S(2)}, u32[]{:S(2)}) collective-permute-start(bf16[512,896]{1,0:T(8,128)(2,1)S(1)} %get-tuple-element.28.refs_2_.refs_0_.refs_1_), channel_id=1, source_target_pairs={{0,16},{16,0},{1,17},{17,1},{2,18},{18,2},{3,19},{19,3},{4,20},{20... | collective-permute-start | bytes 2752520 | tf_op jit(solution)/shard_map/ppermute | solution.py:202
  19.6 8.9 %copy-start = (bf16[896,256]{1,0:T(8,128)(2,1)S(1)}, bf16[896,256]{1,0:T(8,128)(2,1)}, u32[]{:S(2)}) copy-start(bf16[896,256]{1,0:T(8,128)(2,1)} %refs_4_.1) | copy-start | bytes 1376260
  19.6 21.6 %all-to-all-start = ((bf16[16,88,128]{2,1,0:T(8,128)(2,1)}), bf16[16,88,128]{2,1,0:T(8,128)(2,1)S(1)}, u32[]{:S(2)}, u32[]{:S(2)}) async-start(bf16[16,88,128]{2,1,0:T(8,128)(2,1)} %get-tuple-element.26), calls=%async_computation | async-start | bytes 720896 | tf_op jit(solution)/shard_map/all_to_all | solution.py:228
  28.5 3.7 %collective-permute-start.2 = (bf16[896,256]{1,0:T(8,128)(2,1)S(1)}, bf16[896,256]{1,0:T(8,128)(2,1)S(1)}, u32[]{:S(2)}, u32[]{:S(2)}) collective-permute-start(bf16[896,256]{1,0:T(8,128)(2,1)S(1)} %copy-done), channel_id=1, source_target_pairs={{0,16},{16,0},{1,17},{17,1},{2,18},{18,2},{3,19},{19,3},{4,20},{20... | collective-permute-start | bytes 1376264 | tf_op jit(solution)/shard_map/ppermute | solution.py:202
  43.5 0.7 copy-start.3
  44.2 31.9 %all-to-all-start.1 = ((bf16[16,240,128]{2,1,0:T(8,128)(2,1)}), bf16[16,240,128]{2,1,0:T(8,128)(2,1)S(1)}, u32[]{:S(2)}, u32[]{:S(2)}) async-start(bf16[16,240,128]{2,1,0:T(8,128)(2,1)} %get-tuple-element.29), calls=%async_computation.1 | async-start | bytes 1966080 | tf_op jit(solution)/shard_map/all_to_all | solution.py:252
  53.8 3.0 %copy-start.4 = (bf16[192,512]{1,0:T(8,128)(2,1)S(1)}, bf16[192,512]{1,0:T(8,128)(2,1)}, u32[]{:S(2)}) copy-start(bf16[192,512]{1,0:T(8,128)(2,1)} %copy-done.3) | copy-start | bytes 589828
  54.8 31.6 %collective-permute-start.3 = (bf16[512,896]{1,0:T(8,128)(2,1)}, bf16[512,896]{1,0:T(8,128)(2,1)}, u32[]{:S(2)}, u32[]{:S(2)}) collective-permute-start(bf16[512,896]{1,0:T(8,128)(2,1)} %get-tuple-element.32), channel_id=1, source_target_pairs={{0,32},{32,0},{1,33},{33,1},{2,34},{34,2},{3,35},{35,3},{4,36},{36... | collective-permute-start | bytes 2752520 | tf_op jit(solution)/shard_map/ppermute | solution.py:202
  57.5 23.3 %collective-permute-start.4 = (bf16[192,512]{1,0:T(8,128)(2,1)S(1)}, bf16[192,512]{1,0:T(8,128)(2,1)S(1)}, u32[]{:S(2)}, u32[]{:S(2)}) collective-permute-start(bf16[192,512]{1,0:T(8,128)(2,1)S(1)} %get-tuple-element.35), channel_id=1, source_target_pairs={{0,16},{16,0},{1,17},{17,1},{2,18},{18,2},{3,19},{19,3},{4,20},{20... | collective-permute-start | bytes 589832 | tf_op jit(solution)/shard_map/ppermute | solution.py:202
  77.0 19.3 %all-to-all-start.2 = ((bf16[8,240,128]{2,1,0:T(8,128)(2,1)}), bf16[8,240,128]{2,1,0:T(8,128)(2,1)S(1)}, u32[]{:S(2)}, u32[]{:S(2)}) async-start(bf16[8,240,128]{2,1,0:T(8,128)(2,1)} %get-tuple-element.30), calls=%async_computation.2 | async-start | bytes 983040 | tf_op jit(solution)/shard_map/all_to_all | solution.py:257
  88.6 12.6 %collective-permute-start.5 = (bf16[512,896]{1,0:T(8,128)(2,1)}, bf16[512,896]{1,0:T(8,128)(2,1)}, u32[]{:S(2)}, u32[]{:S(2)}) collective-permute-start(bf16[512,896]{1,0:T(8,128)(2,1)} %get-tuple-element.36), channel_id=1, source_target_pairs={{0,16},{16,0},{1,17},{17,1},{2,18},{18,2},{3,19},{19,3},{4,20},{20... | collective-permute-start | bytes 2752520 | tf_op jit(solution)/shard_map/ppermute | solution.py:202
  96.3 29.4 %collective-permute-start.8 = (bf16[8,240,128]{2,1,0:T(8,128)(2,1)S(1)}, bf16[8,240,128]{2,1,0:T(8,128)(2,1)S(1)}, u32[]{:S(2)}, u32[]{:S(2)}) collective-permute-start(bf16[8,240,128]{2,1,0:T(8,128)(2,1)S(1)} %all-to-all-done.2.refs_0_.refs_2_), channel_id=1, source_target_pairs={{0,32},{32,0},{1,33},{33,1},{2,34},{34,2},{3,35},{35,3},{4,36},{36... | collective-permute-start | bytes 1474568 | tf_op jit(solution)/shard_map/ppermute | solution.py:202
  121.1 11.3 %collective-permute-start.6 = (bf16[11,512]{1,0:T(8,128)(2,1)S(1)}, bf16[11,512]{1,0:T(8,128)(2,1)S(1)}, u32[]{:S(2)}, u32[]{:S(2)}) collective-permute-start(bf16[11,512]{1,0:T(8,128)(2,1)S(1)} %get-tuple-element.38), channel_id=1, source_target_pairs={{0,0},{8,1},{64,2},{72,3},{128,4},{136,5},{192,6},{200,7},{256,8},... | collective-permute-start | bytes 33800 | tf_op jit(solution)/shard_map/ppermute | solution.py:282
  123.7 9.3 %collective-permute-start.7 = (bf16[8,240,128]{2,1,0:T(8,128)(2,1)S(1)}, bf16[8,240,128]{2,1,0:T(8,128)(2,1)S(1)}, u32[]{:S(2)}, u32[]{:S(2)}) collective-permute-start(bf16[8,240,128]{2,1,0:T(8,128)(2,1)S(1)} %get-tuple-element.42), channel_id=1, source_target_pairs={{0,16},{16,0},{1,17},{17,1},{2,18},{18,2},{3,19},{19,3},{4,20},{20... | collective-permute-start | bytes 1474568 | tf_op jit(solution)/shard_map/ppermute | solution.py:202
  125.7 7.3 %collective-permute-start.9 = (bf16[8,240,128]{2,1,0:T(8,128)(2,1)S(1)}, bf16[8,240,128]{2,1,0:T(8,128)(2,1)S(1)}, u32[]{:S(2)}, u32[]{:S(2)}) collective-permute-start(bf16[8,240,128]{2,1,0:T(8,128)(2,1)S(1)} %collective-permute-done.8.refs_4_), channel_id=1, source_target_pairs={{0,16},{16,0},{1,17},{17,1},{2,18},{18,2},{3,19},{19,3},{4,20},{20... | collective-permute-start | bytes 1474568 | tf_op jit(solution)/shard_map/ppermute | solution.py:202

commit v4 on v3

--- a/solution.py
+++ b/solution.py
@@ -59,7 +59,8 @@
         copy.wait()
 
 
-def pack_kernel(place, tok, cot, out, wide):
+def pack_kernel(place, tok_hbm, cot_hbm, out, wide, tok, cot, sems):
+    fetch(sems, (tok_hbm, tok), (cot_hbm, cot))
     odd = place[0] == 1
     for base, ref in ((0, tok), (4, cot)):
         rows = ref[...].astype(F32)
@@ -108,7 +109,9 @@
         out[t] = packed[...]
 
 
-def forward_kernel(place, rows, gu0, gu1, down0, down1, out, x_own, x_oth, wide, parts, sems):
+def forward_kernel(
+    place, rows, gu0, gu1, down0, down1, out, own_out, oth_out, wide, parts, x_own, x_oth, sems
+):
     for t in range(16):
         wide[t * 88 : (t + 1) * 88, :] = rows[t].astype(F32)
     blank = jnp.zeros((PADDED - QUARTER, 128), F32)
@@ -120,7 +123,12 @@
             ref[far * PADDED : (far + 1) * PADDED, at : at + 128] = piece.astype(BF16)
     by_cols = (((1,), (0,)), ((), ()))
     by_rows = (((1,), (1,)), ((), ()))
-    copies = []
+    copies = [
+        pltpu.make_async_copy(x_own, own_out, sems.at[3]),
+        pltpu.make_async_copy(x_oth, oth_out, sems.at[4]),
+    ]
+    for copy in copies:
+        copy.start()
     for m in range(3):
         cols, dims = (slice(256, 512), by_rows) if m == 2 else (slice(0, 256), by_cols)
         own, oth = (down0[...], down1[...]) if m == 2 else (gu[m * 256 : (m + 1) * 256, :] for gu in (gu0, gu1))
@@ -130,7 +138,7 @@
         put_tiles(parts, m, total[PADDED:], 1 - place[1])
         here = pl.ds(m * SIZE, SIZE)
         copies.append(pltpu.make_async_copy(parts.at[:, here], out.at[:, here], sems.at[m]))
-        copies[m].start()
+        copies[-1].start()
     for copy in copies:
         copy.wait()
 
@@ -194,8 +202,12 @@
     out[...] = x[...]
 
 
-def after(x, *deps, flops=0):
-    return call(copy_kernel, (shape(*x.shape, dtype=x.dtype),), (x,), deps=deps, flops=flops)[0]
+def after(x, *deps):
+    return call(copy_kernel, (shape(*x.shape, dtype=x.dtype),), (x,), deps=deps)[0]
+
+
+def in_hbm(x):
+    return pltpu.with_memory_space_constraint(x, pltpu.HBM)
 
 
 def swap(axis, x):
@@ -216,12 +228,17 @@
     there = permutation(lambda z, xh, c, xl, y: (4 * xl + y // 2, y % 2, c, xh ^ y % 2, z))
     home = [(b, a) for a, b in permutation(lambda z, xh, c, xl, y: (4 * xl + y // 2, xh, c, xh ^ y % 2, z))]
 
-    packed, ready = call(
+    packed, ready0 = call(
         pack_kernel,
         (shape(88, 128),),
-        (place, tokens, cotangent),
-        [pltpu.VMEM((88, 128), F32)],
-        specs=[SMEM, VMEM, VMEM],
+        (place, in_hbm(tokens), in_hbm(cotangent)),
+        [
+            pltpu.VMEM((88, 128), F32),
+            pltpu.VMEM((ROWS, 512), BF16),
+            pltpu.VMEM((ROWS, 512), BF16),
+            pltpu.SemaphoreType.DMA((2,)),
+        ],
+        specs=[SMEM, HBM, HBM],
     )
     packed = lax.ppermute(packed, ALL, there)
     spread, _ = call(spread_kernel, (shape(16, 88, 128),), (packed,), flops=10**11)
@@ -229,25 +246,26 @@
     gu0, _ = call(
         weights_kernel,
         (shape(512, 896),),
-        (gate_weight, up_weight),
+        (in_hbm(gate_weight), in_hbm(up_weight)),
         [pltpu.SemaphoreType.DMA((2,))],
         specs=[HBM, HBM],
-        deps=(ready,),
+        deps=(ready0,),
     )
     gu1, down1 = swap("core", gu0), swap("core", down_weight)
 
     parts, x_own, x_oth, ready = call(
         forward_kernel,
-        (pltpu.HBM((16, 3 * SIZE, 128), BF16), shape(2 * PADDED, 512), shape(2 * PADDED, 512)),
+        (pltpu.HBM((16, 3 * SIZE, 128), BF16), *[pltpu.HBM((2 * PADDED, 512), BF16)] * 2),
         (place, rows, gu0, gu1, down_weight, down1),
         [
             pltpu.VMEM((16 * 88, 128), F32),
             pltpu.VMEM((16, 3 * SIZE, 128), BF16),
-            pltpu.SemaphoreType.DMA((3,)),
+            pltpu.VMEM((2 * PADDED, 512), BF16),
+            pltpu.VMEM((2 * PADDED, 512), BF16),
+            pltpu.SemaphoreType.DMA((5,)),
         ],
         specs=[SMEM] + [VMEM] * 5,
-        outs=[HBM, VMEM, VMEM],
-        flops=12 * PADDED * 512 * 896,
+        outs=[HBM] * 3,
     )
     parts = lax.all_to_all(parts, ("z", "xh"), 0, 0, tiled=True)
     x_got = swap("core", after(x_oth, ready))
@@ -256,8 +274,6 @@
     acts0, ready = call(activation_kernel, (shape(8, 3 * SIZE, 128),), (parts,))
     acts0 = lax.all_to_all(acts0, "z", 0, 0, tiled=True)
     gu3 = swap("core", after(gu2, ready, x_got))
-    acts2 = swap("xh", acts0)
-
     token_parts, ready = call(
         token_grad_kernel,
         (shape(16, 4 * ROWS, 128),),
@@ -267,10 +283,11 @@
             pltpu.VMEM((PADDED, 896), BF16),
             pltpu.VMEM((2, 4 * QUARTER, 128), F32),
         ],
-        flops=4 * PADDED * 1024 * 896,
     )
     token_parts = lax.all_to_all(token_parts, TENSOR, 0, 0, tiled=True)
-    acts1 = swap("core", after(acts0, ready))
+    acts2 = swap("xh", acts0)
+    acts1 = swap("core", acts0)
+    acts3 = swap("core", acts2)
 
     grad_tokens, _ = call(
         token_sum_kernel,
@@ -278,18 +295,17 @@
         (place, token_parts),
         [pltpu.VMEM((4 * ROWS, 128), F32)],
         specs=[SMEM, VMEM],
-    )
-    grad_tokens = after(lax.ppermute(grad_tokens, ALL, home), flops=10**11)
-    acts3 = swap("core", acts2)
-
-    grad_gate, grad_up, grad_down, _ = call(
+        flops=10**11,
+    )
+    grad_tokens = lax.ppermute(grad_tokens, ALL, home)
+
+    grad_gate, grad_up, grad_down, ready = call(
         weight_grad_kernel,
         (shape(256, 896), shape(256, 896), shape(896, 256)),
         (x_own, x_got, acts0, acts1, acts2, acts3),
         [pltpu.VMEM((4 * PADDED, 512), BF16), pltpu.VMEM((4 * PADDED, 896), BF16)],
-        flops=6 * 4 * PADDED * 256 * 896,
-    )
-    return (grad_tokens, grad_gate, grad_up, grad_down)
+    )
+    return (after(grad_tokens, ready), grad_gate, grad_up, grad_down)
 
 
 def solution(mesh):

time: 136 us -> 133 us (0.978)
  blocking collectives: 16 us -> 0 us
  starting transfers between devices: 54.3 us -> 64.1 us
  waiting for transfers between devices: 43.1 us -> 49.6 us
  local copies, waits for them, and re-layouts: 4.06 us -> 0.01 us
  Pallas kernels: 16.6 us -> 18 us
    all_to_all x1 -> x0, blocking collectives: 16 us -> none  [per_device(): token_parts = lax.all_to_all(token_parts, TENSOR, 0, 0, tiled=True)]
    all_to_all x0 -> x1, starting transfers between devices: none -> 7.59 us  [per_device(): token_parts = lax.all_to_all(token_parts, TENSOR, 0, 0, tiled=True)]
    all_to_all x0 -> x1, waiting for transfers between devices: none -> 4.07 us  [per_device(): token_parts = lax.all_to_all(token_parts, TENSOR, 0, 0, tiled=True)]
    unnamed x14 -> x6, local copies, waits for them, and re-layouts: 4.06 us -> 0.01 us
    ppermute x1, waiting for transfers between devices: 4.3 us -> 7.28 us  [per_device(): grad_tokens = lax.ppermute(grad_tokens, ALL, home)]
    pallas_call x13 -> x12, Pallas kernels: 16.6 us -> 18 us  [call(): pl.pallas_call(body, out_shape=(*out_shape, shape(8, 128, dtype=F32)), in...]
    all_to_all x1, starting transfers between devices: 9.65 us -> 11 us  [per_device(): parts = lax.all_to_all(parts, ('z', 'xh'), 0, 0, tiled=True)]
  transfers between devices with their start and end apart: 13 -> 14, of which waited for: 6 -> 7; matrix products, arithmetic and copies ran while one was open for 0% -> 0% of each run, Pallas kernels for 9% -> 10%
where the time goes in v4:
time: 133 us
  starting transfers between devices  64.1 us (48%)
  waiting for transfers between devices  49.6 us (37%)
  Pallas kernels  18 us (14%)
    ppermute x8, starting transfers between devices, swap(): return lax.ppermute(x, axis, [(0, 1), (1, 0)])  19.1 us
    pallas_call x12, Pallas kernels, call(): pl.pallas_call(body, out_shape=(*out_shape, shape(8, 128, dtype=F32)), in...  18 us
    all_to_all x1, waiting for transfers between devices, per_device(): parts = lax.all_to_all(parts, ('z', 'xh'), 0, 0, tiled=True)  16.6 us
    ppermute x1, starting transfers between devices, per_device(): packed = lax.ppermute(packed, ALL, there)  11.1 us
    all_to_all x1, starting transfers between devices, per_device(): parts = lax.all_to_all(parts, ('z', 'xh'), 0, 0, tiled=True)  11 us
    all_to_all x1, starting transfers between devices, per_device(): rows = lax.all_to_all(spread, TENSOR, 0, 0, tiled=True)  9.43 us
    all_to_all x1, waiting for transfers between devices, per_device(): rows = lax.all_to_all(spread, TENSOR, 0, 0, tiled=True)  8.46 us
    all_to_all x1, starting transfers between devices, per_device(): token_parts = lax.all_to_all(token_parts, TENSOR, 0, 0, tiled=True)  7.59 us
  transfers between devices with their start and end apart: 14, of which 7 were waited for; matrix products, arithmetic and copies ran while one was open for 0% of the time, Pallas kernels for 10%

profile of v4, /device:TPU:14, one launch (start us, length us, event | category | flops | bytes accessed | tf_op | source)
XLA Modules:
  0.0 132.6 jit_solution(9244193671028690800)
XLA Ops:
  2.0 11.1 %collective-permute-start = (bf16[88,128]{1,0:T(8,128)(2,1)S(1)}, bf16[88,128]{1,0:T(8,128)(2,1)S(1)}, u32[]{:S(2)}, u32[]{:S(2)}) collective-permute-start(bf16[88,128]{1,0:T(8,128)(2,1)S(1)} %get-tuple-element.24), channel_id=1, source_target_pairs={{0,0},{1,40},{2,64},{3,104},{4,128},{5,168},{6,192},{7,232},{8,256... | collective-permute-start | bytes 67592 | tf_op jit(solution)/shard_map/ppermute | solution.py:243
  14.9 1.9 %collective-permute-start.1 = (bf16[512,896]{1,0:T(8,128)(2,1)S(1)}, bf16[512,896]{1,0:T(8,128)(2,1)S(1)}, u32[]{:S(2)}, u32[]{:S(2)}) collective-permute-start(bf16[512,896]{1,0:T(8,128)(2,1)S(1)} %get-tuple-element.27.refs_2_.refs_0_.refs_1_), channel_id=1, source_target_pairs={{0,16},{16,0},{1,17},{17,1},{2,18},{18,2},{3,19},{19,3},{4,20},{20... | collective-permute-start | bytes 2752520 | tf_op jit(solution)/shard_map/ppermute | solution.py:214
  17.6 9.4 %all-to-all-start = ((bf16[16,88,128]{2,1,0:T(8,128)(2,1)}), bf16[16,88,128]{2,1,0:T(8,128)(2,1)S(1)}, u32[]{:S(2)}, u32[]{:S(2)}) async-start(bf16[16,88,128]{2,1,0:T(8,128)(2,1)} %get-tuple-element.25), calls=%async_computation | async-start | bytes 720896 | tf_op jit(solution)/shard_map/all_to_all | solution.py:245
  27.0 1.9 %collective-permute-start.2 = (bf16[896,256]{1,0:T(8,128)(2,1)S(1)}, bf16[896,256]{1,0:T(8,128)(2,1)S(1)}, u32[]{:S(2)}, u32[]{:S(2)}) collective-permute-start(bf16[896,256]{1,0:T(8,128)(2,1)S(1)} %copy-done), channel_id=1, source_target_pairs={{0,16},{16,0},{1,17},{17,1},{2,18},{18,2},{3,19},{19,3},{4,20},{20... | collective-permute-start | bytes 1376264 | tf_op jit(solution)/shard_map/ppermute | solution.py:214
  30.8 8.5 %all-to-all-done.refs_1_ = bf16[16,88,128]{2,1,0:T(8,128)(2,1)S(1)} async-done(((bf16[16,88,128]{2,1,0:T(8,128)(2,1)}), bf16[16,88,128]{2,1,0:T(8,128)(2,1)S(1)}, u32[]{:S(2)}, u32[]{:S(2)}) %all-to-all-start) | async-done | bytes 360480 | tf_op jit(solution)/shard_map/all_to_all | solution.py:245
  39.2 2.3 %shard_map.87 = (bf16[16,240,128]{2,1,0:T(8,128)(2,1)}, bf16[192,512]{1,0:T(8,128)(2,1)}, bf16[192,512]{1,0:T(8,128)(2,1)}, f32[8,128]{1,0:T(8,128)S(1)}) custom-call(s32[2]{0:T(128)S(1)} %pad_add_fusion.refs_0_, bf16[16,88,128]{2,1,0:T(8,128)(2,1)S(1)} %all-to-all-done.refs_1_, bf16[512,896]{1,0:T(8,128)(2,1)S(1)} %get-tuple-element.27.refs_2_.refs_0_.refs_1_, ...), custom_call_target="tpu_custom_call" | custom-call | bytes 4489224 | tf_op jit(solution)/shard_map/pallas_call | solution.py:35
  41.5 11.0 %all-to-all-start.1 = ((bf16[16,240,128]{2,1,0:T(8,128)(2,1)}), bf16[16,240,128]{2,1,0:T(8,128)(2,1)S(1)}, u32[]{:S(2)}, u32[]{:S(2)}) async-start(bf16[16,240,128]{2,1,0:T(8,128)(2,1)} %get-tuple-element.28), calls=%async_computation.1 | async-start | bytes 1966080 | tf_op jit(solution)/shard_map/all_to_all | solution.py:270
  53.6 2.0 %collective-permute-start.3 = (bf16[512,896]{1,0:T(8,128)(2,1)}, bf16[512,896]{1,0:T(8,128)(2,1)}, u32[]{:S(2)}, u32[]{:S(2)}) collective-permute-start(bf16[512,896]{1,0:T(8,128)(2,1)} %get-tuple-element.31), channel_id=1, source_target_pairs={{0,32},{32,0},{1,33},{33,1},{2,34},{34,2},{3,35},{35,3},{4,36},{36... | collective-permute-start | bytes 2752520 | tf_op jit(solution)/shard_map/ppermute | solution.py:214
  56.2 1.9 %collective-permute-start.4 = (bf16[192,512]{1,0:T(8,128)(2,1)S(1)}, bf16[192,512]{1,0:T(8,128)(2,1)S(1)}, u32[]{:S(2)}, u32[]{:S(2)}) collective-permute-start(bf16[192,512]{1,0:T(8,128)(2,1)S(1)} %get-tuple-element.34), channel_id=1, source_target_pairs={{0,16},{16,0},{1,17},{17,1},{2,18},{18,2},{3,19},{19,3},{4,20},{20... | collective-permute-start | bytes 589832 | tf_op jit(solution)/shard_map/ppermute | solution.py:214
  58.1 16.6 %all-to-all-done.1.refs_0_ = bf16[16,240,128]{2,1,0:T(8,128)(2,1)S(1)} async-done(((bf16[16,240,128]{2,1,0:T(8,128)(2,1)}), bf16[16,240,128]{2,1,0:T(8,128)(2,1)S(1)}, u32[]{:S(2)}, u32[]{:S(2)}) %all-to-all-start.1) | async-done | bytes 983072 | tf_op jit(solution)/shard_map/all_to_all | solution.py:270
  75.7 3.8 %all-to-all-start.2 = ((bf16[8,240,128]{2,1,0:T(8,128)(2,1)}), bf16[8,240,128]{2,1,0:T(8,128)(2,1)S(1)}, u32[]{:S(2)}, u32[]{:S(2)}) async-start(bf16[8,240,128]{2,1,0:T(8,128)(2,1)} %get-tuple-element.29), calls=%async_computation.2 | async-start | bytes 983040 | tf_op jit(solution)/shard_map/all_to_all | solution.py:275
  79.5 5.7 %collective-permute-done.3.refs_0_.refs_3_ = bf16[512,896]{1,0:T(8,128)(2,1)} collective-permute-done((bf16[512,896]{1,0:T(8,128)(2,1)}, bf16[512,896]{1,0:T(8,128)(2,1)}, u32[]{:S(2)}, u32[]{:S(2)}) %collective-permute-start.3) | collective-permute-done | bytes 917536 | tf_op jit(solution)/shard_map/ppermute | solution.py:214
  85.2 2.2 %shard_map.91 = (bf16[512,896]{1,0:T(8,128)(2,1)}, f32[8,128]{1,0:T(8,128)}) custom-call(bf16[512,896]{1,0:T(8,128)(2,1)} %collective-permute-done.3.refs_0_.refs_3_, f32[8,128]{1,0:T(8,128)S(1)} %get-tuple-element.32.refs_1_, bf16[192,512]{1,0:T(8,128)(2,1)S(1)} %collective-permute-done.4.refs_2_.refs_1_), custom_call_target="tpu_custom_call" | custom-call | bytes 1835008 | tf_op jit(solution)/shard_map/pallas_call | solution.py:35
  87.4 1.9 %collective-permute-start.5 = (bf16[512,896]{1,0:T(8,128)(2,1)}, bf16[512,896]{1,0:T(8,128)(2,1)}, u32[]{:S(2)}, u32[]{:S(2)}) collective-permute-start(bf16[512,896]{1,0:T(8,128)(2,1)} %get-tuple-element.35), channel_id=1, source_target_pairs={{0,16},{16,0},{1,17},{17,1},{2,18},{18,2},{3,19},{19,3},{4,20},{20... | collective-permute-start | bytes 2752520 | tf_op jit(solution)/shard_map/ppermute | solution.py:214
  89.3 5.7 %all-to-all-done.2.refs_0_.refs_2_ = bf16[8,240,128]{2,1,0:T(8,128)(2,1)S(1)} async-done(((bf16[8,240,128]{2,1,0:T(8,128)(2,1)}), bf16[8,240,128]{2,1,0:T(8,128)(2,1)S(1)}, u32[]{:S(2)}, u32[]{:S(2)}) %all-to-all-start.2) | async-done | bytes 491552 | tf_op jit(solution)/shard_map/all_to_all | solution.py:275
  95.0 4.9 %collective-permute-start.8 = (bf16[8,240,128]{2,1,0:T(8,128)(2,1)S(1)}, bf16[8,240,128]{2,1,0:T(8,128)(2,1)S(1)}, u32[]{:S(2)}, u32[]{:S(2)}) collective-permute-start(bf16[8,240,128]{2,1,0:T(8,128)(2,1)S(1)} %all-to-all-done.2.refs_0_.refs_2_), channel_id=1, source_target_pairs={{0,32},{32,0},{1,33},{33,1},{2,34},{34,2},{3,35},{35,3},{4,36},{36... | collective-permute-start | bytes 1474568 | tf_op jit(solution)/shard_map/ppermute | solution.py:214
  100.0 3.4 %shard_map.92 = (bf16[16,44,128]{2,1,0:T(8,128)(2,1)}, f32[8,128]{1,0:T(8,128)}) custom-call(bf16[8,240,128]{2,1,0:T(8,128)(2,1)S(1)} %all-to-all-done.2.refs_0_.refs_2_, bf16[512,896]{1,0:T(8,128)(2,1)S(1)} %get-tuple-element.27.refs_2_.refs_0_.refs_1_, bf16[512,896]{1,0:T(8,128)(2,1)S(1)} %collective-permute-done.1.refs_3_.refs_2_, ...), custom_call_target="tpu_custom_call" | custom-call | bytes 4341760 | tf_op jit(solution)/shard_map/pallas_call | solution.py:35
  103.4 7.6 %all-to-all-start.3 = ((bf16[16,44,128]{2,1,0:T(8,128)(2,1)}), bf16[16,44,128]{2,1,0:T(8,128)(2,1)S(1)}, u32[]{:S(2)}, u32[]{:S(2)}) async-start(bf16[16,44,128]{2,1,0:T(8,128)(2,1)} %get-tuple-element.36), calls=%async_computation.3 | async-start | bytes 393216 | tf_op jit(solution)/shard_map/all_to_all | solution.py:287
  111.0 2.1 %collective-permute-start.7 = (bf16[8,240,128]{2,1,0:T(8,128)(2,1)S(1)}, bf16[8,240,128]{2,1,0:T(8,128)(2,1)S(1)}, u32[]{:S(2)}, u32[]{:S(2)}) collective-permute-start(bf16[8,240,128]{2,1,0:T(8,128)(2,1)S(1)} %all-to-all-done.2.refs_0_.refs_2_), channel_id=1, source_target_pairs={{0,16},{16,0},{1,17},{17,1},{2,18},{18,2},{3,19},{19,3},{4,20},{20... | collective-permute-start | bytes 1474568 | tf_op jit(solution)/shard_map/ppermute | solution.py:214
  113.1 2.4 %collective-permute-start.9 = (bf16[8,240,128]{2,1,0:T(8,128)(2,1)S(1)}, bf16[8,240,128]{2,1,0:T(8,128)(2,1)S(1)}, u32[]{:S(2)}, u32[]{:S(2)}) collective-permute-start(bf16[8,240,128]{2,1,0:T(8,128)(2,1)S(1)} %collective-permute-done.8.refs_4_), channel_id=1, source_target_pairs={{0,16},{16,0},{1,17},{17,1},{2,18},{18,2},{3,19},{19,3},{4,20},{20... | collective-permute-start | bytes 1474568 | tf_op jit(solution)/shard_map/ppermute | solution.py:214
  115.5 4.1 %all-to-all-done.3.refs_1_ = bf16[16,44,128]{2,1,0:T(8,128)(2,1)S(1)} async-done(((bf16[16,44,128]{2,1,0:T(8,128)(2,1)}), bf16[16,44,128]{2,1,0:T(8,128)(2,1)S(1)}, u32[]{:S(2)}, u32[]{:S(2)}) %all-to-all-start.3) | async-done | bytes 180256 | tf_op jit(solution)/shard_map/all_to_all | solution.py:287
  120.7 2.1 %collective-permute-start.6 = (bf16[11,512]{1,0:T(8,128)(2,1)S(1)}, bf16[11,512]{1,0:T(8,128)(2,1)S(1)}, u32[]{:S(2)}, u32[]{:S(2)}) collective-permute-start(bf16[11,512]{1,0:T(8,128)(2,1)S(1)} %get-tuple-element.37), channel_id=1, source_target_pairs={{0,0},{8,1},{64,2},{72,3},{128,4},{136,5},{192,6},{200,7},{256,8},... | collective-permute-start | bytes 33800 | tf_op jit(solution)/shard_map/ppermute | solution.py:300
  122.8 2.0 %shard_map.94 = (bf16[256,896]{1,0:T(8,128)(2,1)}, bf16[256,896]{1,0:T(8,128)(2,1)}, bf16[896,256]{1,0:T(8,128)(2,1)}, f32[8,128]{1,0:T(8,128)S(1)}) custom-call(bf16[192,512]{1,0:T(8,128)(2,1)S(1)} %copy-done.1, bf16[192,512]{1,0:T(8,128)(2,1)S(1)} %collective-permute-done.4.refs_2_.refs_1_, bf16[8,240,128]{2,1,0:T(8,128)(2,1)S(1)} %all-to-all-done.2.refs_0_.refs_2_, ...), custom_call_target="tpu_custom_call" | custom-call | bytes 3735552 | tf_op jit(solution)/shard_map/pallas_call | solution.py:35
  124.8 7.3 %collective-permute-done.6.refs_0_ = bf16[11,512]{1,0:T(8,128)(2,1)S(1)} collective-permute-done((bf16[11,512]{1,0:T(8,128)(2,1)S(1)}, bf16[11,512]{1,0:T(8,128)(2,1)S(1)}, u32[]{:S(2)}, u32[]{:S(2)}) %collective-permute-start.6) | collective-permute-done | bytes 11296 | tf_op jit(solution)/shard_map/ppermute | solution.py:300
  (23 shorter events, 10.1 us)
Async XLA Ops:
  2.0 14.8 %collective-permute-start = (bf16[88,128]{1,0:T(8,128)(2,1)S(1)}, bf16[88,128]{1,0:T(8,128)(2,1)S(1)}, u32[]{:S(2)}, u32[]{:S(2)}) collective-permute-start(bf16[88,128]{1,0:T(8,128)(2,1)S(1)} %get-tuple-element.24), channel_id=1, source_target_pairs={{0,0},{1,40},{2,64},{3,104},{4,128},{5,168},{6,192},{7,232},{8,256... | collective-permute-start | bytes 67592 | tf_op jit(solution)/shard_map/ppermute | solution.py:243
  14.9 24.3 %collective-permute-start.1 = (bf16[512,896]{1,0:T(8,128)(2,1)S(1)}, bf16[512,896]{1,0:T(8,128)(2,1)S(1)}, u32[]{:S(2)}, u32[]{:S(2)}) collective-permute-start(bf16[512,896]{1,0:T(8,128)(2,1)S(1)} %get-tuple-element.27.refs_2_.refs_0_.refs_1_), channel_id=1, source_target_pairs={{0,16},{16,0},{1,17},{17,1},{2,18},{18,2},{3,19},{19,3},{4,20},{20... | collective-permute-start | bytes 2752520 | tf_op jit(solution)/shard_map/ppermute | solution.py:214
  17.6 9.4 %copy-start = (bf16[896,256]{1,0:T(8,128)(2,1)S(1)}, bf16[896,256]{1,0:T(8,128)(2,1)}, u32[]{:S(2)}) copy-start(bf16[896,256]{1,0:T(8,128)(2,1)} %refs_4_.1) | copy-start | bytes 1376260
  17.6 21.6 %all-to-all-start = ((bf16[16,88,128]{2,1,0:T(8,128)(2,1)}), bf16[16,88,128]{2,1,0:T(8,128)(2,1)S(1)}, u32[]{:S(2)}, u32[]{:S(2)}) async-start(bf16[16,88,128]{2,1,0:T(8,128)(2,1)} %get-tuple-element.25), calls=%async_computation | async-start | bytes 720896 | tf_op jit(solution)/shard_map/all_to_all | solution.py:245
  27.0 3.7 %collective-permute-start.2 = (bf16[896,256]{1,0:T(8,128)(2,1)S(1)}, bf16[896,256]{1,0:T(8,128)(2,1)S(1)}, u32[]{:S(2)}, u32[]{:S(2)}) collective-permute-start(bf16[896,256]{1,0:T(8,128)(2,1)S(1)} %copy-done), channel_id=1, source_target_pairs={{0,16},{16,0},{1,17},{17,1},{2,18},{18,2},{3,19},{19,3},{4,20},{20... | collective-permute-start | bytes 1376264 | tf_op jit(solution)/shard_map/ppermute | solution.py:214
  41.5 33.2 %all-to-all-start.1 = ((bf16[16,240,128]{2,1,0:T(8,128)(2,1)}), bf16[16,240,128]{2,1,0:T(8,128)(2,1)S(1)}, u32[]{:S(2)}, u32[]{:S(2)}) async-start(bf16[16,240,128]{2,1,0:T(8,128)(2,1)} %get-tuple-element.28), calls=%async_computation.1 | async-start | bytes 1966080 | tf_op jit(solution)/shard_map/all_to_all | solution.py:270
  52.6 3.0 %copy-start.2 = (bf16[192,512]{1,0:T(8,128)(2,1)S(1)}, bf16[192,512]{1,0:T(8,128)(2,1)}, u32[]{:S(2)}) copy-start(bf16[192,512]{1,0:T(8,128)(2,1)} %get-tuple-element.33.refs_0_) | copy-start | bytes 589828
  53.6 31.6 %collective-permute-start.3 = (bf16[512,896]{1,0:T(8,128)(2,1)}, bf16[512,896]{1,0:T(8,128)(2,1)}, u32[]{:S(2)}, u32[]{:S(2)}) collective-permute-start(bf16[512,896]{1,0:T(8,128)(2,1)} %get-tuple-element.31), channel_id=1, source_target_pairs={{0,32},{32,0},{1,33},{33,1},{2,34},{34,2},{3,35},{35,3},{4,36},{36... | collective-permute-start | bytes 2752520 | tf_op jit(solution)/shard_map/ppermute | solution.py:214
  56.2 23.3 %collective-permute-start.4 = (bf16[192,512]{1,0:T(8,128)(2,1)S(1)}, bf16[192,512]{1,0:T(8,128)(2,1)S(1)}, u32[]{:S(2)}, u32[]{:S(2)}) collective-permute-start(bf16[192,512]{1,0:T(8,128)(2,1)S(1)} %get-tuple-element.34), channel_id=1, source_target_pairs={{0,16},{16,0},{1,17},{17,1},{2,18},{18,2},{3,19},{19,3},{4,20},{20... | collective-permute-start | bytes 589832 | tf_op jit(solution)/shard_map/ppermute | solution.py:214
  75.7 19.3 %all-to-all-start.2 = ((bf16[8,240,128]{2,1,0:T(8,128)(2,1)}), bf16[8,240,128]{2,1,0:T(8,128)(2,1)S(1)}, u32[]{:S(2)}, u32[]{:S(2)}) async-start(bf16[8,240,128]{2,1,0:T(8,128)(2,1)} %get-tuple-element.29), calls=%async_computation.2 | async-start | bytes 983040 | tf_op jit(solution)/shard_map/all_to_all | solution.py:275
  87.4 12.6 %collective-permute-start.5 = (bf16[512,896]{1,0:T(8,128)(2,1)}, bf16[512,896]{1,0:T(8,128)(2,1)}, u32[]{:S(2)}, u32[]{:S(2)}) collective-permute-start(bf16[512,896]{1,0:T(8,128)(2,1)} %get-tuple-element.35), channel_id=1, source_target_pairs={{0,16},{16,0},{1,17},{17,1},{2,18},{18,2},{3,19},{19,3},{4,20},{20... | collective-permute-start | bytes 2752520 | tf_op jit(solution)/shard_map/ppermute | solution.py:214
  95.0 18.0 %collective-permute-start.8 = (bf16[8,240,128]{2,1,0:T(8,128)(2,1)S(1)}, bf16[8,240,128]{2,1,0:T(8,128)(2,1)S(1)}, u32[]{:S(2)}, u32[]{:S(2)}) collective-permute-start(bf16[8,240,128]{2,1,0:T(8,128)(2,1)S(1)} %all-to-all-done.2.refs_0_.refs_2_), channel_id=1, source_target_pairs={{0,32},{32,0},{1,33},{33,1},{2,34},{34,2},{3,35},{35,3},{4,36},{36... | collective-permute-start | bytes 1474568 | tf_op jit(solution)/shard_map/ppermute | solution.py:214
  103.4 16.2 %all-to-all-start.3 = ((bf16[16,44,128]{2,1,0:T(8,128)(2,1)}), bf16[16,44,128]{2,1,0:T(8,128)(2,1)S(1)}, u32[]{:S(2)}, u32[]{:S(2)}) async-start(bf16[16,44,128]{2,1,0:T(8,128)(2,1)} %get-tuple-element.36), calls=%async_computation.3 | async-start | bytes 393216 | tf_op jit(solution)/shard_map/all_to_all | solution.py:287
  111.0 11.8 %copy-start.1 = (bf16[192,512]{1,0:T(8,128)(2,1)S(1)}, bf16[192,512]{1,0:T(8,128)(2,1)}, u32[]{:S(2)}) copy-start(bf16[192,512]{1,0:T(8,128)(2,1)} %get-tuple-element.38.refs_0_) | copy-start | bytes 589828
  111.0 11.8 %collective-permute-start.7 = (bf16[8,240,128]{2,1,0:T(8,128)(2,1)S(1)}, bf16[8,240,128]{2,1,0:T(8,128)(2,1)S(1)}, u32[]{:S(2)}, u32[]{:S(2)}) collective-permute-start(bf16[8,240,128]{2,1,0:T(8,128)(2,1)S(1)} %all-to-all-done.2.refs_0_.refs_2_), channel_id=1, source_target_pairs={{0,16},{16,0},{1,17},{17,1},{2,18},{18,2},{3,19},{19,3},{4,20},{20... | collective-permute-start | bytes 1474568 | tf_op jit(solution)/shard_map/ppermute | solution.py:214
  113.1 9.7 %collective-permute-start.9 = (bf16[8,240,128]{2,1,0:T(8,128)(2,1)S(1)}, bf16[8,240,128]{2,1,0:T(8,128)(2,1)S(1)}, u32[]{:S(2)}, u32[]{:S(2)}) collective-permute-start(bf16[8,240,128]{2,1,0:T(8,128)(2,1)S(1)} %collective-permute-done.8.refs_4_), channel_id=1, source_target_pairs={{0,16},{16,0},{1,17},{17,1},{2,18},{18,2},{3,19},{19,3},{4,20},{20... | collective-permute-start | bytes 1474568 | tf_op jit(solution)/shard_map/ppermute | solution.py:214
  120.7 11.3 %collective-permute-start.6 = (bf16[11,512]{1,0:T(8,128)(2,1)S(1)}, bf16[11,512]{1,0:T(8,128)(2,1)S(1)}, u32[]{:S(2)}, u32[]{:S(2)}) collective-permute-start(bf16[11,512]{1,0:T(8,128)(2,1)S(1)} %get-tuple-element.37), channel_id=1, source_target_pairs={{0,0},{8,1},{64,2},{72,3},{128,4},{136,5},{192,6},{200,7},{256,8},... | collective-permute-start | bytes 33800 | tf_op jit(solution)/shard_map/ppermute | solution.py:300

commit v5 on v4

--- a/solution.py
+++ b/solution.py
@@ -109,11 +109,22 @@
         out[t] = packed[...]
 
 
+def came_from(base, i):
+    return lax.rem(base - i + 8, 8)
+
+
+def transpose_kernel(gu, out):
+    out[:, :256] = gu[:256, :].T
+    out[:, 256:] = gu[256:, :].T
+
+
 def forward_kernel(
     place, rows, gu0, gu1, down0, down1, out, own_out, oth_out, wide, parts, x_own, x_oth, sems
 ):
-    for t in range(16):
-        wide[t * 88 : (t + 1) * 88, :] = rows[t].astype(F32)
+    for far in range(2):
+        for i in range(8):
+            at = (far * 8 + i) * 88
+            wide[at : at + 88, :] = rows[far * 8 + came_from(place[2], i)].astype(F32)
     blank = jnp.zeros((PADDED - QUARTER, 128), F32)
     for far in range(2):
         for j in range(8):
@@ -158,18 +169,25 @@
         acts[i, 2 * SIZE :, :] = hidden
 
 
-def token_grad_kernel(acts, gu0, gu1, gu2, gu3, out, gate_act, up_act, wide):
+def token_grad_kernel(
+    place, acts, gu1, gu3, gu0_hbm, gu2_hbm, out, gate_act, up_act, wide, gu0, gu2, sems
+):
+    copies = {0: pltpu.make_async_copy(gu0_hbm, gu0, sems.at[0]), 2: pltpu.make_async_copy(gu2_hbm, gu2, sems.at[1])}
+    for copy in copies.values():
+        copy.start()
     get_tiles(acts, 0, gate_act, 0)
     get_tiles(acts, 1, up_act, 0)
-    dims = (((1,), (1,)), ((), ()))
-    for k, gu in enumerate((gu0, gu1, gu2, gu3)):
-        part = lax.dot_general(gate_act[...], gu[:256, :], dims, preferred_element_type=F32)
-        part = part + lax.dot_general(up_act[...], gu[256:, :], dims, preferred_element_type=F32)
+    for k, gu in ((1, gu1), (3, gu3), (0, gu0), (2, gu2)):
+        if k in copies:
+            copies[k].wait()
+        part = jnp.dot(gate_act[...], gu[:, :256], preferred_element_type=F32)
+        part = part + jnp.dot(up_act[...], gu[:, 256:], preferred_element_type=F32)
         for j in range(2):
             wide[k // 2, pl.ds(k % 2 * 2 + j, QUARTER, stride=4), :] = tile(part[:QUARTER], j)
     for far in range(2):
         for i in range(8):
-            out[far * 8 + i] = wide[far, i * 4 * ROWS : (i + 1) * 4 * ROWS, :].astype(BF16)
+            rows = wide[far, i * 4 * ROWS : (i + 1) * 4 * ROWS, :]
+            out[far * 8 + came_from(place[2 + far], i)] = rows.astype(BF16)
 
 
 def token_sum_kernel(place, parts, out, total):
@@ -206,6 +224,17 @@
     return call(copy_kernel, (shape(*x.shape, dtype=x.dtype),), (x,), deps=deps)[0]
 
 
+def after_in_hbm(x, dep):
+    return pl.pallas_call(
+        lambda *refs: None,
+        out_shape=pltpu.HBM(x.shape, x.dtype),
+        in_specs=[HBM, VMEM],
+        out_specs=HBM,
+        input_output_aliases={0: 0},
+        compiler_params=PARAMS,
+    )(in_hbm(x), dep)
+
+
 def in_hbm(x):
     return pltpu.with_memory_space_constraint(x, pltpu.HBM)
 
@@ -224,9 +253,22 @@
 
 
 def per_device(tokens, cotangent, gate_weight, up_weight, down_weight):
-    place = jnp.stack([lax.axis_index("core"), lax.axis_index("xh")]).astype(jnp.int32)
-    there = permutation(lambda z, xh, c, xl, y: (4 * xl + y // 2, y % 2, c, xh ^ y % 2, z))
-    home = [(b, a) for a, b in permutation(lambda z, xh, c, xl, y: (4 * xl + y // 2, xh, c, xh ^ y % 2, z))]
+    z, xh, core = (lax.axis_index(axis) for axis in FSDP)
+    base = z + 4 + z % 4 * 2
+    place = jnp.stack([core, xh, (base + xh) % 8, (base + 1 - xh) % 8]).astype(jnp.int32)
+    def chip(z, xl, y):
+        return 4 * xl + y // 2, (y + 4 - z + 4 * xl + y // 2) % 8
+
+    def forth(z, xh, c, xl, y):
+        to, row = chip(z, xl, y)
+        return to, y % 2, c, xh ^ y % 2, row
+
+    def back(z, xh, c, xl, y):
+        to, row = chip(z, xl, y)
+        return to, xh, c, xh ^ y % 2, row
+
+    there = permutation(forth)
+    home = [(b, a) for a, b in permutation(back)]
 
     packed, ready0 = call(
         pack_kernel,
@@ -269,20 +311,28 @@
     )
     parts = lax.all_to_all(parts, ("z", "xh"), 0, 0, tiled=True)
     x_got = swap("core", after(x_oth, ready))
-    gu2 = swap("xh", after(gu0, ready))
+    t0, _ = call(transpose_kernel, (shape(896, 512),), (gu0,), deps=(ready,))
+    t2 = swap("xh", t0)
 
     acts0, ready = call(activation_kernel, (shape(8, 3 * SIZE, 128),), (parts,))
     acts0 = lax.all_to_all(acts0, "z", 0, 0, tiled=True)
-    gu3 = swap("core", after(gu2, ready, x_got))
+    t1, ready = call(transpose_kernel, (shape(896, 512),), (gu1,), deps=(ready,))
+    t2 = after_in_hbm(t2, ready)
+    t3 = swap("core", t2)
     token_parts, ready = call(
         token_grad_kernel,
         (shape(16, 4 * ROWS, 128),),
-        (acts0, gu0, gu1, gu2, gu3),
+        (place, acts0, t1, t3, in_hbm(t0), in_hbm(t2)),
         [
             pltpu.VMEM((PADDED, 896), BF16),
             pltpu.VMEM((PADDED, 896), BF16),
             pltpu.VMEM((2, 4 * QUARTER, 128), F32),
+            pltpu.VMEM((896, 512), BF16),
+            pltpu.VMEM((896, 512), BF16),
+            pltpu.SemaphoreType.DMA((2,)),
         ],
+        specs=[SMEM] + [VMEM] * 3 + [HBM] * 2,
+        deps=(x_got,),
     )
     token_parts = lax.all_to_all(token_parts, TENSOR, 0, 0, tiled=True)
     acts2 = swap("xh", acts0)

time: 133 us -> 131 us (0.985)
  the two profiles are of different devices: /device:TPU:14 before, /device:TPU:6 now
where the time goes in v5:
time: 131 us; the launch traced here: 130 us
  starting transfers between devices  66.4 us (51%)
  waiting for transfers between devices  45.7 us (35%)
  Pallas kernels  16.5 us (13%)
    ppermute x8, starting transfers between devices, swap(): return lax.ppermute(x, axis, [(0, 1), (1, 0)])  19.9 us
    all_to_all x1, waiting for transfers between devices, per_device(): parts = lax.all_to_all(parts, ('z', 'xh'), 0, 0, tiled=True)  18.1 us
    pallas_call x12, Pallas kernels, call(): pl.pallas_call(body, out_shape=(*out_shape, shape(8, 128, dtype=F32)), in...  16.5 us
    ppermute x1, starting transfers between devices, per_device(): packed = lax.ppermute(packed, ALL, there)  11.8 us
    all_to_all x1, starting transfers between devices, per_device(): token_parts = lax.all_to_all(token_parts, TENSOR, 0, 0, tiled=True)  11.2 us
    all_to_all x1, starting transfers between devices, per_device(): rows = lax.all_to_all(spread, TENSOR, 0, 0, tiled=True)  8.96 us
    all_to_all x1, starting transfers between devices, per_device(): parts = lax.all_to_all(parts, ('z', 'xh'), 0, 0, tiled=True)  8.7 us
    all_to_all x1, waiting for transfers between devices, per_device(): rows = lax.all_to_all(spread, TENSOR, 0, 0, tiled=True)  8.25 us
  transfers between devices with their start and end apart: 14, of which 7 were waited for; matrix products, arithmetic and copies ran while one was open for 0% of the time, Pallas kernels for 9%

profile of v5, /device:TPU:6, one launch (start us, length us, event | category | flops | bytes accessed | tf_op | source)
XLA Modules:
  0.0 129.5 jit_solution(15534019508974205311)
XLA Ops:
  2.1 11.8 %collective-permute-start = (bf16[88,128]{1,0:T(8,128)(2,1)S(1)}, bf16[88,128]{1,0:T(8,128)(2,1)S(1)}, u32[]{:S(2)}, u32[]{:S(2)}) collective-permute-start(bf16[88,128]{1,0:T(8,128)(2,1)S(1)} %get-tuple-element.25), channel_id=1, source_target_pairs={{0,4},{1,45},{2,71},{3,104},{4,130},{5,171},{6,197},{7,238},{8,256... | collective-permute-start | bytes 67592 | tf_op jit(solution)/shard_map/ppermute | solution.py:285
  15.6 1.9 %collective-permute-start.1 = (bf16[512,896]{1,0:T(8,128)(2,1)S(1)}, bf16[512,896]{1,0:T(8,128)(2,1)S(1)}, u32[]{:S(2)}, u32[]{:S(2)}) collective-permute-start(bf16[512,896]{1,0:T(8,128)(2,1)S(1)} %get-tuple-element.28.refs_2_.refs_0_), channel_id=1, source_target_pairs={{0,16},{16,0},{1,17},{17,1},{2,18},{18,2},{3,19},{19,3},{4,20},{20... | collective-permute-start | bytes 2752520 | tf_op jit(solution)/shard_map/ppermute | solution.py:243
  18.3 9.0 %all-to-all-start = ((bf16[16,88,128]{2,1,0:T(8,128)(2,1)}), bf16[16,88,128]{2,1,0:T(8,128)(2,1)S(1)}, u32[]{:S(2)}, u32[]{:S(2)}) async-start(bf16[16,88,128]{2,1,0:T(8,128)(2,1)} %get-tuple-element.26), calls=%async_computation | async-start | bytes 720896 | tf_op jit(solution)/shard_map/all_to_all | solution.py:287
  27.3 1.9 %collective-permute-start.2 = (bf16[896,256]{1,0:T(8,128)(2,1)S(1)}, bf16[896,256]{1,0:T(8,128)(2,1)S(1)}, u32[]{:S(2)}, u32[]{:S(2)}) collective-permute-start(bf16[896,256]{1,0:T(8,128)(2,1)S(1)} %copy-done), channel_id=1, source_target_pairs={{0,16},{16,0},{1,17},{17,1},{2,18},{18,2},{3,19},{19,3},{4,20},{20... | collective-permute-start | bytes 1376264 | tf_op jit(solution)/shard_map/ppermute | solution.py:243
  29.2 1.8 %collective-permute-done.2.refs_5_ = bf16[896,256]{1,0:T(8,128)(2,1)S(1)} collective-permute-done((bf16[896,256]{1,0:T(8,128)(2,1)S(1)}, bf16[896,256]{1,0:T(8,128)(2,1)S(1)}, u32[]{:S(2)}, u32[]{:S(2)}) %collective-permute-start.2) | collective-permute-done | bytes 458784 | tf_op jit(solution)/shard_map/ppermute | solution.py:243
  31.0 8.3 %all-to-all-done.refs_1_ = bf16[16,88,128]{2,1,0:T(8,128)(2,1)S(1)} async-done(((bf16[16,88,128]{2,1,0:T(8,128)(2,1)}), bf16[16,88,128]{2,1,0:T(8,128)(2,1)S(1)}, u32[]{:S(2)}, u32[]{:S(2)}) %all-to-all-start) | async-done | bytes 360480 | tf_op jit(solution)/shard_map/all_to_all | solution.py:287
  39.3 2.3 %shard_map.87 = (bf16[16,240,128]{2,1,0:T(8,128)(2,1)}, bf16[192,512]{1,0:T(8,128)(2,1)}, bf16[192,512]{1,0:T(8,128)(2,1)}, f32[8,128]{1,0:T(8,128)S(1)}) custom-call(s32[4]{0:T(128)S(1)} %pad_add_fusion.refs_0_, bf16[16,88,128]{2,1,0:T(8,128)(2,1)S(1)} %all-to-all-done.refs_1_, bf16[512,896]{1,0:T(8,128)(2,1)S(1)} %get-tuple-element.28.refs_2_.refs_0_, ...), custom_call_target="tpu_custom_call" | custom-call | bytes 4489232 | tf_op jit(solution)/shard_map/pallas_call | solution.py:35
  41.6 8.7 %all-to-all-start.1 = ((bf16[16,240,128]{2,1,0:T(8,128)(2,1)}), bf16[16,240,128]{2,1,0:T(8,128)(2,1)S(1)}, u32[]{:S(2)}, u32[]{:S(2)}) async-start(bf16[16,240,128]{2,1,0:T(8,128)(2,1)} %get-tuple-element.29), calls=%async_computation.1 | async-start | bytes 1966080 | tf_op jit(solution)/shard_map/all_to_all | solution.py:312
  51.6 2.0 %collective-permute-start.3 = (bf16[896,512]{1,0:T(8,128)(2,1)}, bf16[896,512]{1,0:T(8,128)(2,1)}, u32[]{:S(2)}, u32[]{:S(2)}) collective-permute-start(bf16[896,512]{1,0:T(8,128)(2,1)} %get-tuple-element.34.refs_4_), channel_id=1, source_target_pairs={{0,32},{32,0},{1,33},{33,1},{2,34},{34,2},{3,35},{35,3},{4,36},{36... | collective-permute-start | bytes 2752520 | tf_op jit(solution)/shard_map/ppermute | solution.py:243
  53.6 18.1 %all-to-all-done.1.refs_0_ = bf16[16,240,128]{2,1,0:T(8,128)(2,1)S(1)} async-done(((bf16[16,240,128]{2,1,0:T(8,128)(2,1)}), bf16[16,240,128]{2,1,0:T(8,128)(2,1)S(1)}, u32[]{:S(2)}, u32[]{:S(2)}) %all-to-all-start.1) | async-done | bytes 983072 | tf_op jit(solution)/shard_map/all_to_all | solution.py:312
  72.6 3.6 %all-to-all-start.2 = ((bf16[8,240,128]{2,1,0:T(8,128)(2,1)}), bf16[8,240,128]{2,1,0:T(8,128)(2,1)S(1)}, u32[]{:S(2)}, u32[]{:S(2)}) async-start(bf16[8,240,128]{2,1,0:T(8,128)(2,1)} %get-tuple-element.30), calls=%async_computation.2 | async-start | bytes 983040 | tf_op jit(solution)/shard_map/all_to_all | solution.py:318
  76.5 5.6 %collective-permute-done.3.refs_0_ = bf16[896,512]{1,0:T(8,128)(2,1)} collective-permute-done((bf16[896,512]{1,0:T(8,128)(2,1)}, bf16[896,512]{1,0:T(8,128)(2,1)}, u32[]{:S(2)}, u32[]{:S(2)}) %collective-permute-start.3) | collective-permute-done | bytes 917536 | tf_op jit(solution)/shard_map/ppermute | solution.py:243
  82.1 2.0 %collective-permute-start.4 = (bf16[896,512]{1,0:T(8,128)(2,1)}, bf16[896,512]{1,0:T(8,128)(2,1)S(1)}, u32[]{:S(2)}, u32[]{:S(2)}) collective-permute-start(bf16[896,512]{1,0:T(8,128)(2,1)} %shard_map.91.refs_5_), channel_id=1, source_target_pairs={{0,16},{16,0},{1,17},{17,1},{2,18},{18,2},{3,19},{19,3},{4,20},{20... | collective-permute-start | bytes 2752520 | tf_op jit(solution)/shard_map/ppermute | solution.py:243
  84.7 2.4 %collective-permute-start.5 = (bf16[192,512]{1,0:T(8,128)(2,1)S(1)}, bf16[192,512]{1,0:T(8,128)(2,1)S(1)}, u32[]{:S(2)}, u32[]{:S(2)}) collective-permute-start(bf16[192,512]{1,0:T(8,128)(2,1)S(1)} %get-tuple-element.37), channel_id=1, source_target_pairs={{0,16},{16,0},{1,17},{17,1},{2,18},{18,2},{3,19},{19,3},{4,20},{20... | collective-permute-start | bytes 589832 | tf_op jit(solution)/shard_map/ppermute | solution.py:243
  87.1 2.9 %all-to-all-done.2.refs_1_.refs_2_ = bf16[8,240,128]{2,1,0:T(8,128)(2,1)S(1)} async-done(((bf16[8,240,128]{2,1,0:T(8,128)(2,1)}), bf16[8,240,128]{2,1,0:T(8,128)(2,1)S(1)}, u32[]{:S(2)}, u32[]{:S(2)}) %all-to-all-start.2) | async-done | bytes 491552 | tf_op jit(solution)/shard_map/all_to_all | solution.py:318
  90.0 5.1 %collective-permute-start.8 = (bf16[8,240,128]{2,1,0:T(8,128)(2,1)S(1)}, bf16[8,240,128]{2,1,0:T(8,128)(2,1)S(1)}, u32[]{:S(2)}, u32[]{:S(2)}) collective-permute-start(bf16[8,240,128]{2,1,0:T(8,128)(2,1)S(1)} %all-to-all-done.2.refs_1_.refs_2_), channel_id=1, source_target_pairs={{0,32},{32,0},{1,33},{33,1},{2,34},{34,2},{3,35},{35,3},{4,36},{36... | collective-permute-start | bytes 1474568 | tf_op jit(solution)/shard_map/ppermute | solution.py:243
  95.2 3.5 %shard_map.93 = (bf16[16,44,128]{2,1,0:T(8,128)(2,1)}, f32[8,128]{1,0:T(8,128)}) custom-call(s32[4]{0:T(128)S(1)} %pad_add_fusion.refs_0_, bf16[8,240,128]{2,1,0:T(8,128)(2,1)S(1)} %all-to-all-done.2.refs_1_.refs_2_, bf16[896,512]{1,0:T(8,128)(2,1)S(1)} %get-tuple-element.32.refs_2_, bf16[896,512]{1,0:T(8,128)(2,1)S(1)} %collective-permute-done.4.refs_3_, ...), custom_call_target="tpu_custom_call" | custom-call | bytes 4341776 | tf_op jit(solution)/shard_map/pallas_call | solution.py:35
  98.7 11.2 %all-to-all-start.3 = ((bf16[16,44,128]{2,1,0:T(8,128)(2,1)}), bf16[16,44,128]{2,1,0:T(8,128)(2,1)S(1)}, u32[]{:S(2)}, u32[]{:S(2)}) async-start(bf16[16,44,128]{2,1,0:T(8,128)(2,1)} %get-tuple-element.38), calls=%async_computation.3 | async-start | bytes 393216 | tf_op jit(solution)/shard_map/all_to_all | solution.py:337
  109.9 2.1 %collective-permute-start.7 = (bf16[8,240,128]{2,1,0:T(8,128)(2,1)S(1)}, bf16[8,240,128]{2,1,0:T(8,128)(2,1)S(1)}, u32[]{:S(2)}, u32[]{:S(2)}) collective-permute-start(bf16[8,240,128]{2,1,0:T(8,128)(2,1)S(1)} %all-to-all-done.2.refs_1_.refs_2_), channel_id=1, source_target_pairs={{0,16},{16,0},{1,17},{17,1},{2,18},{18,2},{3,19},{19,3},{4,20},{20... | collective-permute-start | bytes 1474568 | tf_op jit(solution)/shard_map/ppermute | solution.py:243
  112.0 2.4 %collective-permute-start.9 = (bf16[8,240,128]{2,1,0:T(8,128)(2,1)S(1)}, bf16[8,240,128]{2,1,0:T(8,128)(2,1)S(1)}, u32[]{:S(2)}, u32[]{:S(2)}) collective-permute-start(bf16[8,240,128]{2,1,0:T(8,128)(2,1)S(1)} %collective-permute-done.8.refs_4_), channel_id=1, source_target_pairs={{0,16},{16,0},{1,17},{17,1},{2,18},{18,2},{3,19},{19,3},{4,20},{20... | collective-permute-start | bytes 1474568 | tf_op jit(solution)/shard_map/ppermute | solution.py:243
  114.4 3.8 %all-to-all-done.3.refs_1_ = bf16[16,44,128]{2,1,0:T(8,128)(2,1)S(1)} async-done(((bf16[16,44,128]{2,1,0:T(8,128)(2,1)}), bf16[16,44,128]{2,1,0:T(8,128)(2,1)S(1)}, u32[]{:S(2)}, u32[]{:S(2)}) %all-to-all-start.3) | async-done | bytes 180256 | tf_op jit(solution)/shard_map/all_to_all | solution.py:337
  119.4 2.3 %collective-permute-start.6 = (bf16[11,512]{1,0:T(8,128)(2,1)S(1)}, bf16[11,512]{1,0:T(8,128)(2,1)S(1)}, u32[]{:S(2)}, u32[]{:S(2)}) collective-permute-start(bf16[11,512]{1,0:T(8,128)(2,1)S(1)} %get-tuple-element.39), channel_id=1, source_target_pairs={{4,0},{13,1},{71,2},{72,3},{130,4},{139,5},{197,6},{206,7},{256,8}... | collective-permute-start | bytes 33800 | tf_op jit(solution)/shard_map/ppermute | solution.py:350
  121.7 1.9 %shard_map.95 = (bf16[256,896]{1,0:T(8,128)(2,1)}, bf16[256,896]{1,0:T(8,128)(2,1)}, bf16[896,256]{1,0:T(8,128)(2,1)}, f32[8,128]{1,0:T(8,128)S(1)}) custom-call(bf16[192,512]{1,0:T(8,128)(2,1)S(1)} %copy-done.1, bf16[192,512]{1,0:T(8,128)(2,1)S(1)} %collective-permute-done.5.refs_6_.refs_1_, bf16[8,240,128]{2,1,0:T(8,128)(2,1)S(1)} %all-to-all-done.2.refs_1_.refs_2_, ...), custom_call_target="tpu_custom_call" | custom-call | bytes 3735552 | tf_op jit(solution)/shard_map/pallas_call | solution.py:35
  123.6 5.3 %collective-permute-done.6.refs_0_ = bf16[11,512]{1,0:T(8,128)(2,1)S(1)} collective-permute-done((bf16[11,512]{1,0:T(8,128)(2,1)S(1)}, bf16[11,512]{1,0:T(8,128)(2,1)S(1)}, u32[]{:S(2)}, u32[]{:S(2)}) %collective-permute-start.6) | collective-permute-done | bytes 11296 | tf_op jit(solution)/shard_map/ppermute | solution.py:350
  (24 shorter events, 8.8 us)
Async XLA Ops:
  2.1 15.5 %collective-permute-start = (bf16[88,128]{1,0:T(8,128)(2,1)S(1)}, bf16[88,128]{1,0:T(8,128)(2,1)S(1)}, u32[]{:S(2)}, u32[]{:S(2)}) collective-permute-start(bf16[88,128]{1,0:T(8,128)(2,1)S(1)} %get-tuple-element.25), channel_id=1, source_target_pairs={{0,4},{1,45},{2,71},{3,104},{4,130},{5,171},{6,197},{7,238},{8,256... | collective-permute-start | bytes 67592 | tf_op jit(solution)/shard_map/ppermute | solution.py:285
  15.6 23.7 %collective-permute-start.1 = (bf16[512,896]{1,0:T(8,128)(2,1)S(1)}, bf16[512,896]{1,0:T(8,128)(2,1)S(1)}, u32[]{:S(2)}, u32[]{:S(2)}) collective-permute-start(bf16[512,896]{1,0:T(8,128)(2,1)S(1)} %get-tuple-element.28.refs_2_.refs_0_), channel_id=1, source_target_pairs={{0,16},{16,0},{1,17},{17,1},{2,18},{18,2},{3,19},{19,3},{4,20},{20... | collective-permute-start | bytes 2752520 | tf_op jit(solution)/shard_map/ppermute | solution.py:243
  18.3 9.0 %copy-start = (bf16[896,256]{1,0:T(8,128)(2,1)S(1)}, bf16[896,256]{1,0:T(8,128)(2,1)}, u32[]{:S(2)}) copy-start(bf16[896,256]{1,0:T(8,128)(2,1)} %refs_4_.1) | copy-start | bytes 1376260
  18.3 20.9 %all-to-all-start = ((bf16[16,88,128]{2,1,0:T(8,128)(2,1)}), bf16[16,88,128]{2,1,0:T(8,128)(2,1)S(1)}, u32[]{:S(2)}, u32[]{:S(2)}) async-start(bf16[16,88,128]{2,1,0:T(8,128)(2,1)} %get-tuple-element.26), calls=%async_computation | async-start | bytes 720896 | tf_op jit(solution)/shard_map/all_to_all | solution.py:287
  27.3 3.7 %collective-permute-start.2 = (bf16[896,256]{1,0:T(8,128)(2,1)S(1)}, bf16[896,256]{1,0:T(8,128)(2,1)S(1)}, u32[]{:S(2)}, u32[]{:S(2)}) collective-permute-start(bf16[896,256]{1,0:T(8,128)(2,1)S(1)} %copy-done), channel_id=1, source_target_pairs={{0,16},{16,0},{1,17},{17,1},{2,18},{18,2},{3,19},{19,3},{4,20},{20... | collective-permute-start | bytes 1376264 | tf_op jit(solution)/shard_map/ppermute | solution.py:243
  41.6 30.0 %all-to-all-start.1 = ((bf16[16,240,128]{2,1,0:T(8,128)(2,1)}), bf16[16,240,128]{2,1,0:T(8,128)(2,1)S(1)}, u32[]{:S(2)}, u32[]{:S(2)}) async-start(bf16[16,240,128]{2,1,0:T(8,128)(2,1)} %get-tuple-element.29), calls=%async_computation.1 | async-start | bytes 1966080 | tf_op jit(solution)/shard_map/all_to_all | solution.py:312
  51.6 30.5 %collective-permute-start.3 = (bf16[896,512]{1,0:T(8,128)(2,1)}, bf16[896,512]{1,0:T(8,128)(2,1)}, u32[]{:S(2)}, u32[]{:S(2)}) collective-permute-start(bf16[896,512]{1,0:T(8,128)(2,1)} %get-tuple-element.34.refs_4_), channel_id=1, source_target_pairs={{0,32},{32,0},{1,33},{33,1},{2,34},{34,2},{3,35},{35,3},{4,36},{36... | collective-permute-start | bytes 2752520 | tf_op jit(solution)/shard_map/ppermute | solution.py:243
  72.6 17.4 %all-to-all-start.2 = ((bf16[8,240,128]{2,1,0:T(8,128)(2,1)}), bf16[8,240,128]{2,1,0:T(8,128)(2,1)S(1)}, u32[]{:S(2)}, u32[]{:S(2)}) async-start(bf16[8,240,128]{2,1,0:T(8,128)(2,1)} %get-tuple-element.30), calls=%async_computation.2 | async-start | bytes 983040 | tf_op jit(solution)/shard_map/all_to_all | solution.py:318
  82.1 2.1 %copy-start.2 = (bf16[192,512]{1,0:T(8,128)(2,1)S(1)}, bf16[192,512]{1,0:T(8,128)(2,1)}, u32[]{:S(2)}) copy-start(bf16[192,512]{1,0:T(8,128)(2,1)} %get-tuple-element.36.refs_0_) | copy-start | bytes 589828
  82.1 13.1 %collective-permute-start.4 = (bf16[896,512]{1,0:T(8,128)(2,1)}, bf16[896,512]{1,0:T(8,128)(2,1)S(1)}, u32[]{:S(2)}, u32[]{:S(2)}) collective-permute-start(bf16[896,512]{1,0:T(8,128)(2,1)} %shard_map.91.refs_5_), channel_id=1, source_target_pairs={{0,16},{16,0},{1,17},{17,1},{2,18},{18,2},{3,19},{19,3},{4,20},{20... | collective-permute-start | bytes 2752520 | tf_op jit(solution)/shard_map/ppermute | solution.py:243
  84.7 10.4 %collective-permute-start.5 = (bf16[192,512]{1,0:T(8,128)(2,1)S(1)}, bf16[192,512]{1,0:T(8,128)(2,1)S(1)}, u32[]{:S(2)}, u32[]{:S(2)}) collective-permute-start(bf16[192,512]{1,0:T(8,128)(2,1)S(1)} %get-tuple-element.37), channel_id=1, source_target_pairs={{0,16},{16,0},{1,17},{17,1},{2,18},{18,2},{3,19},{19,3},{4,20},{20... | collective-permute-start | bytes 589832 | tf_op jit(solution)/shard_map/ppermute | solution.py:243
  90.0 22.0 %collective-permute-start.8 = (bf16[8,240,128]{2,1,0:T(8,128)(2,1)S(1)}, bf16[8,240,128]{2,1,0:T(8,128)(2,1)S(1)}, u32[]{:S(2)}, u32[]{:S(2)}) collective-permute-start(bf16[8,240,128]{2,1,0:T(8,128)(2,1)S(1)} %all-to-all-done.2.refs_1_.refs_2_), channel_id=1, source_target_pairs={{0,32},{32,0},{1,33},{33,1},{2,34},{34,2},{3,35},{35,3},{4,36},{36... | collective-permute-start | bytes 1474568 | tf_op jit(solution)/shard_map/ppermute | solution.py:243
  98.7 19.5 %all-to-all-start.3 = ((bf16[16,44,128]{2,1,0:T(8,128)(2,1)}), bf16[16,44,128]{2,1,0:T(8,128)(2,1)S(1)}, u32[]{:S(2)}, u32[]{:S(2)}) async-start(bf16[16,44,128]{2,1,0:T(8,128)(2,1)} %get-tuple-element.38), calls=%async_computation.3 | async-start | bytes 393216 | tf_op jit(solution)/shard_map/all_to_all | solution.py:337
  109.9 11.8 %copy-start.1 = (bf16[192,512]{1,0:T(8,128)(2,1)S(1)}, bf16[192,512]{1,0:T(8,128)(2,1)}, u32[]{:S(2)}) copy-start(bf16[192,512]{1,0:T(8,128)(2,1)} %get-tuple-element.40.refs_0_) | copy-start | bytes 589828
  109.9 11.8 %collective-permute-start.7 = (bf16[8,240,128]{2,1,0:T(8,128)(2,1)S(1)}, bf16[8,240,128]{2,1,0:T(8,128)(2,1)S(1)}, u32[]{:S(2)}, u32[]{:S(2)}) collective-permute-start(bf16[8,240,128]{2,1,0:T(8,128)(2,1)S(1)} %all-to-all-done.2.refs_1_.refs_2_), channel_id=1, source_target_pairs={{0,16},{16,0},{1,17},{17,1},{2,18},{18,2},{3,19},{19,3},{4,20},{20... | collective-permute-start | bytes 1474568 | tf_op jit(solution)/shard_map/ppermute | solution.py:243
  112.0 9.7 %collective-permute-start.9 = (bf16[8,240,128]{2,1,0:T(8,128)(2,1)S(1)}, bf16[8,240,128]{2,1,0:T(8,128)(2,1)S(1)}, u32[]{:S(2)}, u32[]{:S(2)}) collective-permute-start(bf16[8,240,128]{2,1,0:T(8,128)(2,1)S(1)} %collective-permute-done.8.refs_4_), channel_id=1, source_target_pairs={{0,16},{16,0},{1,17},{17,1},{2,18},{18,2},{3,19},{19,3},{4,20},{20... | collective-permute-start | bytes 1474568 | tf_op jit(solution)/shard_map/ppermute | solution.py:243
  119.4 9.5 %collective-permute-start.6 = (bf16[11,512]{1,0:T(8,128)(2,1)S(1)}, bf16[11,512]{1,0:T(8,128)(2,1)S(1)}, u32[]{:S(2)}, u32[]{:S(2)}) collective-permute-start(bf16[11,512]{1,0:T(8,128)(2,1)S(1)} %get-tuple-element.39), channel_id=1, source_target_pairs={{4,0},{13,1},{71,2},{72,3},{130,4},{139,5},{197,6},{206,7},{256,8}... | collective-permute-start | bytes 33800 | tf_op jit(solution)/shard_map/ppermute | solution.py:350

commit v6 on v5

--- a/solution.py
+++ b/solution.py
@@ -124,7 +124,7 @@
     for far in range(2):
         for i in range(8):
             at = (far * 8 + i) * 88
-            wide[at : at + 88, :] = rows[far * 8 + came_from(place[2], i)].astype(F32)
+            wide[at : at + 88, :] = rows[lax.rem(far + place[4], 2) * 8 + came_from(place[2], i)].astype(F32)
     blank = jnp.zeros((PADDED - QUARTER, 128), F32)
     for far in range(2):
         for j in range(8):
@@ -169,25 +169,35 @@
         acts[i, 2 * SIZE :, :] = hidden
 
 
-def token_grad_kernel(
-    place, acts, gu1, gu3, gu0_hbm, gu2_hbm, out, gate_act, up_act, wide, gu0, gu2, sems
-):
-    copies = {0: pltpu.make_async_copy(gu0_hbm, gu0, sems.at[0]), 2: pltpu.make_async_copy(gu2_hbm, gu2, sems.at[1])}
-    for copy in copies.values():
+HALVES = (pl.ds(0, 448), pl.ds(448, 448))
+
+
+def token_grad_kernel(place, acts, gu0, gu1, t2_hbm, t3_hbm, out, gate_act, up_act, wide, ts, sems):
+    copies = [
+        [pltpu.make_async_copy(t_hbm.at[rows], ts.at[k, rows], sems.at[k, i]) for i, rows in enumerate(parts)]
+        for k, t_hbm, parts in ((0, t2_hbm, HALVES), (1, t3_hbm, HALVES))
+    ]
+    for copy in copies[0] + copies[1]:
         copy.start()
     get_tiles(acts, 0, gate_act, 0)
     get_tiles(acts, 1, up_act, 0)
-    for k, gu in ((1, gu1), (3, gu3), (0, gu0), (2, gu2)):
-        if k in copies:
-            copies[k].wait()
-        part = jnp.dot(gate_act[...], gu[:, :256], preferred_element_type=F32)
-        part = part + jnp.dot(up_act[...], gu[:, 256:], preferred_element_type=F32)
+    contract_cols = (((1,), (1,)), ((), ()))
+    for k in range(4):
+        if k < 2:
+            gu = (gu0, gu1)[k]
+            part = lax.dot_general(gate_act[...], gu[:256, :], contract_cols, preferred_element_type=F32)
+            part = part + lax.dot_general(up_act[...], gu[256:, :], contract_cols, preferred_element_type=F32)
+        else:
+            for copy in copies[k - 2]:
+                copy.wait()
+            part = jnp.dot(gate_act[...], ts[k - 2, :, :256], preferred_element_type=F32)
+            part = part + jnp.dot(up_act[...], ts[k - 2, :, 256:], preferred_element_type=F32)
         for j in range(2):
             wide[k // 2, pl.ds(k % 2 * 2 + j, QUARTER, stride=4), :] = tile(part[:QUARTER], j)
     for far in range(2):
         for i in range(8):
             rows = wide[far, i * 4 * ROWS : (i + 1) * 4 * ROWS, :]
-            out[far * 8 + came_from(place[2 + far], i)] = rows.astype(BF16)
+            out[lax.rem(far + place[4], 2) * 8 + came_from(place[2 + far], i)] = rows.astype(BF16)
 
 
 def token_sum_kernel(place, parts, out, total):
@@ -255,17 +265,17 @@
 def per_device(tokens, cotangent, gate_weight, up_weight, down_weight):
     z, xh, core = (lax.axis_index(axis) for axis in FSDP)
     base = z + 4 + z % 4 * 2
-    place = jnp.stack([core, xh, (base + xh) % 8, (base + 1 - xh) % 8]).astype(jnp.int32)
+    place = jnp.stack([core, xh, (base + xh) % 8, (base + 1 - xh) % 8, z // 4]).astype(jnp.int32)
     def chip(z, xl, y):
         return 4 * xl + y // 2, (y + 4 - z + 4 * xl + y // 2) % 8
 
     def forth(z, xh, c, xl, y):
         to, row = chip(z, xl, y)
-        return to, y % 2, c, xh ^ y % 2, row
+        return to, y % 2, c, xh ^ y % 2 ^ xl, row
 
     def back(z, xh, c, xl, y):
         to, row = chip(z, xl, y)
-        return to, xh, c, xh ^ y % 2, row
+        return to, xh, c, xh ^ y % 2 ^ xl, row
 
     there = permutation(forth)
     home = [(b, a) for a, b in permutation(back)]
@@ -316,20 +326,18 @@
 
     acts0, ready = call(activation_kernel, (shape(8, 3 * SIZE, 128),), (parts,))
     acts0 = lax.all_to_all(acts0, "z", 0, 0, tiled=True)
-    t1, ready = call(transpose_kernel, (shape(896, 512),), (gu1,), deps=(ready,))
     t2 = after_in_hbm(t2, ready)
     t3 = swap("core", t2)
     token_parts, ready = call(
         token_grad_kernel,
         (shape(16, 4 * ROWS, 128),),
-        (place, acts0, t1, t3, in_hbm(t0), in_hbm(t2)),
+        (place, acts0, gu0, gu1, in_hbm(t2), in_hbm(t3)),
         [
             pltpu.VMEM((PADDED, 896), BF16),
             pltpu.VMEM((PADDED, 896), BF16),
             pltpu.VMEM((2, 4 * QUARTER, 128), F32),
-            pltpu.VMEM((896, 512), BF16),
-            pltpu.VMEM((896, 512), BF16),
-            pltpu.SemaphoreType.DMA((2,)),
+            pltpu.VMEM((2, 896, 512), BF16),
+            pltpu.SemaphoreType.DMA((2, 2)),
         ],
         specs=[SMEM] + [VMEM] * 3 + [HBM] * 2,
         deps=(x_got,),

time: 131 us -> 129 us (0.985)
  starting transfers between devices: 66.4 us -> 63.2 us
  waiting for transfers between devices: 45.7 us -> 47.9 us
    all_to_all x1, starting transfers between devices: 11.2 us -> 9.77 us  [per_device(): token_parts = lax.all_to_all(token_parts, TENSOR, 0, 0, tiled=True)]
    pallas_call x12 -> x11, Pallas kernels: 16.5 us -> 16.3 us  [call(): pl.pallas_call(body, out_shape=(*out_shape, shape(8, 128, dtype=F32)), in...]
where the time goes in v6:
time: 129 us; the launch traced here: 128 us
  starting transfers between devices  63.2 us (49%)
  waiting for transfers between devices  47.9 us (37%)
  Pallas kernels  16.3 us (13%)
    ppermute x8, starting transfers between devices, swap(): return lax.ppermute(x, axis, [(0, 1), (1, 0)])  20.1 us
    all_to_all x1, waiting for transfers between devices, per_device(): parts = lax.all_to_all(parts, ('z', 'xh'), 0, 0, tiled=True)  18.4 us
    pallas_call x11, Pallas kernels, call(): pl.pallas_call(body, out_shape=(*out_shape, shape(8, 128, dtype=F32)), in...  16.3 us
    ppermute x1, starting transfers between devices, per_device(): packed = lax.ppermute(packed, ALL, there)  10.8 us
    all_to_all x1, starting transfers between devices, per_device(): token_parts = lax.all_to_all(token_parts, TENSOR, 0, 0, tiled=True)  9.77 us
    all_to_all x1, starting transfers between devices, per_device(): rows = lax.all_to_all(spread, TENSOR, 0, 0, tiled=True)  8.96 us
    all_to_all x1, waiting for transfers between devices, per_device(): rows = lax.all_to_all(spread, TENSOR, 0, 0, tiled=True)  8.25 us
    ppermute x8, waiting for transfers between devices, swap(): return lax.ppermute(x, axis, [(0, 1), (1, 0)])  7.67 us
  transfers between devices with their start and end apart: 14, of which 7 were waited for; matrix products, arithmetic and copies ran while one was open for 0% of the time, Pallas kernels for 9%

profile of v6, /device:TPU:6, one launch (start us, length us, event | category | flops | bytes accessed | tf_op | source)
XLA Modules:
  0.0 128.5 jit_solution(15116356007056122120)
XLA Ops:
  2.1 10.8 %collective-permute-start = (bf16[88,128]{1,0:T(8,128)(2,1)S(1)}, bf16[88,128]{1,0:T(8,128)(2,1)S(1)}, u32[]{:S(2)}, u32[]{:S(2)}) collective-permute-start(bf16[88,128]{1,0:T(8,128)(2,1)S(1)} %get-tuple-element.23), channel_id=1, source_target_pairs={{0,4},{1,45},{2,71},{3,104},{4,130},{5,171},{6,197},{7,238},{8,264... | collective-permute-start | bytes 67592 | tf_op jit(solution)/shard_map/ppermute | solution.py:295
  14.7 1.9 %collective-permute-start.1 = (bf16[512,896]{1,0:T(8,128)(2,1)S(1)}, bf16[512,896]{1,0:T(8,128)(2,1)S(1)}, u32[]{:S(2)}, u32[]{:S(2)}) collective-permute-start(bf16[512,896]{1,0:T(8,128)(2,1)S(1)} %get-tuple-element.26.refs_2_.refs_0_), channel_id=1, source_target_pairs={{0,16},{16,0},{1,17},{17,1},{2,18},{18,2},{3,19},{19,3},{4,20},{20... | collective-permute-start | bytes 2752520 | tf_op jit(solution)/shard_map/ppermute | solution.py:253
  17.4 9.0 %all-to-all-start = ((bf16[16,88,128]{2,1,0:T(8,128)(2,1)}), bf16[16,88,128]{2,1,0:T(8,128)(2,1)S(1)}, u32[]{:S(2)}, u32[]{:S(2)}) async-start(bf16[16,88,128]{2,1,0:T(8,128)(2,1)} %get-tuple-element.24), calls=%async_computation | async-start | bytes 720896 | tf_op jit(solution)/shard_map/all_to_all | solution.py:297
  26.4 1.9 %collective-permute-start.2 = (bf16[896,256]{1,0:T(8,128)(2,1)S(1)}, bf16[896,256]{1,0:T(8,128)(2,1)S(1)}, u32[]{:S(2)}, u32[]{:S(2)}) collective-permute-start(bf16[896,256]{1,0:T(8,128)(2,1)S(1)} %copy-done), channel_id=1, source_target_pairs={{0,16},{16,0},{1,17},{17,1},{2,18},{18,2},{3,19},{19,3},{4,20},{20... | collective-permute-start | bytes 1376264 | tf_op jit(solution)/shard_map/ppermute | solution.py:253
  28.3 1.8 %collective-permute-done.2.refs_5_ = bf16[896,256]{1,0:T(8,128)(2,1)S(1)} collective-permute-done((bf16[896,256]{1,0:T(8,128)(2,1)S(1)}, bf16[896,256]{1,0:T(8,128)(2,1)S(1)}, u32[]{:S(2)}, u32[]{:S(2)}) %collective-permute-start.2) | collective-permute-done | bytes 458784 | tf_op jit(solution)/shard_map/ppermute | solution.py:253
  30.1 8.3 %all-to-all-done.refs_1_ = bf16[16,88,128]{2,1,0:T(8,128)(2,1)S(1)} async-done(((bf16[16,88,128]{2,1,0:T(8,128)(2,1)}), bf16[16,88,128]{2,1,0:T(8,128)(2,1)S(1)}, u32[]{:S(2)}, u32[]{:S(2)}) %all-to-all-start) | async-done | bytes 360480 | tf_op jit(solution)/shard_map/all_to_all | solution.py:297
  38.4 2.3 %shard_map.87 = (bf16[16,240,128]{2,1,0:T(8,128)(2,1)}, bf16[192,512]{1,0:T(8,128)(2,1)}, bf16[192,512]{1,0:T(8,128)(2,1)}, f32[8,128]{1,0:T(8,128)S(1)}) custom-call(s32[5]{0:T(128)S(1)} %stack.23.refs_0_, bf16[16,88,128]{2,1,0:T(8,128)(2,1)S(1)} %all-to-all-done.refs_1_, bf16[512,896]{1,0:T(8,128)(2,1)S(1)} %get-tuple-element.26.refs_2_.refs_0_, ...), custom_call_target="tpu_custom_call" | custom-call | bytes 4489236 | tf_op jit(solution)/shard_map/pallas_call | solution.py:35
  40.7 7.5 %all-to-all-start.1 = ((bf16[16,240,128]{2,1,0:T(8,128)(2,1)}), bf16[16,240,128]{2,1,0:T(8,128)(2,1)S(1)}, u32[]{:S(2)}, u32[]{:S(2)}) async-start(bf16[16,240,128]{2,1,0:T(8,128)(2,1)} %get-tuple-element.27), calls=%async_computation.1 | async-start | bytes 1966080 | tf_op jit(solution)/shard_map/all_to_all | solution.py:322
  49.4 2.0 %collective-permute-start.3 = (bf16[896,512]{1,0:T(8,128)(2,1)}, bf16[896,512]{1,0:T(8,128)(2,1)}, u32[]{:S(2)}, u32[]{:S(2)}) collective-permute-start(bf16[896,512]{1,0:T(8,128)(2,1)} %get-tuple-element.30), channel_id=1, source_target_pairs={{0,32},{32,0},{1,33},{33,1},{2,34},{34,2},{3,35},{35,3},{4,36},{36... | collective-permute-start | bytes 2752520 | tf_op jit(solution)/shard_map/ppermute | solution.py:253
  51.4 18.4 %all-to-all-done.1.refs_0_ = bf16[16,240,128]{2,1,0:T(8,128)(2,1)S(1)} async-done(((bf16[16,240,128]{2,1,0:T(8,128)(2,1)}), bf16[16,240,128]{2,1,0:T(8,128)(2,1)S(1)}, u32[]{:S(2)}, u32[]{:S(2)}) %all-to-all-start.1) | async-done | bytes 983072 | tf_op jit(solution)/shard_map/all_to_all | solution.py:322
  70.8 3.7 %all-to-all-start.2 = ((bf16[8,240,128]{2,1,0:T(8,128)(2,1)}), bf16[8,240,128]{2,1,0:T(8,128)(2,1)S(1)}, u32[]{:S(2)}, u32[]{:S(2)}) async-start(bf16[8,240,128]{2,1,0:T(8,128)(2,1)} %get-tuple-element.28), calls=%async_computation.2 | async-start | bytes 983040 | tf_op jit(solution)/shard_map/all_to_all | solution.py:328
  74.5 5.9 %collective-permute-done.3.refs_0_ = bf16[896,512]{1,0:T(8,128)(2,1)} collective-permute-done((bf16[896,512]{1,0:T(8,128)(2,1)}, bf16[896,512]{1,0:T(8,128)(2,1)}, u32[]{:S(2)}, u32[]{:S(2)}) %collective-permute-start.3) | collective-permute-done | bytes 917536 | tf_op jit(solution)/shard_map/ppermute | solution.py:253
  80.4 2.0 %collective-permute-start.4 = (bf16[896,512]{1,0:T(8,128)(2,1)}, bf16[896,512]{1,0:T(8,128)(2,1)}, u32[]{:S(2)}, u32[]{:S(2)}) collective-permute-start(bf16[896,512]{1,0:T(8,128)(2,1)} %shard_map.90.refs_4_), channel_id=1, source_target_pairs={{0,16},{16,0},{1,17},{17,1},{2,18},{18,2},{3,19},{19,3},{4,20},{20... | collective-permute-start | bytes 2752520 | tf_op jit(solution)/shard_map/ppermute | solution.py:253
  83.1 2.4 %collective-permute-start.5 = (bf16[192,512]{1,0:T(8,128)(2,1)S(1)}, bf16[192,512]{1,0:T(8,128)(2,1)S(1)}, u32[]{:S(2)}, u32[]{:S(2)}) collective-permute-start(bf16[192,512]{1,0:T(8,128)(2,1)S(1)} %get-tuple-element.33), channel_id=1, source_target_pairs={{0,16},{16,0},{1,17},{17,1},{2,18},{18,2},{3,19},{19,3},{4,20},{20... | collective-permute-start | bytes 589832 | tf_op jit(solution)/shard_map/ppermute | solution.py:253
  85.5 3.6 %all-to-all-done.2.refs_1_.refs_2_ = bf16[8,240,128]{2,1,0:T(8,128)(2,1)S(1)} async-done(((bf16[8,240,128]{2,1,0:T(8,128)(2,1)}), bf16[8,240,128]{2,1,0:T(8,128)(2,1)S(1)}, u32[]{:S(2)}, u32[]{:S(2)}) %all-to-all-start.2) | async-done | bytes 491552 | tf_op jit(solution)/shard_map/all_to_all | solution.py:328
  89.1 5.4 %collective-permute-start.8 = (bf16[8,240,128]{2,1,0:T(8,128)(2,1)S(1)}, bf16[8,240,128]{2,1,0:T(8,128)(2,1)S(1)}, u32[]{:S(2)}, u32[]{:S(2)}) collective-permute-start(bf16[8,240,128]{2,1,0:T(8,128)(2,1)S(1)} %all-to-all-done.2.refs_1_.refs_2_), channel_id=1, source_target_pairs={{0,32},{32,0},{1,33},{33,1},{2,34},{34,2},{3,35},{35,3},{4,36},{36... | collective-permute-start | bytes 1474568 | tf_op jit(solution)/shard_map/ppermute | solution.py:253
  94.5 3.7 %shard_map.92 = (bf16[16,44,128]{2,1,0:T(8,128)(2,1)}, f32[8,128]{1,0:T(8,128)}) custom-call(s32[5]{0:T(128)S(1)} %stack.23.refs_0_, bf16[8,240,128]{2,1,0:T(8,128)(2,1)S(1)} %all-to-all-done.2.refs_1_.refs_2_, bf16[512,896]{1,0:T(8,128)(2,1)S(1)} %get-tuple-element.26.refs_2_.refs_0_, bf16[512,896]{1,0:T(8,128)(2,1)S(1)} %collective-permute-done.1.refs_3_, ...), custom_call_target="tpu_custom_call" | custom-call | bytes 4341780 | tf_op jit(solution)/shard_map/pallas_call | solution.py:35
  98.2 9.8 %all-to-all-start.3 = ((bf16[16,44,128]{2,1,0:T(8,128)(2,1)}), bf16[16,44,128]{2,1,0:T(8,128)(2,1)S(1)}, u32[]{:S(2)}, u32[]{:S(2)}) async-start(bf16[16,44,128]{2,1,0:T(8,128)(2,1)} %get-tuple-element.34), calls=%async_computation.3 | async-start | bytes 393216 | tf_op jit(solution)/shard_map/all_to_all | solution.py:345
  108.0 2.1 %collective-permute-start.7 = (bf16[8,240,128]{2,1,0:T(8,128)(2,1)S(1)}, bf16[8,240,128]{2,1,0:T(8,128)(2,1)S(1)}, u32[]{:S(2)}, u32[]{:S(2)}) collective-permute-start(bf16[8,240,128]{2,1,0:T(8,128)(2,1)S(1)} %all-to-all-done.2.refs_1_.refs_2_), channel_id=1, source_target_pairs={{0,16},{16,0},{1,17},{17,1},{2,18},{18,2},{3,19},{19,3},{4,20},{20... | collective-permute-start | bytes 1474568 | tf_op jit(solution)/shard_map/ppermute | solution.py:253
  110.1 2.4 %collective-permute-start.9 = (bf16[8,240,128]{2,1,0:T(8,128)(2,1)S(1)}, bf16[8,240,128]{2,1,0:T(8,128)(2,1)S(1)}, u32[]{:S(2)}, u32[]{:S(2)}) collective-permute-start(bf16[8,240,128]{2,1,0:T(8,128)(2,1)S(1)} %collective-permute-done.8.refs_4_), channel_id=1, source_target_pairs={{0,16},{16,0},{1,17},{17,1},{2,18},{18,2},{3,19},{19,3},{4,20},{20... | collective-permute-start | bytes 1474568 | tf_op jit(solution)/shard_map/ppermute | solution.py:253
  112.5 3.8 %all-to-all-done.3.refs_1_ = bf16[16,44,128]{2,1,0:T(8,128)(2,1)S(1)} async-done(((bf16[16,44,128]{2,1,0:T(8,128)(2,1)}), bf16[16,44,128]{2,1,0:T(8,128)(2,1)S(1)}, u32[]{:S(2)}, u32[]{:S(2)}) %all-to-all-start.3) | async-done | bytes 180256 | tf_op jit(solution)/shard_map/all_to_all | solution.py:345
  117.4 2.3 %collective-permute-start.6 = (bf16[11,512]{1,0:T(8,128)(2,1)S(1)}, bf16[11,512]{1,0:T(8,128)(2,1)S(1)}, u32[]{:S(2)}, u32[]{:S(2)}) collective-permute-start(bf16[11,512]{1,0:T(8,128)(2,1)S(1)} %get-tuple-element.35), channel_id=1, source_target_pairs={{4,0},{13,1},{71,2},{72,3},{130,4},{139,5},{197,6},{206,7},{264,8}... | collective-permute-start | bytes 33800 | tf_op jit(solution)/shard_map/ppermute | solution.py:358
  119.8 1.9 %shard_map.94 = (bf16[256,896]{1,0:T(8,128)(2,1)}, bf16[256,896]{1,0:T(8,128)(2,1)}, bf16[896,256]{1,0:T(8,128)(2,1)}, f32[8,128]{1,0:T(8,128)S(1)}) custom-call(bf16[192,512]{1,0:T(8,128)(2,1)S(1)} %copy-done.1, bf16[192,512]{1,0:T(8,128)(2,1)S(1)} %collective-permute-done.5.refs_6_.refs_1_, bf16[8,240,128]{2,1,0:T(8,128)(2,1)S(1)} %all-to-all-done.2.refs_1_.refs_2_, ...), custom_call_target="tpu_custom_call" | custom-call | bytes 3735552 | tf_op jit(solution)/shard_map/pallas_call | solution.py:35
  121.7 6.2 %collective-permute-done.6.refs_0_ = bf16[11,512]{1,0:T(8,128)(2,1)S(1)} collective-permute-done((bf16[11,512]{1,0:T(8,128)(2,1)S(1)}, bf16[11,512]{1,0:T(8,128)(2,1)S(1)}, u32[]{:S(2)}, u32[]{:S(2)}) %collective-permute-start.6) | collective-permute-done | bytes 11296 | tf_op jit(solution)/shard_map/ppermute | solution.py:358
  (23 shorter events, 8.5 us)
Async XLA Ops:
  2.1 14.5 %collective-permute-start = (bf16[88,128]{1,0:T(8,128)(2,1)S(1)}, bf16[88,128]{1,0:T(8,128)(2,1)S(1)}, u32[]{:S(2)}, u32[]{:S(2)}) collective-permute-start(bf16[88,128]{1,0:T(8,128)(2,1)S(1)} %get-tuple-element.23), channel_id=1, source_target_pairs={{0,4},{1,45},{2,71},{3,104},{4,130},{5,171},{6,197},{7,238},{8,264... | collective-permute-start | bytes 67592 | tf_op jit(solution)/shard_map/ppermute | solution.py:295
  14.7 23.7 %collective-permute-start.1 = (bf16[512,896]{1,0:T(8,128)(2,1)S(1)}, bf16[512,896]{1,0:T(8,128)(2,1)S(1)}, u32[]{:S(2)}, u32[]{:S(2)}) collective-permute-start(bf16[512,896]{1,0:T(8,128)(2,1)S(1)} %get-tuple-element.26.refs_2_.refs_0_), channel_id=1, source_target_pairs={{0,16},{16,0},{1,17},{17,1},{2,18},{18,2},{3,19},{19,3},{4,20},{20... | collective-permute-start | bytes 2752520 | tf_op jit(solution)/shard_map/ppermute | solution.py:253
  17.4 9.0 %copy-start = (bf16[896,256]{1,0:T(8,128)(2,1)S(1)}, bf16[896,256]{1,0:T(8,128)(2,1)}, u32[]{:S(2)}) copy-start(bf16[896,256]{1,0:T(8,128)(2,1)} %refs_4_.1) | copy-start | bytes 1376260
  17.4 20.9 %all-to-all-start = ((bf16[16,88,128]{2,1,0:T(8,128)(2,1)}), bf16[16,88,128]{2,1,0:T(8,128)(2,1)S(1)}, u32[]{:S(2)}, u32[]{:S(2)}) async-start(bf16[16,88,128]{2,1,0:T(8,128)(2,1)} %get-tuple-element.24), calls=%async_computation | async-start | bytes 720896 | tf_op jit(solution)/shard_map/all_to_all | solution.py:297
  26.4 3.7 %collective-permute-start.2 = (bf16[896,256]{1,0:T(8,128)(2,1)S(1)}, bf16[896,256]{1,0:T(8,128)(2,1)S(1)}, u32[]{:S(2)}, u32[]{:S(2)}) collective-permute-start(bf16[896,256]{1,0:T(8,128)(2,1)S(1)} %copy-done), channel_id=1, source_target_pairs={{0,16},{16,0},{1,17},{17,1},{2,18},{18,2},{3,19},{19,3},{4,20},{20... | collective-permute-start | bytes 1376264 | tf_op jit(solution)/shard_map/ppermute | solution.py:253
  40.7 29.2 %all-to-all-start.1 = ((bf16[16,240,128]{2,1,0:T(8,128)(2,1)}), bf16[16,240,128]{2,1,0:T(8,128)(2,1)S(1)}, u32[]{:S(2)}, u32[]{:S(2)}) async-start(bf16[16,240,128]{2,1,0:T(8,128)(2,1)} %get-tuple-element.27), calls=%async_computation.1 | async-start | bytes 1966080 | tf_op jit(solution)/shard_map/all_to_all | solution.py:322
  49.4 31.0 %collective-permute-start.3 = (bf16[896,512]{1,0:T(8,128)(2,1)}, bf16[896,512]{1,0:T(8,128)(2,1)}, u32[]{:S(2)}, u32[]{:S(2)}) collective-permute-start(bf16[896,512]{1,0:T(8,128)(2,1)} %get-tuple-element.30), channel_id=1, source_target_pairs={{0,32},{32,0},{1,33},{33,1},{2,34},{34,2},{3,35},{35,3},{4,36},{36... | collective-permute-start | bytes 2752520 | tf_op jit(solution)/shard_map/ppermute | solution.py:253
  70.8 18.3 %all-to-all-start.2 = ((bf16[8,240,128]{2,1,0:T(8,128)(2,1)}), bf16[8,240,128]{2,1,0:T(8,128)(2,1)S(1)}, u32[]{:S(2)}, u32[]{:S(2)}) async-start(bf16[8,240,128]{2,1,0:T(8,128)(2,1)} %get-tuple-element.28), calls=%async_computation.2 | async-start | bytes 983040 | tf_op jit(solution)/shard_map/all_to_all | solution.py:328
  80.4 2.1 %copy-start.2 = (bf16[192,512]{1,0:T(8,128)(2,1)S(1)}, bf16[192,512]{1,0:T(8,128)(2,1)}, u32[]{:S(2)}) copy-start(bf16[192,512]{1,0:T(8,128)(2,1)} %get-tuple-element.32.refs_0_) | copy-start | bytes 589828
  80.4 14.1 %collective-permute-start.4 = (bf16[896,512]{1,0:T(8,128)(2,1)}, bf16[896,512]{1,0:T(8,128)(2,1)}, u32[]{:S(2)}, u32[]{:S(2)}) collective-permute-start(bf16[896,512]{1,0:T(8,128)(2,1)} %shard_map.90.refs_4_), channel_id=1, source_target_pairs={{0,16},{16,0},{1,17},{17,1},{2,18},{18,2},{3,19},{19,3},{4,20},{20... | collective-permute-start | bytes 2752520 | tf_op jit(solution)/shard_map/ppermute | solution.py:253
  83.1 11.4 %collective-permute-start.5 = (bf16[192,512]{1,0:T(8,128)(2,1)S(1)}, bf16[192,512]{1,0:T(8,128)(2,1)S(1)}, u32[]{:S(2)}, u32[]{:S(2)}) collective-permute-start(bf16[192,512]{1,0:T(8,128)(2,1)S(1)} %get-tuple-element.33), channel_id=1, source_target_pairs={{0,16},{16,0},{1,17},{17,1},{2,18},{18,2},{3,19},{19,3},{4,20},{20... | collective-permute-start | bytes 589832 | tf_op jit(solution)/shard_map/ppermute | solution.py:253
  89.1 21.0 %collective-permute-start.8 = (bf16[8,240,128]{2,1,0:T(8,128)(2,1)S(1)}, bf16[8,240,128]{2,1,0:T(8,128)(2,1)S(1)}, u32[]{:S(2)}, u32[]{:S(2)}) collective-permute-start(bf16[8,240,128]{2,1,0:T(8,128)(2,1)S(1)} %all-to-all-done.2.refs_1_.refs_2_), channel_id=1, source_target_pairs={{0,32},{32,0},{1,33},{33,1},{2,34},{34,2},{3,35},{35,3},{4,36},{36... | collective-permute-start | bytes 1474568 | tf_op jit(solution)/shard_map/ppermute | solution.py:253
  98.2 18.1 %all-to-all-start.3 = ((bf16[16,44,128]{2,1,0:T(8,128)(2,1)}), bf16[16,44,128]{2,1,0:T(8,128)(2,1)S(1)}, u32[]{:S(2)}, u32[]{:S(2)}) async-start(bf16[16,44,128]{2,1,0:T(8,128)(2,1)} %get-tuple-element.34), calls=%async_computation.3 | async-start | bytes 393216 | tf_op jit(solution)/shard_map/all_to_all | solution.py:345
  108.0 11.8 %copy-start.1 = (bf16[192,512]{1,0:T(8,128)(2,1)S(1)}, bf16[192,512]{1,0:T(8,128)(2,1)}, u32[]{:S(2)}) copy-start(bf16[192,512]{1,0:T(8,128)(2,1)} %get-tuple-element.36.refs_0_) | copy-start | bytes 589828
  108.0 11.8 %collective-permute-start.7 = (bf16[8,240,128]{2,1,0:T(8,128)(2,1)S(1)}, bf16[8,240,128]{2,1,0:T(8,128)(2,1)S(1)}, u32[]{:S(2)}, u32[]{:S(2)}) collective-permute-start(bf16[8,240,128]{2,1,0:T(8,128)(2,1)S(1)} %all-to-all-done.2.refs_1_.refs_2_), channel_id=1, source_target_pairs={{0,16},{16,0},{1,17},{17,1},{2,18},{18,2},{3,19},{19,3},{4,20},{20... | collective-permute-start | bytes 1474568 | tf_op jit(solution)/shard_map/ppermute | solution.py:253
  110.1 9.7 %collective-permute-start.9 = (bf16[8,240,128]{2,1,0:T(8,128)(2,1)S(1)}, bf16[8,240,128]{2,1,0:T(8,128)(2,1)S(1)}, u32[]{:S(2)}, u32[]{:S(2)}) collective-permute-start(bf16[8,240,128]{2,1,0:T(8,128)(2,1)S(1)} %collective-permute-done.8.refs_4_), channel_id=1, source_target_pairs={{0,16},{16,0},{1,17},{17,1},{2,18},{18,2},{3,19},{19,3},{4,20},{20... | collective-permute-start | bytes 1474568 | tf_op jit(solution)/shard_map/ppermute | solution.py:253
  117.4 10.4 %collective-permute-start.6 = (bf16[11,512]{1,0:T(8,128)(2,1)S(1)}, bf16[11,512]{1,0:T(8,128)(2,1)S(1)}, u32[]{:S(2)}, u32[]{:S(2)}) collective-permute-start(bf16[11,512]{1,0:T(8,128)(2,1)S(1)} %get-tuple-element.35), channel_id=1, source_target_pairs={{4,0},{13,1},{71,2},{72,3},{130,4},{139,5},{197,6},{206,7},{264,8}... | collective-permute-start | bytes 33800 | tf_op jit(solution)/shard_map/ppermute | solution.py:358

commit v7 on v6

--- a/solution.py
+++ b/solution.py
@@ -12,6 +12,7 @@
 ALL = ("z", "xh", "core", "xl", "y")
 FSDP = ("z", "xh", "core")
 TENSOR = ("xl", "y")
+AROUND = ("y", "xl")
 
 ROWS, QUARTER, PADDED = 11, 88, 96
 UP, ACROSS, PER = 5, 7, 5
@@ -73,7 +74,7 @@
 def put_tiles(out, m, value, half):
     def put(slot, rows):
         row = m * SIZE + slot % PER * 16
-        out[slot // PER * 2 + half, row : row + 16, :] = rows.astype(BF16)
+        out[half * 8 + slot // PER, row : row + 16, :] = rows.astype(BF16)
 
     blank = jnp.zeros((8, 128), F32)
     for i in range(UP):
@@ -124,7 +125,7 @@
     for far in range(2):
         for i in range(8):
             at = (far * 8 + i) * 88
-            wide[at : at + 88, :] = rows[lax.rem(far + place[4], 2) * 8 + came_from(place[2], i)].astype(F32)
+            wide[at : at + 88, :] = rows[came_from(place[2], i) * 2 + lax.rem(far + place[4], 2)].astype(F32)
     blank = jnp.zeros((PADDED - QUARTER, 128), F32)
     for far in range(2):
         for j in range(8):
@@ -197,7 +198,7 @@
     for far in range(2):
         for i in range(8):
             rows = wide[far, i * 4 * ROWS : (i + 1) * 4 * ROWS, :]
-            out[lax.rem(far + place[4], 2) * 8 + came_from(place[2 + far], i)] = rows.astype(BF16)
+            out[came_from(place[2 + far], i) * 2 + lax.rem(far + place[4], 2)] = rows.astype(BF16)
 
 
 def token_sum_kernel(place, parts, out, total):
@@ -234,15 +235,15 @@
     return call(copy_kernel, (shape(*x.shape, dtype=x.dtype),), (x,), deps=deps)[0]
 
 
-def after_in_hbm(x, dep):
+def after_in_hbm(x, *deps):
     return pl.pallas_call(
         lambda *refs: None,
         out_shape=pltpu.HBM(x.shape, x.dtype),
-        in_specs=[HBM, VMEM],
+        in_specs=[HBM] + [VMEM] * len(deps),
         out_specs=HBM,
         input_output_aliases={0: 0},
         compiler_params=PARAMS,
-    )(in_hbm(x), dep)
+    )(in_hbm(x), *deps)
 
 
 def in_hbm(x):
@@ -294,7 +295,7 @@
     )
     packed = lax.ppermute(packed, ALL, there)
     spread, _ = call(spread_kernel, (shape(16, 88, 128),), (packed,), flops=10**11)
-    rows = lax.all_to_all(spread, TENSOR, 0, 0, tiled=True)
+    rows = lax.all_to_all(spread, AROUND, 0, 0, tiled=True)
     gu0, _ = call(
         weights_kernel,
         (shape(512, 896),),
@@ -319,14 +320,14 @@
         specs=[SMEM] + [VMEM] * 5,
         outs=[HBM] * 3,
     )
-    parts = lax.all_to_all(parts, ("z", "xh"), 0, 0, tiled=True)
+    parts = lax.all_to_all(parts, ("xh", "z"), 0, 0, tiled=True)
     x_got = swap("core", after(x_oth, ready))
     t0, _ = call(transpose_kernel, (shape(896, 512),), (gu0,), deps=(ready,))
     t2 = swap("xh", t0)
 
     acts0, ready = call(activation_kernel, (shape(8, 3 * SIZE, 128),), (parts,))
     acts0 = lax.all_to_all(acts0, "z", 0, 0, tiled=True)
-    t2 = after_in_hbm(t2, ready)
+    t2 = after_in_hbm(t2, ready, x_got)
     t3 = swap("core", t2)
     token_parts, ready = call(
         token_grad_kernel,
@@ -340,9 +341,8 @@
             pltpu.SemaphoreType.DMA((2, 2)),
         ],
         specs=[SMEM] + [VMEM] * 3 + [HBM] * 2,
-        deps=(x_got,),
-    )
-    token_parts = lax.all_to_all(token_parts, TENSOR, 0, 0, tiled=True)
+    )
+    token_parts = lax.all_to_all(token_parts, AROUND, 0, 0, tiled=True)
     acts2 = swap("xh", acts0)
     acts1 = swap("core", acts0)
     acts3 = swap("core", acts2)

time: 129 us -> 128 us (level); the launches traced: 128 us -> 126 us
  starting transfers between devices: 63.2 us -> 58.4 us
  waiting for transfers between devices: 47.9 us -> 50.2 us
    all_to_all x1, waiting for transfers between devices: 3.59 us -> 8.58 us  [per_device(): acts0 = lax.all_to_all(acts0, 'z', 0, 0, tiled=True)]
    all_to_all x3, starting transfers between devices: 26.2 us -> 22.6 us  [the longest x1 8.96 us: per_device(): rows = lax.all_to_all(spread, AROUND, 0, 0, tiled=True)]
    ppermute x8, starting transfers between devices: 20.1 us -> 16.9 us  [swap(): return lax.ppermute(x, axis, [(0, 1), (1, 0)])]
    ppermute x8, waiting for transfers between devices: 7.67 us -> 6.21 us  [swap(): return lax.ppermute(x, axis, [(0, 1), (1, 0)])]
  transfers between devices with their start and end apart: 14 -> 14, of which waited for: 7 -> 7; matrix products, arithmetic and copies ran while one was open for 0% -> 0% of each run, Pallas kernels for 9% -> 10%
where the time goes in v7:
time: 128 us; the launch traced here: 126 us
  starting transfers between devices  58.4 us (46%)
  waiting for transfers between devices  50.2 us (39%)
  Pallas kernels  16.4 us (13%)
    ppermute x8, starting transfers between devices, swap(): return lax.ppermute(x, axis, [(0, 1), (1, 0)])  16.9 us
    pallas_call x11, Pallas kernels, call(): pl.pallas_call(body, out_shape=(*out_shape, shape(8, 128, dtype=F32)), in...  16.4 us
    all_to_all x1, waiting for transfers between devices, per_device(): parts = lax.all_to_all(parts, ('xh', 'z'), 0, 0, tiled=True)  15.4 us
    ppermute x1, starting transfers between devices, per_device(): packed = lax.ppermute(packed, ALL, there)  10.8 us
    all_to_all x1, waiting for transfers between devices, per_device(): rows = lax.all_to_all(spread, AROUND, 0, 0, tiled=True)  10 us
    all_to_all x1, starting transfers between devices, per_device(): rows = lax.all_to_all(spread, AROUND, 0, 0, tiled=True)  8.96 us
    all_to_all x1, waiting for transfers between devices, per_device(): acts0 = lax.all_to_all(acts0, 'z', 0, 0, tiled=True)  8.58 us
    all_to_all x1, starting transfers between devices, per_device(): parts = lax.all_to_all(parts, ('xh', 'z'), 0, 0, tiled=True)  7.37 us
  transfers between devices with their start and end apart: 14, of which 7 were waited for; matrix products, arithmetic and copies ran while one was open for 0% of the time, Pallas kernels for 10%

profile of v7, /device:TPU:6, one launch (start us, length us, event | category | flops | bytes accessed | tf_op | source)
XLA Modules:
  0.0 125.9 jit_solution(5744405768031375402)
XLA Ops:
  2.1 10.8 %collective-permute-start = (bf16[88,128]{1,0:T(8,128)(2,1)S(1)}, bf16[88,128]{1,0:T(8,128)(2,1)S(1)}, u32[]{:S(2)}, u32[]{:S(2)}) collective-permute-start(bf16[88,128]{1,0:T(8,128)(2,1)S(1)} %get-tuple-element.23), channel_id=1, source_target_pairs={{0,4},{1,45},{2,71},{3,104},{4,130},{5,171},{6,197},{7,238},{8,264... | collective-permute-start | bytes 67592 | tf_op jit(solution)/shard_map/ppermute | solution.py:296
  14.7 1.9 %collective-permute-start.1 = (bf16[512,896]{1,0:T(8,128)(2,1)S(1)}, bf16[512,896]{1,0:T(8,128)(2,1)S(1)}, u32[]{:S(2)}, u32[]{:S(2)}) collective-permute-start(bf16[512,896]{1,0:T(8,128)(2,1)S(1)} %get-tuple-element.26.refs_2_.refs_0_), channel_id=1, source_target_pairs={{0,16},{16,0},{1,17},{17,1},{2,18},{18,2},{3,19},{19,3},{4,20},{20... | collective-permute-start | bytes 2752520 | tf_op jit(solution)/shard_map/ppermute | solution.py:254
  17.4 9.0 %all-to-all-start = ((bf16[16,88,128]{2,1,0:T(8,128)(2,1)}), bf16[16,88,128]{2,1,0:T(8,128)(2,1)S(1)}, u32[]{:S(2)}, u32[]{:S(2)}) async-start(bf16[16,88,128]{2,1,0:T(8,128)(2,1)} %get-tuple-element.24), calls=%async_computation | async-start | bytes 720896 | tf_op jit(solution)/shard_map/all_to_all | solution.py:298
  26.4 1.9 %collective-permute-start.2 = (bf16[896,256]{1,0:T(8,128)(2,1)S(1)}, bf16[896,256]{1,0:T(8,128)(2,1)S(1)}, u32[]{:S(2)}, u32[]{:S(2)}) collective-permute-start(bf16[896,256]{1,0:T(8,128)(2,1)S(1)} %copy-done), channel_id=1, source_target_pairs={{0,16},{16,0},{1,17},{17,1},{2,18},{18,2},{3,19},{19,3},{4,20},{20... | collective-permute-start | bytes 1376264 | tf_op jit(solution)/shard_map/ppermute | solution.py:254
  28.3 1.8 %collective-permute-done.2.refs_5_ = bf16[896,256]{1,0:T(8,128)(2,1)S(1)} collective-permute-done((bf16[896,256]{1,0:T(8,128)(2,1)S(1)}, bf16[896,256]{1,0:T(8,128)(2,1)S(1)}, u32[]{:S(2)}, u32[]{:S(2)}) %collective-permute-start.2) | collective-permute-done | bytes 458784 | tf_op jit(solution)/shard_map/ppermute | solution.py:254
  30.1 10.0 %all-to-all-done.refs_1_ = bf16[16,88,128]{2,1,0:T(8,128)(2,1)S(1)} async-done(((bf16[16,88,128]{2,1,0:T(8,128)(2,1)}), bf16[16,88,128]{2,1,0:T(8,128)(2,1)S(1)}, u32[]{:S(2)}, u32[]{:S(2)}) %all-to-all-start) | async-done | bytes 360480 | tf_op jit(solution)/shard_map/all_to_all | solution.py:298
  40.1 2.4 %shard_map.87 = (bf16[16,240,128]{2,1,0:T(8,128)(2,1)}, bf16[192,512]{1,0:T(8,128)(2,1)}, bf16[192,512]{1,0:T(8,128)(2,1)}, f32[8,128]{1,0:T(8,128)S(1)}) custom-call(s32[5]{0:T(128)S(1)} %stack.23.refs_0_, bf16[16,88,128]{2,1,0:T(8,128)(2,1)S(1)} %all-to-all-done.refs_1_, bf16[512,896]{1,0:T(8,128)(2,1)S(1)} %get-tuple-element.26.refs_2_.refs_0_, ...), custom_call_target="tpu_custom_call" | custom-call | bytes 4489236 | tf_op jit(solution)/shard_map/pallas_call | solution.py:36
  42.5 7.4 %all-to-all-start.1 = ((bf16[16,240,128]{2,1,0:T(8,128)(2,1)}), bf16[16,240,128]{2,1,0:T(8,128)(2,1)S(1)}, u32[]{:S(2)}, u32[]{:S(2)}) async-start(bf16[16,240,128]{2,1,0:T(8,128)(2,1)} %get-tuple-element.27), calls=%async_computation.1 | async-start | bytes 1966080 | tf_op jit(solution)/shard_map/all_to_all | solution.py:323
  51.1 2.0 %collective-permute-start.3 = (bf16[896,512]{1,0:T(8,128)(2,1)}, bf16[896,512]{1,0:T(8,128)(2,1)}, u32[]{:S(2)}, u32[]{:S(2)}) collective-permute-start(bf16[896,512]{1,0:T(8,128)(2,1)} %get-tuple-element.30), channel_id=1, source_target_pairs={{0,32},{32,0},{1,33},{33,1},{2,34},{34,2},{3,35},{35,3},{4,36},{36... | collective-permute-start | bytes 2752520 | tf_op jit(solution)/shard_map/ppermute | solution.py:254
  53.7 1.9 %collective-permute-start.4 = (bf16[192,512]{1,0:T(8,128)(2,1)S(1)}, bf16[192,512]{1,0:T(8,128)(2,1)S(1)}, u32[]{:S(2)}, u32[]{:S(2)}) collective-permute-start(bf16[192,512]{1,0:T(8,128)(2,1)S(1)} %get-tuple-element.33), channel_id=1, source_target_pairs={{0,16},{16,0},{1,17},{17,1},{2,18},{18,2},{3,19},{19,3},{4,20},{20... | collective-permute-start | bytes 589832 | tf_op jit(solution)/shard_map/ppermute | solution.py:254
  55.6 15.4 %all-to-all-done.1.refs_0_ = bf16[16,240,128]{2,1,0:T(8,128)(2,1)S(1)} async-done(((bf16[16,240,128]{2,1,0:T(8,128)(2,1)}), bf16[16,240,128]{2,1,0:T(8,128)(2,1)S(1)}, u32[]{:S(2)}, u32[]{:S(2)}) %all-to-all-start.1) | async-done | bytes 983072 | tf_op jit(solution)/shard_map/all_to_all | solution.py:323
  71.9 4.9 %all-to-all-start.2 = ((bf16[8,240,128]{2,1,0:T(8,128)(2,1)}), bf16[8,240,128]{2,1,0:T(8,128)(2,1)S(1)}, u32[]{:S(2)}, u32[]{:S(2)}) async-start(bf16[8,240,128]{2,1,0:T(8,128)(2,1)} %get-tuple-element.28), calls=%async_computation.2 | async-start | bytes 983040 | tf_op jit(solution)/shard_map/all_to_all | solution.py:329
  76.9 4.4 %collective-permute-done.3.refs_0_ = bf16[896,512]{1,0:T(8,128)(2,1)} collective-permute-done((bf16[896,512]{1,0:T(8,128)(2,1)}, bf16[896,512]{1,0:T(8,128)(2,1)}, u32[]{:S(2)}, u32[]{:S(2)}) %collective-permute-start.3) | collective-permute-done | bytes 917536 | tf_op jit(solution)/shard_map/ppermute | solution.py:254
  81.3 1.9 %collective-permute-start.5 = (bf16[896,512]{1,0:T(8,128)(2,1)}, bf16[896,512]{1,0:T(8,128)(2,1)}, u32[]{:S(2)}, u32[]{:S(2)}) collective-permute-start(bf16[896,512]{1,0:T(8,128)(2,1)} %shard_map.91.refs_4_), channel_id=1, source_target_pairs={{0,16},{16,0},{1,17},{17,1},{2,18},{18,2},{3,19},{19,3},{4,20},{20... | collective-permute-start | bytes 2752520 | tf_op jit(solution)/shard_map/ppermute | solution.py:254
  83.2 8.6 %all-to-all-done.2.refs_1_.refs_2_ = bf16[8,240,128]{2,1,0:T(8,128)(2,1)S(1)} async-done(((bf16[8,240,128]{2,1,0:T(8,128)(2,1)}), bf16[8,240,128]{2,1,0:T(8,128)(2,1)S(1)}, u32[]{:S(2)}, u32[]{:S(2)}) %all-to-all-start.2) | async-done | bytes 491552 | tf_op jit(solution)/shard_map/all_to_all | solution.py:329
  91.8 2.8 %collective-permute-start.8 = (bf16[8,240,128]{2,1,0:T(8,128)(2,1)S(1)}, bf16[8,240,128]{2,1,0:T(8,128)(2,1)S(1)}, u32[]{:S(2)}, u32[]{:S(2)}) collective-permute-start(bf16[8,240,128]{2,1,0:T(8,128)(2,1)S(1)} %all-to-all-done.2.refs_1_.refs_2_), channel_id=1, source_target_pairs={{0,32},{32,0},{1,33},{33,1},{2,34},{34,2},{3,35},{35,3},{4,36},{36... | collective-permute-start | bytes 1474568 | tf_op jit(solution)/shard_map/ppermute | solution.py:254
  94.6 3.7 %shard_map.92 = (bf16[16,44,128]{2,1,0:T(8,128)(2,1)}, f32[8,128]{1,0:T(8,128)}) custom-call(s32[5]{0:T(128)S(1)} %stack.23.refs_0_, bf16[8,240,128]{2,1,0:T(8,128)(2,1)S(1)} %all-to-all-done.2.refs_1_.refs_2_, bf16[512,896]{1,0:T(8,128)(2,1)S(1)} %get-tuple-element.26.refs_2_.refs_0_, bf16[512,896]{1,0:T(8,128)(2,1)S(1)} %collective-permute-done.1.refs_3_, ...), custom_call_target="tpu_custom_call" | custom-call | bytes 4341780 | tf_op jit(solution)/shard_map/pallas_call | solution.py:36
  98.4 6.2 %all-to-all-start.3 = ((bf16[16,44,128]{2,1,0:T(8,128)(2,1)}), bf16[16,44,128]{2,1,0:T(8,128)(2,1)S(1)}, u32[]{:S(2)}, u32[]{:S(2)}) async-start(bf16[16,44,128]{2,1,0:T(8,128)(2,1)} %get-tuple-element.34), calls=%async_computation.3 | async-start | bytes 393216 | tf_op jit(solution)/shard_map/all_to_all | solution.py:345
  104.6 2.1 %collective-permute-start.7 = (bf16[8,240,128]{2,1,0:T(8,128)(2,1)S(1)}, bf16[8,240,128]{2,1,0:T(8,128)(2,1)S(1)}, u32[]{:S(2)}, u32[]{:S(2)}) collective-permute-start(bf16[8,240,128]{2,1,0:T(8,128)(2,1)S(1)} %all-to-all-done.2.refs_1_.refs_2_), channel_id=1, source_target_pairs={{0,16},{16,0},{1,17},{17,1},{2,18},{18,2},{3,19},{19,3},{4,20},{20... | collective-permute-start | bytes 1474568 | tf_op jit(solution)/shard_map/ppermute | solution.py:254
  106.7 2.4 %collective-permute-start.9 = (bf16[8,240,128]{2,1,0:T(8,128)(2,1)S(1)}, bf16[8,240,128]{2,1,0:T(8,128)(2,1)S(1)}, u32[]{:S(2)}, u32[]{:S(2)}) collective-permute-start(bf16[8,240,128]{2,1,0:T(8,128)(2,1)S(1)} %collective-permute-done.8.refs_4_), channel_id=1, source_target_pairs={{0,16},{16,0},{1,17},{17,1},{2,18},{18,2},{3,19},{19,3},{4,20},{20... | collective-permute-start | bytes 1474568 | tf_op jit(solution)/shard_map/ppermute | solution.py:254
  109.1 4.6 %all-to-all-done.3.refs_1_ = bf16[16,44,128]{2,1,0:T(8,128)(2,1)S(1)} async-done(((bf16[16,44,128]{2,1,0:T(8,128)(2,1)}), bf16[16,44,128]{2,1,0:T(8,128)(2,1)S(1)}, u32[]{:S(2)}, u32[]{:S(2)}) %all-to-all-start.3) | async-done | bytes 180256 | tf_op jit(solution)/shard_map/all_to_all | solution.py:345
  114.8 3.1 %collective-permute-start.6 = (bf16[11,512]{1,0:T(8,128)(2,1)S(1)}, bf16[11,512]{1,0:T(8,128)(2,1)S(1)}, u32[]{:S(2)}, u32[]{:S(2)}) collective-permute-start(bf16[11,512]{1,0:T(8,128)(2,1)S(1)} %get-tuple-element.35), channel_id=1, source_target_pairs={{4,0},{13,1},{71,2},{72,3},{130,4},{139,5},{197,6},{206,7},{264,8}... | collective-permute-start | bytes 33800 | tf_op jit(solution)/shard_map/ppermute | solution.py:358
  118.0 1.9 %shard_map.94 = (bf16[256,896]{1,0:T(8,128)(2,1)}, bf16[256,896]{1,0:T(8,128)(2,1)}, bf16[896,256]{1,0:T(8,128)(2,1)}, f32[8,128]{1,0:T(8,128)S(1)}) custom-call(bf16[192,512]{1,0:T(8,128)(2,1)S(1)} %copy-done.1, bf16[192,512]{1,0:T(8,128)(2,1)S(1)} %collective-permute-done.4.refs_2_.refs_1_, bf16[8,240,128]{2,1,0:T(8,128)(2,1)S(1)} %all-to-all-done.2.refs_1_.refs_2_, ...), custom_call_target="tpu_custom_call" | custom-call | bytes 3735552 | tf_op jit(solution)/shard_map/pallas_call | solution.py:36
  119.9 5.4 %collective-permute-done.6.refs_0_ = bf16[11,512]{1,0:T(8,128)(2,1)S(1)} collective-permute-done((bf16[11,512]{1,0:T(8,128)(2,1)S(1)}, bf16[11,512]{1,0:T(8,128)(2,1)S(1)}, u32[]{:S(2)}, u32[]{:S(2)}) %collective-permute-start.6) | collective-permute-done | bytes 11296 | tf_op jit(solution)/shard_map/ppermute | solution.py:358
  (23 shorter events, 8.5 us)
Async XLA Ops:
  2.1 14.5 %collective-permute-start = (bf16[88,128]{1,0:T(8,128)(2,1)S(1)}, bf16[88,128]{1,0:T(8,128)(2,1)S(1)}, u32[]{:S(2)}, u32[]{:S(2)}) collective-permute-start(bf16[88,128]{1,0:T(8,128)(2,1)S(1)} %get-tuple-element.23), channel_id=1, source_target_pairs={{0,4},{1,45},{2,71},{3,104},{4,130},{5,171},{6,197},{7,238},{8,264... | collective-permute-start | bytes 67592 | tf_op jit(solution)/shard_map/ppermute | solution.py:296
  14.7 25.4 %collective-permute-start.1 = (bf16[512,896]{1,0:T(8,128)(2,1)S(1)}, bf16[512,896]{1,0:T(8,128)(2,1)S(1)}, u32[]{:S(2)}, u32[]{:S(2)}) collective-permute-start(bf16[512,896]{1,0:T(8,128)(2,1)S(1)} %get-tuple-element.26.refs_2_.refs_0_), channel_id=1, source_target_pairs={{0,16},{16,0},{1,17},{17,1},{2,18},{18,2},{3,19},{19,3},{4,20},{20... | collective-permute-start | bytes 2752520 | tf_op jit(solution)/shard_map/ppermute | solution.py:254
  17.4 9.0 %copy-start = (bf16[896,256]{1,0:T(8,128)(2,1)S(1)}, bf16[896,256]{1,0:T(8,128)(2,1)}, u32[]{:S(2)}) copy-start(bf16[896,256]{1,0:T(8,128)(2,1)} %refs_4_.1) | copy-start | bytes 1376260
  17.4 22.7 %all-to-all-start = ((bf16[16,88,128]{2,1,0:T(8,128)(2,1)}), bf16[16,88,128]{2,1,0:T(8,128)(2,1)S(1)}, u32[]{:S(2)}, u32[]{:S(2)}) async-start(bf16[16,88,128]{2,1,0:T(8,128)(2,1)} %get-tuple-element.24), calls=%async_computation | async-start | bytes 720896 | tf_op jit(solution)/shard_map/all_to_all | solution.py:298
  26.4 3.7 %collective-permute-start.2 = (bf16[896,256]{1,0:T(8,128)(2,1)S(1)}, bf16[896,256]{1,0:T(8,128)(2,1)S(1)}, u32[]{:S(2)}, u32[]{:S(2)}) collective-permute-start(bf16[896,256]{1,0:T(8,128)(2,1)S(1)} %copy-done), channel_id=1, source_target_pairs={{0,16},{16,0},{1,17},{17,1},{2,18},{18,2},{3,19},{19,3},{4,20},{20... | collective-permute-start | bytes 1376264 | tf_op jit(solution)/shard_map/ppermute | solution.py:254
  42.5 28.5 %all-to-all-start.1 = ((bf16[16,240,128]{2,1,0:T(8,128)(2,1)}), bf16[16,240,128]{2,1,0:T(8,128)(2,1)S(1)}, u32[]{:S(2)}, u32[]{:S(2)}) async-start(bf16[16,240,128]{2,1,0:T(8,128)(2,1)} %get-tuple-element.27), calls=%async_computation.1 | async-start | bytes 1966080 | tf_op jit(solution)/shard_map/all_to_all | solution.py:323
  49.8 3.2 %copy-start.2 = (bf16[192,512]{1,0:T(8,128)(2,1)S(1)}, bf16[192,512]{1,0:T(8,128)(2,1)}, u32[]{:S(2)}) copy-start(bf16[192,512]{1,0:T(8,128)(2,1)} %get-tuple-element.32.refs_0_) | copy-start | bytes 589828
  51.1 30.2 %collective-permute-start.3 = (bf16[896,512]{1,0:T(8,128)(2,1)}, bf16[896,512]{1,0:T(8,128)(2,1)}, u32[]{:S(2)}, u32[]{:S(2)}) collective-permute-start(bf16[896,512]{1,0:T(8,128)(2,1)} %get-tuple-element.30), channel_id=1, source_target_pairs={{0,32},{32,0},{1,33},{33,1},{2,34},{34,2},{3,35},{35,3},{4,36},{36... | collective-permute-start | bytes 2752520 | tf_op jit(solution)/shard_map/ppermute | solution.py:254
  53.7 23.2 %collective-permute-start.4 = (bf16[192,512]{1,0:T(8,128)(2,1)S(1)}, bf16[192,512]{1,0:T(8,128)(2,1)S(1)}, u32[]{:S(2)}, u32[]{:S(2)}) collective-permute-start(bf16[192,512]{1,0:T(8,128)(2,1)S(1)} %get-tuple-element.33), channel_id=1, source_target_pairs={{0,16},{16,0},{1,17},{17,1},{2,18},{18,2},{3,19},{19,3},{4,20},{20... | collective-permute-start | bytes 589832 | tf_op jit(solution)/shard_map/ppermute | solution.py:254
  71.9 19.9 %all-to-all-start.2 = ((bf16[8,240,128]{2,1,0:T(8,128)(2,1)}), bf16[8,240,128]{2,1,0:T(8,128)(2,1)S(1)}, u32[]{:S(2)}, u32[]{:S(2)}) async-start(bf16[8,240,128]{2,1,0:T(8,128)(2,1)} %get-tuple-element.28), calls=%async_computation.2 | async-start | bytes 983040 | tf_op jit(solution)/shard_map/all_to_all | solution.py:329
  81.3 13.3 %collective-permute-start.5 = (bf16[896,512]{1,0:T(8,128)(2,1)}, bf16[896,512]{1,0:T(8,128)(2,1)}, u32[]{:S(2)}, u32[]{:S(2)}) collective-permute-start(bf16[896,512]{1,0:T(8,128)(2,1)} %shard_map.91.refs_4_), channel_id=1, source_target_pairs={{0,16},{16,0},{1,17},{17,1},{2,18},{18,2},{3,19},{19,3},{4,20},{20... | collective-permute-start | bytes 2752520 | tf_op jit(solution)/shard_map/ppermute | solution.py:254
  91.8 14.9 %collective-permute-start.8 = (bf16[8,240,128]{2,1,0:T(8,128)(2,1)S(1)}, bf16[8,240,128]{2,1,0:T(8,128)(2,1)S(1)}, u32[]{:S(2)}, u32[]{:S(2)}) collective-permute-start(bf16[8,240,128]{2,1,0:T(8,128)(2,1)S(1)} %all-to-all-done.2.refs_1_.refs_2_), channel_id=1, source_target_pairs={{0,32},{32,0},{1,33},{33,1},{2,34},{34,2},{3,35},{35,3},{4,36},{36... | collective-permute-start | bytes 1474568 | tf_op jit(solution)/shard_map/ppermute | solution.py:254
  98.4 15.3 %all-to-all-start.3 = ((bf16[16,44,128]{2,1,0:T(8,128)(2,1)}), bf16[16,44,128]{2,1,0:T(8,128)(2,1)S(1)}, u32[]{:S(2)}, u32[]{:S(2)}) async-start(bf16[16,44,128]{2,1,0:T(8,128)(2,1)} %get-tuple-element.34), calls=%async_computation.3 | async-start | bytes 393216 | tf_op jit(solution)/shard_map/all_to_all | solution.py:345
  104.6 13.3 %copy-start.1 = (bf16[192,512]{1,0:T(8,128)(2,1)S(1)}, bf16[192,512]{1,0:T(8,128)(2,1)}, u32[]{:S(2)}) copy-start(bf16[192,512]{1,0:T(8,128)(2,1)} %get-tuple-element.36.refs_0_) | copy-start | bytes 589828
  104.6 13.3 %collective-permute-start.7 = (bf16[8,240,128]{2,1,0:T(8,128)(2,1)S(1)}, bf16[8,240,128]{2,1,0:T(8,128)(2,1)S(1)}, u32[]{:S(2)}, u32[]{:S(2)}) collective-permute-start(bf16[8,240,128]{2,1,0:T(8,128)(2,1)S(1)} %all-to-all-done.2.refs_1_.refs_2_), channel_id=1, source_target_pairs={{0,16},{16,0},{1,17},{17,1},{2,18},{18,2},{3,19},{19,3},{4,20},{20... | collective-permute-start | bytes 1474568 | tf_op jit(solution)/shard_map/ppermute | solution.py:254
  106.7 11.3 %collective-permute-start.9 = (bf16[8,240,128]{2,1,0:T(8,128)(2,1)S(1)}, bf16[8,240,128]{2,1,0:T(8,128)(2,1)S(1)}, u32[]{:S(2)}, u32[]{:S(2)}) collective-permute-start(bf16[8,240,128]{2,1,0:T(8,128)(2,1)S(1)} %collective-permute-done.8.refs_4_), channel_id=1, source_target_pairs={{0,16},{16,0},{1,17},{17,1},{2,18},{18,2},{3,19},{19,3},{4,20},{20... | collective-permute-start | bytes 1474568 | tf_op jit(solution)/shard_map/ppermute | solution.py:254
  114.8 10.4 %collective-permute-start.6 = (bf16[11,512]{1,0:T(8,128)(2,1)S(1)}, bf16[11,512]{1,0:T(8,128)(2,1)S(1)}, u32[]{:S(2)}, u32[]{:S(2)}) collective-permute-start(bf16[11,512]{1,0:T(8,128)(2,1)S(1)} %get-tuple-element.35), channel_id=1, source_target_pairs={{4,0},{13,1},{71,2},{72,3},{130,4},{139,5},{197,6},{206,7},{264,8}... | collective-permute-start | bytes 33800 | tf_op jit(solution)/shard_map/ppermute | solution.py:358

commit v8 on v7

--- a/solution.py
+++ b/solution.py
@@ -15,29 +15,30 @@
 AROUND = ("y", "xl")
 
 ROWS, QUARTER, PADDED = 11, 88, 96
+BLOCK = 48
 UP, ACROSS, PER = 5, 7, 5
 SIZE = PER * 16
 VMEM = pl.BlockSpec(memory_space=pltpu.VMEM)
 HBM = pl.BlockSpec(memory_space=pltpu.HBM)
-SMEM = pl.BlockSpec(memory_space=pltpu.SMEM)
 PARAMS = pltpu.CompilerParams(vmem_limit_bytes=20 * 1024 * 1024)
 
 
-def call(kernel, out_shape, inputs, scratch=(), specs=None, flops=0, deps=(), outs=None):
+def call(kernel, out_shape, inputs, scratch=(), specs=None, flops=0, deps=(), outs=None, token=True):
     moved = sum(x.size * x.dtype.itemsize for x in inputs)
     moved += sum(math.prod(s.shape) * s.dtype.itemsize for s in out_shape)
     n, m = len(inputs), len(out_shape)
 
     def body(*refs):
         rest = refs[n + len(deps) :]
-        rest[m][...] = jnp.zeros((8, 128), F32)
-        kernel(*refs[:n], *rest[:m], *rest[m + 1 :])
+        if token:
+            rest[m][...] = jnp.zeros((8, 128), F32)
+        kernel(*refs[:n], *rest[:m], *rest[m + token :])
 
     return pl.pallas_call(
         body,
-        out_shape=(*out_shape, shape(8, 128, dtype=F32)),
+        out_shape=(*out_shape, *[shape(8, 128, dtype=F32)] * token),
         in_specs=list(specs or [VMEM] * n) + [VMEM] * len(deps),
-        out_specs=list(outs or [VMEM] * m) + [VMEM],
+        out_specs=list(outs or [VMEM] * m) + [VMEM] * token,
         scratch_shapes=list(scratch),
         compiler_params=PARAMS,
         cost_estimate=pl.CostEstimate(flops=flops, bytes_accessed=moved, transcendentals=0),
@@ -60,15 +61,21 @@
         copy.wait()
 
 
-def pack_kernel(place, tok_hbm, cot_hbm, out, wide, tok, cot, sems):
+def here():
+    z, xh, core = (lax.axis_index(axis) for axis in FSDP)
+    base = z + 4 + lax.rem(z, 4) * 2
+    return core, xh, lax.rem(base + xh, 8), lax.rem(base + 1 - xh, 8), z // 4
+
+
+def pack_kernel(tok_hbm, cot_hbm, out, wide, tok, cot, sems):
     fetch(sems, (tok_hbm, tok), (cot_hbm, cot))
-    odd = place[0] == 1
+    odd = here()[0] == 1
     for base, ref in ((0, tok), (4, cot)):
         rows = ref[...].astype(F32)
         for j in range(4):
             piece = jnp.where(odd, tile(rows, (j + 2) % 4), tile(rows, j))
             wide[pl.ds(base + j, ROWS, stride=8), :] = piece
-    out[...] = wide[...].astype(BF16)
+    out[...] = wide[:88, :].astype(BF16)
 
 
 def put_tiles(out, m, value, half):
@@ -120,8 +127,9 @@
 
 
 def forward_kernel(
-    place, rows, gu0, gu1, down0, down1, out, own_out, oth_out, wide, parts, x_own, x_oth, sems
+    rows, gu0, gu1, down0, down1, out, own_out, oth_out, wide, parts, x_own, x_oth, sems
 ):
+    place = here()
     for far in range(2):
         for i in range(8):
             at = (far * 8 + i) * 88
@@ -148,8 +156,8 @@
         total = total + lax.dot_general(x_oth[:, cols], oth, dims, preferred_element_type=F32)
         put_tiles(parts, m, total[:PADDED], place[1])
         put_tiles(parts, m, total[PADDED:], 1 - place[1])
-        here = pl.ds(m * SIZE, SIZE)
-        copies.append(pltpu.make_async_copy(parts.at[:, here], out.at[:, here], sems.at[m]))
+        which = pl.ds(m * SIZE, SIZE)
+        copies.append(pltpu.make_async_copy(parts.at[:, which], out.at[:, which], sems.at[m]))
         copies[-1].start()
     for copy in copies:
         copy.wait()
@@ -173,7 +181,7 @@
 HALVES = (pl.ds(0, 448), pl.ds(448, 448))
 
 
-def token_grad_kernel(place, acts, gu0, gu1, t2_hbm, t3_hbm, out, gate_act, up_act, wide, ts, sems):
+def token_grad_kernel(acts, gu0, gu1, t2_hbm, t3_hbm, out, gate_act, up_act, wide, ts, sems):
     copies = [
         [pltpu.make_async_copy(t_hbm.at[rows], ts.at[k, rows], sems.at[k, i]) for i, rows in enumerate(parts)]
         for k, t_hbm, parts in ((0, t2_hbm, HALVES), (1, t3_hbm, HALVES))
@@ -182,6 +190,7 @@
         copy.start()
     get_tiles(acts, 0, gate_act, 0)
     get_tiles(acts, 1, up_act, 0)
+    place = here()
     contract_cols = (((1,), (1,)), ((), ()))
     for k in range(4):
         if k < 2:
@@ -195,14 +204,15 @@
             part = part + jnp.dot(up_act[...], ts[k - 2, :, 256:], preferred_element_type=F32)
         for j in range(2):
             wide[k // 2, pl.ds(k % 2 * 2 + j, QUARTER, stride=4), :] = tile(part[:QUARTER], j)
+    wide[:, 4 * QUARTER :, :] = jnp.zeros((2, 8, 128), F32)
     for far in range(2):
         for i in range(8):
-            rows = wide[far, i * 4 * ROWS : (i + 1) * 4 * ROWS, :]
+            rows = wide[far, i * 4 * ROWS : i * 4 * ROWS + BLOCK, :]
             out[came_from(place[2 + far], i) * 2 + lax.rem(far + place[4], 2)] = rows.astype(BF16)
 
 
-def token_sum_kernel(place, parts, out, total):
-    odd = place[0] == 1
+def token_sum_kernel(parts, out, total):
+    odd = here()[0] == 1
     acc = parts[0].astype(F32)
     for t in range(1, 16):
         acc = acc + parts[t].astype(F32)
@@ -232,7 +242,7 @@
 
 
 def after(x, *deps):
-    return call(copy_kernel, (shape(*x.shape, dtype=x.dtype),), (x,), deps=deps)[0]
+    return call(copy_kernel, (shape(*x.shape, dtype=x.dtype),), (x,), deps=deps, token=False)[0]
 
 
 def after_in_hbm(x, *deps):
@@ -264,9 +274,6 @@
 
 
 def per_device(tokens, cotangent, gate_weight, up_weight, down_weight):
-    z, xh, core = (lax.axis_index(axis) for axis in FSDP)
-    base = z + 4 + z % 4 * 2
-    place = jnp.stack([core, xh, (base + xh) % 8, (base + 1 - xh) % 8, z // 4]).astype(jnp.int32)
     def chip(z, xl, y):
         return 4 * xl + y // 2, (y + 4 - z + 4 * xl + y // 2) % 8
 
@@ -284,76 +291,77 @@
     packed, ready0 = call(
         pack_kernel,
         (shape(88, 128),),
-        (place, in_hbm(tokens), in_hbm(cotangent)),
+        (in_hbm(tokens), in_hbm(cotangent)),
         [
-            pltpu.VMEM((88, 128), F32),
+            pltpu.VMEM((96, 128), F32),
             pltpu.VMEM((ROWS, 512), BF16),
             pltpu.VMEM((ROWS, 512), BF16),
             pltpu.SemaphoreType.DMA((2,)),
         ],
-        specs=[SMEM, HBM, HBM],
+        specs=[HBM, HBM],
     )
     packed = lax.ppermute(packed, ALL, there)
-    spread, _ = call(spread_kernel, (shape(16, 88, 128),), (packed,), flops=10**11)
+    (spread,) = call(spread_kernel, (shape(16, 88, 128),), (packed,), flops=10**11, token=False)
     rows = lax.all_to_all(spread, AROUND, 0, 0, tiled=True)
-    gu0, _ = call(
+    (gu0,) = call(
         weights_kernel,
         (shape(512, 896),),
         (in_hbm(gate_weight), in_hbm(up_weight)),
         [pltpu.SemaphoreType.DMA((2,))],
         specs=[HBM, HBM],
         deps=(ready0,),
+        token=False,
     )
     gu1, down1 = swap("core", gu0), swap("core", down_weight)
 
     parts, x_own, x_oth, ready = call(
         forward_kernel,
         (pltpu.HBM((16, 3 * SIZE, 128), BF16), *[pltpu.HBM((2 * PADDED, 512), BF16)] * 2),
-        (place, rows, gu0, gu1, down_weight, down1),
+        (rows, gu0, gu1, down_weight, down1),
         [
-            pltpu.VMEM((16 * 88, 128), F32),
+            pltpu.VMEM((17 * 88, 128), F32),
             pltpu.VMEM((16, 3 * SIZE, 128), BF16),
             pltpu.VMEM((2 * PADDED, 512), BF16),
             pltpu.VMEM((2 * PADDED, 512), BF16),
             pltpu.SemaphoreType.DMA((5,)),
         ],
-        specs=[SMEM] + [VMEM] * 5,
         outs=[HBM] * 3,
     )
     parts = lax.all_to_all(parts, ("xh", "z"), 0, 0, tiled=True)
     x_got = swap("core", after(x_oth, ready))
-    t0, _ = call(transpose_kernel, (shape(896, 512),), (gu0,), deps=(ready,))
+    (t0,) = call(transpose_kernel, (shape(896, 512),), (gu0,), deps=(ready,), token=False)
     t2 = swap("xh", t0)
 
     acts0, ready = call(activation_kernel, (shape(8, 3 * SIZE, 128),), (parts,))
     acts0 = lax.all_to_all(acts0, "z", 0, 0, tiled=True)
     t2 = after_in_hbm(t2, ready, x_got)
     t3 = swap("core", t2)
-    token_parts, ready = call(
+    (token_parts,) = call(
         token_grad_kernel,
-        (shape(16, 4 * ROWS, 128),),
-        (place, acts0, gu0, gu1, in_hbm(t2), in_hbm(t3)),
+        (shape(16, BLOCK, 128),),
+        (acts0, gu0, gu1, in_hbm(t2), in_hbm(t3)),
         [
             pltpu.VMEM((PADDED, 896), BF16),
             pltpu.VMEM((PADDED, 896), BF16),
-            pltpu.VMEM((2, 4 * QUARTER, 128), F32),
+            pltpu.VMEM((2, 4 * QUARTER + 8, 128), F32),
             pltpu.VMEM((2, 896, 512), BF16),
             pltpu.SemaphoreType.DMA((2, 2)),
         ],
-        specs=[SMEM] + [VMEM] * 3 + [HBM] * 2,
+        specs=[VMEM] * 3 + [HBM] * 2,
+        token=False,
     )
     token_parts = lax.all_to_all(token_parts, AROUND, 0, 0, tiled=True)
     acts2 = swap("xh", acts0)
     acts1 = swap("core", acts0)
     acts3 = swap("core", acts2)
 
-    grad_tokens, _ = call(
+    (grad_tokens,) = call(
         token_sum_kernel,
         (shape(ROWS, 512),),
-        (place, token_parts),
-        [pltpu.VMEM((4 * ROWS, 128), F32)],
-        specs=[SMEM, VMEM],
+        (token_parts,),
+        [pltpu.VMEM((BLOCK, 128), F32)],
         flops=10**11,
+        token=False,
     )
     grad_tokens = lax.ppermute(grad_tokens, ALL, home)
 

time: 128 us -> 124 us (0.969)
  Pallas kernels: 16.4 us -> 12.4 us
    pallas_call x11, Pallas kernels: 16.4 us -> 12.4 us  [call(): pl.pallas_call(body, out_shape=(*out_shape, *[shape(8, 128, dtype=F32)] *...]
  transfers between devices with their start and end apart: 14 -> 14, of which waited for: 7 -> 7; matrix products, arithmetic and copies ran while one was open for 0% -> 0% of each run, Pallas kernels for 10% -> 8%
where the time goes in v8:
time: 124 us; the launch traced here: 122 us
  starting transfers between devices  58.5 us (47%)
  waiting for transfers between devices  49.8 us (40%)
  Pallas kernels  12.4 us (10%)
    ppermute x8, starting transfers between devices, swap(): return lax.ppermute(x, axis, [(0, 1), (1, 0)])  17.3 us
    all_to_all x1, waiting for transfers between devices, per_device(): parts = lax.all_to_all(parts, ('xh', 'z'), 0, 0, tiled=True)  15.4 us
    pallas_call x11, Pallas kernels, call(): pl.pallas_call(body, out_shape=(*out_shape, *[shape(8, 128, dtype=F32)] *...  12.4 us
    ppermute x1, starting transfers between devices, per_device(): packed = lax.ppermute(packed, ALL, there)  10.8 us
    all_to_all x1, waiting for transfers between devices, per_device(): rows = lax.all_to_all(spread, AROUND, 0, 0, tiled=True)  10 us
    all_to_all x1, starting transfers between devices, per_device(): rows = lax.all_to_all(spread, AROUND, 0, 0, tiled=True)  8.95 us
    all_to_all x1, waiting for transfers between devices, per_device(): acts0 = lax.all_to_all(acts0, 'z', 0, 0, tiled=True)  8.17 us
    all_to_all x1, starting transfers between devices, per_device(): parts = lax.all_to_all(parts, ('xh', 'z'), 0, 0, tiled=True)  7.97 us
  transfers between devices with their start and end apart: 14, of which 7 were waited for; matrix products, arithmetic and copies ran while one was open for 0% of the time, Pallas kernels for 8%

profile of v8, /device:TPU:6, one launch (start us, length us, event | category | flops | bytes accessed | tf_op | source)
XLA Modules:
  0.0 121.5 jit_solution(6490690198888355255)
XLA Ops:
  1.4 10.8 %collective-permute-start = (bf16[88,128]{1,0:T(8,128)(2,1)S(1)}, bf16[88,128]{1,0:T(8,128)(2,1)S(1)}, u32[]{:S(2)}, u32[]{:S(2)}) collective-permute-start(bf16[88,128]{1,0:T(8,128)(2,1)S(1)} %get-tuple-element.16), channel_id=1, source_target_pairs={{0,4},{1,45},{2,71},{3,104},{4,130},{5,171},{6,197},{7,238},{8,264... | collective-permute-start | bytes 67592 | tf_op jit(solution)/shard_map/ppermute | solution.py:303
  13.4 1.9 %collective-permute-start.1 = (bf16[512,896]{1,0:T(8,128)(2,1)S(1)}, bf16[512,896]{1,0:T(8,128)(2,1)S(1)}, u32[]{:S(2)}, u32[]{:S(2)}) collective-permute-start(bf16[512,896]{1,0:T(8,128)(2,1)S(1)} %shard_map.86.refs_1_.refs_0_), channel_id=1, source_target_pairs={{0,16},{16,0},{1,17},{17,1},{2,18},{18,2},{3,19},{19,3},{4,20},{20... | collective-permute-start | bytes 2752520 | tf_op jit(solution)/shard_map/ppermute | solution.py:264
  16.2 9.0 %all-to-all-start = ((bf16[16,88,128]{2,1,0:T(8,128)(2,1)}), bf16[16,88,128]{2,1,0:T(8,128)(2,1)S(1)}, u32[]{:S(2)}, u32[]{:S(2)}) async-start(bf16[16,88,128]{2,1,0:T(8,128)(2,1)} %shard_map.85), calls=%async_computation | async-start | bytes 720896 | tf_op jit(solution)/shard_map/all_to_all | solution.py:305
  25.1 1.9 %collective-permute-start.2 = (bf16[896,256]{1,0:T(8,128)(2,1)S(1)}, bf16[896,256]{1,0:T(8,128)(2,1)S(1)}, u32[]{:S(2)}, u32[]{:S(2)}) collective-permute-start(bf16[896,256]{1,0:T(8,128)(2,1)S(1)} %copy-done), channel_id=1, source_target_pairs={{0,16},{16,0},{1,17},{17,1},{2,18},{18,2},{3,19},{19,3},{4,20},{20... | collective-permute-start | bytes 1376264 | tf_op jit(solution)/shard_map/ppermute | solution.py:264
  27.0 1.8 %collective-permute-done.2.refs_4_ = bf16[896,256]{1,0:T(8,128)(2,1)S(1)} collective-permute-done((bf16[896,256]{1,0:T(8,128)(2,1)S(1)}, bf16[896,256]{1,0:T(8,128)(2,1)S(1)}, u32[]{:S(2)}, u32[]{:S(2)}) %collective-permute-start.2) | collective-permute-done | bytes 458784 | tf_op jit(solution)/shard_map/ppermute | solution.py:264
  28.8 10.0 %all-to-all-done.refs_0_ = bf16[16,88,128]{2,1,0:T(8,128)(2,1)S(1)} async-done(((bf16[16,88,128]{2,1,0:T(8,128)(2,1)}), bf16[16,88,128]{2,1,0:T(8,128)(2,1)S(1)}, u32[]{:S(2)}, u32[]{:S(2)}) %all-to-all-start) | async-done | bytes 360480 | tf_op jit(solution)/shard_map/all_to_all | solution.py:305
  38.8 1.8 %shard_map.87 = (bf16[16,240,128]{2,1,0:T(8,128)(2,1)}, bf16[192,512]{1,0:T(8,128)(2,1)}, bf16[192,512]{1,0:T(8,128)(2,1)}, f32[8,128]{1,0:T(8,128)S(1)}) custom-call(bf16[16,88,128]{2,1,0:T(8,128)(2,1)S(1)} %all-to-all-done.refs_0_, bf16[512,896]{1,0:T(8,128)(2,1)S(1)} %shard_map.86.refs_1_.refs_0_, bf16[512,896]{1,0:T(8,128)(2,1)S(1)} %collective-permute-done.1.refs_2_, ...), custom_call_target="tpu_custom_call" | custom-call | bytes 4489216 | tf_op jit(solution)/shard_map/pallas_call | solution.py:37
  40.7 8.0 %all-to-all-start.1 = ((bf16[16,240,128]{2,1,0:T(8,128)(2,1)}), bf16[16,240,128]{2,1,0:T(8,128)(2,1)S(1)}, u32[]{:S(2)}, u32[]{:S(2)}) async-start(bf16[16,240,128]{2,1,0:T(8,128)(2,1)} %get-tuple-element.18), calls=%async_computation.1 | async-start | bytes 1966080 | tf_op jit(solution)/shard_map/all_to_all | solution.py:330
  49.9 2.0 %collective-permute-start.3 = (bf16[896,512]{1,0:T(8,128)(2,1)}, bf16[896,512]{1,0:T(8,128)(2,1)}, u32[]{:S(2)}, u32[]{:S(2)}) collective-permute-start(bf16[896,512]{1,0:T(8,128)(2,1)} %shard_map.89), channel_id=1, source_target_pairs={{0,32},{32,0},{1,33},{33,1},{2,34},{34,2},{3,35},{35,3},{4,36},{36... | collective-permute-start | bytes 2752520 | tf_op jit(solution)/shard_map/ppermute | solution.py:264
  51.9 1.9 %collective-permute-start.4 = (bf16[192,512]{1,0:T(8,128)(2,1)S(1)}, bf16[192,512]{1,0:T(8,128)(2,1)S(1)}, u32[]{:S(2)}, u32[]{:S(2)}) collective-permute-start(bf16[192,512]{1,0:T(8,128)(2,1)S(1)} %shard_map.90), channel_id=1, source_target_pairs={{0,16},{16,0},{1,17},{17,1},{2,18},{18,2},{3,19},{19,3},{4,20},{20... | collective-permute-start | bytes 589832 | tf_op jit(solution)/shard_map/ppermute | solution.py:264
  53.8 15.4 %all-to-all-done.1.refs_0_ = bf16[16,240,128]{2,1,0:T(8,128)(2,1)S(1)} async-done(((bf16[16,240,128]{2,1,0:T(8,128)(2,1)}), bf16[16,240,128]{2,1,0:T(8,128)(2,1)S(1)}, u32[]{:S(2)}, u32[]{:S(2)}) %all-to-all-start.1) | async-done | bytes 983072 | tf_op jit(solution)/shard_map/all_to_all | solution.py:330
  70.1 4.9 %all-to-all-start.2 = ((bf16[8,240,128]{2,1,0:T(8,128)(2,1)}), bf16[8,240,128]{2,1,0:T(8,128)(2,1)S(1)}, u32[]{:S(2)}, u32[]{:S(2)}) async-start(bf16[8,240,128]{2,1,0:T(8,128)(2,1)} %get-tuple-element.19), calls=%async_computation.2 | async-start | bytes 983040 | tf_op jit(solution)/shard_map/all_to_all | solution.py:336
  75.0 4.4 %collective-permute-done.3.refs_0_ = bf16[896,512]{1,0:T(8,128)(2,1)} collective-permute-done((bf16[896,512]{1,0:T(8,128)(2,1)}, bf16[896,512]{1,0:T(8,128)(2,1)}, u32[]{:S(2)}, u32[]{:S(2)}) %collective-permute-start.3) | collective-permute-done | bytes 917536 | tf_op jit(solution)/shard_map/ppermute | solution.py:264
  79.5 1.9 %collective-permute-start.5 = (bf16[896,512]{1,0:T(8,128)(2,1)}, bf16[896,512]{1,0:T(8,128)(2,1)}, u32[]{:S(2)}, u32[]{:S(2)}) collective-permute-start(bf16[896,512]{1,0:T(8,128)(2,1)} %shard_map.91.refs_3_), channel_id=1, source_target_pairs={{0,16},{16,0},{1,17},{17,1},{2,18},{18,2},{3,19},{19,3},{4,20},{20... | collective-permute-start | bytes 2752520 | tf_op jit(solution)/shard_map/ppermute | solution.py:264
  81.4 8.2 %all-to-all-done.2.refs_0_.refs_2_ = bf16[8,240,128]{2,1,0:T(8,128)(2,1)S(1)} async-done(((bf16[8,240,128]{2,1,0:T(8,128)(2,1)}), bf16[8,240,128]{2,1,0:T(8,128)(2,1)S(1)}, u32[]{:S(2)}, u32[]{:S(2)}) %all-to-all-start.2) | async-done | bytes 491552 | tf_op jit(solution)/shard_map/all_to_all | solution.py:336
  89.6 3.2 %collective-permute-start.8 = (bf16[8,240,128]{2,1,0:T(8,128)(2,1)S(1)}, bf16[8,240,128]{2,1,0:T(8,128)(2,1)S(1)}, u32[]{:S(2)}, u32[]{:S(2)}) collective-permute-start(bf16[8,240,128]{2,1,0:T(8,128)(2,1)S(1)} %all-to-all-done.2.refs_0_.refs_2_), channel_id=1, source_target_pairs={{0,32},{32,0},{1,33},{33,1},{2,34},{34,2},{3,35},{35,3},{4,36},{36... | collective-permute-start | bytes 1474568 | tf_op jit(solution)/shard_map/ppermute | solution.py:264
  92.8 3.2 %shard_map.92 = bf16[16,48,128]{2,1,0:T(8,128)(2,1)} custom-call(bf16[8,240,128]{2,1,0:T(8,128)(2,1)S(1)} %all-to-all-done.2.refs_0_.refs_2_, bf16[512,896]{1,0:T(8,128)(2,1)S(1)} %shard_map.86.refs_1_.refs_0_, bf16[512,896]{1,0:T(8,128)(2,1)S(1)} %collective-permute-done.1.refs_2_, bf16[896,512]{1,0:T(8,128)(2,1)} %shard_map.91.refs_3_, ...), custom_call_target="tpu_custom_call" | custom-call | bytes 4358144 | tf_op jit(solution)/shard_map/pallas_call | solution.py:37
  96.0 5.4 %all-to-all-start.3 = ((bf16[16,48,128]{2,1,0:T(8,128)(2,1)}), bf16[16,48,128]{2,1,0:T(8,128)(2,1)S(1)}, u32[]{:S(2)}, u32[]{:S(2)}) async-start(bf16[16,48,128]{2,1,0:T(8,128)(2,1)} %shard_map.92), calls=%async_computation.3 | async-start | bytes 393216 | tf_op jit(solution)/shard_map/all_to_all | solution.py:353
  101.3 2.1 %collective-permute-start.7 = (bf16[8,240,128]{2,1,0:T(8,128)(2,1)S(1)}, bf16[8,240,128]{2,1,0:T(8,128)(2,1)S(1)}, u32[]{:S(2)}, u32[]{:S(2)}) collective-permute-start(bf16[8,240,128]{2,1,0:T(8,128)(2,1)S(1)} %all-to-all-done.2.refs_0_.refs_2_), channel_id=1, source_target_pairs={{0,16},{16,0},{1,17},{17,1},{2,18},{18,2},{3,19},{19,3},{4,20},{20... | collective-permute-start | bytes 1474568 | tf_op jit(solution)/shard_map/ppermute | solution.py:264
  103.4 2.4 %collective-permute-start.9 = (bf16[8,240,128]{2,1,0:T(8,128)(2,1)S(1)}, bf16[8,240,128]{2,1,0:T(8,128)(2,1)S(1)}, u32[]{:S(2)}, u32[]{:S(2)}) collective-permute-start(bf16[8,240,128]{2,1,0:T(8,128)(2,1)S(1)} %collective-permute-done.8.refs_4_), channel_id=1, source_target_pairs={{0,16},{16,0},{1,17},{17,1},{2,18},{18,2},{3,19},{19,3},{4,20},{20... | collective-permute-start | bytes 1474568 | tf_op jit(solution)/shard_map/ppermute | solution.py:264
  105.8 4.6 %all-to-all-done.3.refs_0_ = bf16[16,48,128]{2,1,0:T(8,128)(2,1)S(1)} async-done(((bf16[16,48,128]{2,1,0:T(8,128)(2,1)}), bf16[16,48,128]{2,1,0:T(8,128)(2,1)S(1)}, u32[]{:S(2)}, u32[]{:S(2)}) %all-to-all-start.3) | async-done | bytes 196640 | tf_op jit(solution)/shard_map/all_to_all | solution.py:353
  110.5 3.1 %collective-permute-start.6 = (bf16[11,512]{1,0:T(8,128)(2,1)S(1)}, bf16[11,512]{1,0:T(8,128)(2,1)S(1)}, u32[]{:S(2)}, u32[]{:S(2)}) collective-permute-start(bf16[11,512]{1,0:T(8,128)(2,1)S(1)} %shard_map.93), channel_id=1, source_target_pairs={{4,0},{13,1},{71,2},{72,3},{130,4},{139,5},{197,6},{206,7},{264,8}... | collective-permute-start | bytes 33800 | tf_op jit(solution)/shard_map/ppermute | solution.py:366
  113.6 1.9 %shard_map.94 = (bf16[256,896]{1,0:T(8,128)(2,1)}, bf16[256,896]{1,0:T(8,128)(2,1)}, bf16[896,256]{1,0:T(8,128)(2,1)}, f32[8,128]{1,0:T(8,128)S(1)}) custom-call(bf16[192,512]{1,0:T(8,128)(2,1)S(1)} %copy-done.1, bf16[192,512]{1,0:T(8,128)(2,1)S(1)} %collective-permute-done.4.refs_2_.refs_1_, bf16[8,240,128]{2,1,0:T(8,128)(2,1)S(1)} %all-to-all-done.2.refs_0_.refs_2_, ...), custom_call_target="tpu_custom_call" | custom-call | bytes 3735552 | tf_op jit(solution)/shard_map/pallas_call | solution.py:37
  115.5 5.4 %collective-permute-done.6.refs_0_ = bf16[11,512]{1,0:T(8,128)(2,1)S(1)} collective-permute-done((bf16[11,512]{1,0:T(8,128)(2,1)S(1)}, bf16[11,512]{1,0:T(8,128)(2,1)S(1)}, u32[]{:S(2)}, u32[]{:S(2)}) %collective-permute-start.6) | collective-permute-done | bytes 11296 | tf_op jit(solution)/shard_map/ppermute | solution.py:366
  (22 shorter events, 5.6 us)
Async XLA Ops:
  1.4 14.0 %collective-permute-start = (bf16[88,128]{1,0:T(8,128)(2,1)S(1)}, bf16[88,128]{1,0:T(8,128)(2,1)S(1)}, u32[]{:S(2)}, u32[]{:S(2)}) collective-permute-start(bf16[88,128]{1,0:T(8,128)(2,1)S(1)} %get-tuple-element.16), channel_id=1, source_target_pairs={{0,4},{1,45},{2,71},{3,104},{4,130},{5,171},{6,197},{7,238},{8,264... | collective-permute-start | bytes 67592 | tf_op jit(solution)/shard_map/ppermute | solution.py:303
  13.4 25.4 %collective-permute-start.1 = (bf16[512,896]{1,0:T(8,128)(2,1)S(1)}, bf16[512,896]{1,0:T(8,128)(2,1)S(1)}, u32[]{:S(2)}, u32[]{:S(2)}) collective-permute-start(bf16[512,896]{1,0:T(8,128)(2,1)S(1)} %shard_map.86.refs_1_.refs_0_), channel_id=1, source_target_pairs={{0,16},{16,0},{1,17},{17,1},{2,18},{18,2},{3,19},{19,3},{4,20},{20... | collective-permute-start | bytes 2752520 | tf_op jit(solution)/shard_map/ppermute | solution.py:264
  16.2 9.0 %copy-start = (bf16[896,256]{1,0:T(8,128)(2,1)S(1)}, bf16[896,256]{1,0:T(8,128)(2,1)}, u32[]{:S(2)}) copy-start(bf16[896,256]{1,0:T(8,128)(2,1)} %refs_3_.1) | copy-start | bytes 1376260
  16.2 22.7 %all-to-all-start = ((bf16[16,88,128]{2,1,0:T(8,128)(2,1)}), bf16[16,88,128]{2,1,0:T(8,128)(2,1)S(1)}, u32[]{:S(2)}, u32[]{:S(2)}) async-start(bf16[16,88,128]{2,1,0:T(8,128)(2,1)} %shard_map.85), calls=%async_computation | async-start | bytes 720896 | tf_op jit(solution)/shard_map/all_to_all | solution.py:305
  25.1 3.7 %collective-permute-start.2 = (bf16[896,256]{1,0:T(8,128)(2,1)S(1)}, bf16[896,256]{1,0:T(8,128)(2,1)S(1)}, u32[]{:S(2)}, u32[]{:S(2)}) collective-permute-start(bf16[896,256]{1,0:T(8,128)(2,1)S(1)} %copy-done), channel_id=1, source_target_pairs={{0,16},{16,0},{1,17},{17,1},{2,18},{18,2},{3,19},{19,3},{4,20},{20... | collective-permute-start | bytes 1376264 | tf_op jit(solution)/shard_map/ppermute | solution.py:264
  40.7 28.5 %all-to-all-start.1 = ((bf16[16,240,128]{2,1,0:T(8,128)(2,1)}), bf16[16,240,128]{2,1,0:T(8,128)(2,1)S(1)}, u32[]{:S(2)}, u32[]{:S(2)}) async-start(bf16[16,240,128]{2,1,0:T(8,128)(2,1)} %get-tuple-element.18), calls=%async_computation.1 | async-start | bytes 1966080 | tf_op jit(solution)/shard_map/all_to_all | solution.py:330
  48.6 3.2 %copy-start.2 = (bf16[192,512]{1,0:T(8,128)(2,1)S(1)}, bf16[192,512]{1,0:T(8,128)(2,1)}, u32[]{:S(2)}) copy-start(bf16[192,512]{1,0:T(8,128)(2,1)} %get-tuple-element.22.refs_0_) | copy-start | bytes 589828
  49.9 29.6 %collective-permute-start.3 = (bf16[896,512]{1,0:T(8,128)(2,1)}, bf16[896,512]{1,0:T(8,128)(2,1)}, u32[]{:S(2)}, u32[]{:S(2)}) collective-permute-start(bf16[896,512]{1,0:T(8,128)(2,1)} %shard_map.89), channel_id=1, source_target_pairs={{0,32},{32,0},{1,33},{33,1},{2,34},{34,2},{3,35},{35,3},{4,36},{36... | collective-permute-start | bytes 2752520 | tf_op jit(solution)/shard_map/ppermute | solution.py:264
  51.9 23.1 %collective-permute-start.4 = (bf16[192,512]{1,0:T(8,128)(2,1)S(1)}, bf16[192,512]{1,0:T(8,128)(2,1)S(1)}, u32[]{:S(2)}, u32[]{:S(2)}) collective-permute-start(bf16[192,512]{1,0:T(8,128)(2,1)S(1)} %shard_map.90), channel_id=1, source_target_pairs={{0,16},{16,0},{1,17},{17,1},{2,18},{18,2},{3,19},{19,3},{4,20},{20... | collective-permute-start | bytes 589832 | tf_op jit(solution)/shard_map/ppermute | solution.py:264
  70.1 19.4 %all-to-all-start.2 = ((bf16[8,240,128]{2,1,0:T(8,128)(2,1)}), bf16[8,240,128]{2,1,0:T(8,128)(2,1)S(1)}, u32[]{:S(2)}, u32[]{:S(2)}) async-start(bf16[8,240,128]{2,1,0:T(8,128)(2,1)} %get-tuple-element.19), calls=%async_computation.2 | async-start | bytes 983040 | tf_op jit(solution)/shard_map/all_to_all | solution.py:336
  79.5 13.3 %collective-permute-start.5 = (bf16[896,512]{1,0:T(8,128)(2,1)}, bf16[896,512]{1,0:T(8,128)(2,1)}, u32[]{:S(2)}, u32[]{:S(2)}) collective-permute-start(bf16[896,512]{1,0:T(8,128)(2,1)} %shard_map.91.refs_3_), channel_id=1, source_target_pairs={{0,16},{16,0},{1,17},{17,1},{2,18},{18,2},{3,19},{19,3},{4,20},{20... | collective-permute-start | bytes 2752520 | tf_op jit(solution)/shard_map/ppermute | solution.py:264
  89.6 13.9 %collective-permute-start.8 = (bf16[8,240,128]{2,1,0:T(8,128)(2,1)S(1)}, bf16[8,240,128]{2,1,0:T(8,128)(2,1)S(1)}, u32[]{:S(2)}, u32[]{:S(2)}) collective-permute-start(bf16[8,240,128]{2,1,0:T(8,128)(2,1)S(1)} %all-to-all-done.2.refs_0_.refs_2_), channel_id=1, source_target_pairs={{0,32},{32,0},{1,33},{33,1},{2,34},{34,2},{3,35},{35,3},{4,36},{36... | collective-permute-start | bytes 1474568 | tf_op jit(solution)/shard_map/ppermute | solution.py:264
  96.0 14.5 %all-to-all-start.3 = ((bf16[16,48,128]{2,1,0:T(8,128)(2,1)}), bf16[16,48,128]{2,1,0:T(8,128)(2,1)S(1)}, u32[]{:S(2)}, u32[]{:S(2)}) async-start(bf16[16,48,128]{2,1,0:T(8,128)(2,1)} %shard_map.92), calls=%async_computation.3 | async-start | bytes 393216 | tf_op jit(solution)/shard_map/all_to_all | solution.py:353
  101.3 12.3 %copy-start.1 = (bf16[192,512]{1,0:T(8,128)(2,1)S(1)}, bf16[192,512]{1,0:T(8,128)(2,1)}, u32[]{:S(2)}) copy-start(bf16[192,512]{1,0:T(8,128)(2,1)} %get-tuple-element.23.refs_0_) | copy-start | bytes 589828
  101.3 12.2 %collective-permute-start.7 = (bf16[8,240,128]{2,1,0:T(8,128)(2,1)S(1)}, bf16[8,240,128]{2,1,0:T(8,128)(2,1)S(1)}, u32[]{:S(2)}, u32[]{:S(2)}) collective-permute-start(bf16[8,240,128]{2,1,0:T(8,128)(2,1)S(1)} %all-to-all-done.2.refs_0_.refs_2_), channel_id=1, source_target_pairs={{0,16},{16,0},{1,17},{17,1},{2,18},{18,2},{3,19},{19,3},{4,20},{20... | collective-permute-start | bytes 1474568 | tf_op jit(solution)/shard_map/ppermute | solution.py:264
  103.4 10.2 %collective-permute-start.9 = (bf16[8,240,128]{2,1,0:T(8,128)(2,1)S(1)}, bf16[8,240,128]{2,1,0:T(8,128)(2,1)S(1)}, u32[]{:S(2)}, u32[]{:S(2)}) collective-permute-start(bf16[8,240,128]{2,1,0:T(8,128)(2,1)S(1)} %collective-permute-done.8.refs_4_), channel_id=1, source_target_pairs={{0,16},{16,0},{1,17},{17,1},{2,18},{18,2},{3,19},{19,3},{4,20},{20... | collective-permute-start | bytes 1474568 | tf_op jit(solution)/shard_map/ppermute | solution.py:264
  110.5 10.4 %collective-permute-start.6 = (bf16[11,512]{1,0:T(8,128)(2,1)S(1)}, bf16[11,512]{1,0:T(8,128)(2,1)S(1)}, u32[]{:S(2)}, u32[]{:S(2)}) collective-permute-start(bf16[11,512]{1,0:T(8,128)(2,1)S(1)} %shard_map.93), channel_id=1, source_target_pairs={{4,0},{13,1},{71,2},{72,3},{130,4},{139,5},{197,6},{206,7},{264,8}... | collective-permute-start | bytes 33800 | tf_op jit(solution)/shard_map/ppermute | solution.py:366

commit v9 on v8

--- a/solution.py
+++ b/solution.py
@@ -67,8 +67,7 @@
     return core, xh, lax.rem(base + xh, 8), lax.rem(base + 1 - xh, 8), z // 4
 
 
-def pack_kernel(tok_hbm, cot_hbm, out, wide, tok, cot, sems):
-    fetch(sems, (tok_hbm, tok), (cot_hbm, cot))
+def pack_kernel(tok, cot, out, wide):
     odd = here()[0] == 1
     for base, ref in ((0, tok), (4, cot)):
         rows = ref[...].astype(F32)
@@ -291,14 +290,8 @@
     packed, ready0 = call(
         pack_kernel,
         (shape(88, 128),),
-        (in_hbm(tokens), in_hbm(cotangent)),
-        [
-            pltpu.VMEM((96, 128), F32),
-            pltpu.VMEM((ROWS, 512), BF16),
-            pltpu.VMEM((ROWS, 512), BF16),
-            pltpu.SemaphoreType.DMA((2,)),
-        ],
-        specs=[HBM, HBM],
+        (tokens, cotangent),
+        [pltpu.VMEM((96, 128), F32)],
     )
     packed = lax.ppermute(packed, ALL, there)
     (spread,) = call(spread_kernel, (shape(16, 88, 128),), (packed,), flops=10**11, token=False)

time: 124 us -> 125 us (level)
  local copies, waits for them, and re-layouts: 0.01 us -> 1.44 us
    unnamed x6 -> x10, local copies, waits for them, and re-layouts: 0.01 us -> 1.44 us
where the time goes in v9:
time: 125 us; the launch traced here: 122 us
  starting transfers between devices  58.5 us (47%)
  waiting for transfers between devices  49.8 us (40%)
  Pallas kernels  11.7 us (9%)
  local copies, waits for them, and re-layouts  1.44 us (1%)
    ppermute x8, starting transfers between devices, swap(): return lax.ppermute(x, axis, [(0, 1), (1, 0)])  17.3 us
    all_to_all x1, waiting for transfers between devices, per_device(): parts = lax.all_to_all(parts, ('xh', 'z'), 0, 0, tiled=True)  15.4 us
    pallas_call x11, Pallas kernels, call(): pl.pallas_call(body, out_shape=(*out_shape, *[shape(8, 128, dtype=F32)] *...  11.7 us
    ppermute x1, starting transfers between devices, per_device(): packed = lax.ppermute(packed, ALL, there)  10.8 us
    all_to_all x1, waiting for transfers between devices, per_device(): rows = lax.all_to_all(spread, AROUND, 0, 0, tiled=True)  10 us
    all_to_all x1, starting transfers between devices, per_device(): rows = lax.all_to_all(spread, AROUND, 0, 0, tiled=True)  8.95 us
    all_to_all x1, waiting for transfers between devices, per_device(): acts0 = lax.all_to_all(acts0, 'z', 0, 0, tiled=True)  8.15 us
    all_to_all x1, starting transfers between devices, per_device(): parts = lax.all_to_all(parts, ('xh', 'z'), 0, 0, tiled=True)  7.96 us
  transfers between devices with their start and end apart: 14, of which 7 were waited for; matrix products, arithmetic and copies ran while one was open for 0% of the time, Pallas kernels for 8%

profile of v9, /device:TPU:6, one launch (start us, length us, event | category | flops | bytes accessed | tf_op | source)
XLA Modules:
  0.0 122.2 jit_solution(10301014926772823139)
XLA Ops:
  2.1 10.8 %collective-permute-start = (bf16[88,128]{1,0:T(8,128)(2,1)S(1)}, bf16[88,128]{1,0:T(8,128)(2,1)S(1)}, u32[]{:S(2)}, u32[]{:S(2)}) collective-permute-start(bf16[88,128]{1,0:T(8,128)(2,1)S(1)} %get-tuple-element.16), channel_id=1, source_target_pairs={{0,4},{1,45},{2,71},{3,104},{4,130},{5,171},{6,197},{7,238},{8,264... | collective-permute-start | bytes 67592 | tf_op jit(solution)/shard_map/ppermute | solution.py:296
  14.1 1.9 %collective-permute-start.1 = (bf16[512,896]{1,0:T(8,128)(2,1)S(1)}, bf16[512,896]{1,0:T(8,128)(2,1)S(1)}, u32[]{:S(2)}, u32[]{:S(2)}) collective-permute-start(bf16[512,896]{1,0:T(8,128)(2,1)S(1)} %shard_map.86.refs_1_.refs_0_), channel_id=1, source_target_pairs={{0,16},{16,0},{1,17},{17,1},{2,18},{18,2},{3,19},{19,3},{4,20},{20... | collective-permute-start | bytes 2752520 | tf_op jit(solution)/shard_map/ppermute | solution.py:263
  16.8 9.0 %all-to-all-start = ((bf16[16,88,128]{2,1,0:T(8,128)(2,1)}), bf16[16,88,128]{2,1,0:T(8,128)(2,1)S(1)}, u32[]{:S(2)}, u32[]{:S(2)}) async-start(bf16[16,88,128]{2,1,0:T(8,128)(2,1)} %shard_map.85), calls=%async_computation | async-start | bytes 720896 | tf_op jit(solution)/shard_map/all_to_all | solution.py:298
  25.8 1.9 %collective-permute-start.2 = (bf16[896,256]{1,0:T(8,128)(2,1)S(1)}, bf16[896,256]{1,0:T(8,128)(2,1)S(1)}, u32[]{:S(2)}, u32[]{:S(2)}) collective-permute-start(bf16[896,256]{1,0:T(8,128)(2,1)S(1)} %copy-done), channel_id=1, source_target_pairs={{0,16},{16,0},{1,17},{17,1},{2,18},{18,2},{3,19},{19,3},{4,20},{20... | collective-permute-start | bytes 1376264 | tf_op jit(solution)/shard_map/ppermute | solution.py:263
  27.7 1.8 %collective-permute-done.2.refs_4_ = bf16[896,256]{1,0:T(8,128)(2,1)S(1)} collective-permute-done((bf16[896,256]{1,0:T(8,128)(2,1)S(1)}, bf16[896,256]{1,0:T(8,128)(2,1)S(1)}, u32[]{:S(2)}, u32[]{:S(2)}) %collective-permute-start.2) | collective-permute-done | bytes 458784 | tf_op jit(solution)/shard_map/ppermute | solution.py:263
  29.5 10.0 %all-to-all-done.refs_0_ = bf16[16,88,128]{2,1,0:T(8,128)(2,1)S(1)} async-done(((bf16[16,88,128]{2,1,0:T(8,128)(2,1)}), bf16[16,88,128]{2,1,0:T(8,128)(2,1)S(1)}, u32[]{:S(2)}, u32[]{:S(2)}) %all-to-all-start) | async-done | bytes 360480 | tf_op jit(solution)/shard_map/all_to_all | solution.py:298
  39.5 1.8 %shard_map.87 = (bf16[16,240,128]{2,1,0:T(8,128)(2,1)}, bf16[192,512]{1,0:T(8,128)(2,1)}, bf16[192,512]{1,0:T(8,128)(2,1)}, f32[8,128]{1,0:T(8,128)S(1)}) custom-call(bf16[16,88,128]{2,1,0:T(8,128)(2,1)S(1)} %all-to-all-done.refs_0_, bf16[512,896]{1,0:T(8,128)(2,1)S(1)} %shard_map.86.refs_1_.refs_0_, bf16[512,896]{1,0:T(8,128)(2,1)S(1)} %collective-permute-done.1.refs_2_, ...), custom_call_target="tpu_custom_call" | custom-call | bytes 4489216 | tf_op jit(solution)/shard_map/pallas_call | solution.py:37
  41.3 8.0 %all-to-all-start.1 = ((bf16[16,240,128]{2,1,0:T(8,128)(2,1)}), bf16[16,240,128]{2,1,0:T(8,128)(2,1)S(1)}, u32[]{:S(2)}, u32[]{:S(2)}) async-start(bf16[16,240,128]{2,1,0:T(8,128)(2,1)} %get-tuple-element.18), calls=%async_computation.1 | async-start | bytes 1966080 | tf_op jit(solution)/shard_map/all_to_all | solution.py:323
  50.5 2.0 %collective-permute-start.3 = (bf16[896,512]{1,0:T(8,128)(2,1)}, bf16[896,512]{1,0:T(8,128)(2,1)}, u32[]{:S(2)}, u32[]{:S(2)}) collective-permute-start(bf16[896,512]{1,0:T(8,128)(2,1)} %shard_map.89), channel_id=1, source_target_pairs={{0,32},{32,0},{1,33},{33,1},{2,34},{34,2},{3,35},{35,3},{4,36},{36... | collective-permute-start | bytes 2752520 | tf_op jit(solution)/shard_map/ppermute | solution.py:263
  52.6 1.9 %collective-permute-start.4 = (bf16[192,512]{1,0:T(8,128)(2,1)S(1)}, bf16[192,512]{1,0:T(8,128)(2,1)S(1)}, u32[]{:S(2)}, u32[]{:S(2)}) collective-permute-start(bf16[192,512]{1,0:T(8,128)(2,1)S(1)} %shard_map.90), channel_id=1, source_target_pairs={{0,16},{16,0},{1,17},{17,1},{2,18},{18,2},{3,19},{19,3},{4,20},{20... | collective-permute-start | bytes 589832 | tf_op jit(solution)/shard_map/ppermute | solution.py:263
  54.5 15.4 %all-to-all-done.1.refs_0_ = bf16[16,240,128]{2,1,0:T(8,128)(2,1)S(1)} async-done(((bf16[16,240,128]{2,1,0:T(8,128)(2,1)}), bf16[16,240,128]{2,1,0:T(8,128)(2,1)S(1)}, u32[]{:S(2)}, u32[]{:S(2)}) %all-to-all-start.1) | async-done | bytes 983072 | tf_op jit(solution)/shard_map/all_to_all | solution.py:323
  70.8 4.9 %all-to-all-start.2 = ((bf16[8,240,128]{2,1,0:T(8,128)(2,1)}), bf16[8,240,128]{2,1,0:T(8,128)(2,1)S(1)}, u32[]{:S(2)}, u32[]{:S(2)}) async-start(bf16[8,240,128]{2,1,0:T(8,128)(2,1)} %get-tuple-element.19), calls=%async_computation.2 | async-start | bytes 983040 | tf_op jit(solution)/shard_map/all_to_all | solution.py:329
  75.7 4.5 %collective-permute-done.3.refs_0_ = bf16[896,512]{1,0:T(8,128)(2,1)} collective-permute-done((bf16[896,512]{1,0:T(8,128)(2,1)}, bf16[896,512]{1,0:T(8,128)(2,1)}, u32[]{:S(2)}, u32[]{:S(2)}) %collective-permute-start.3) | collective-permute-done | bytes 917536 | tf_op jit(solution)/shard_map/ppermute | solution.py:263
  80.1 1.9 %collective-permute-start.5 = (bf16[896,512]{1,0:T(8,128)(2,1)}, bf16[896,512]{1,0:T(8,128)(2,1)}, u32[]{:S(2)}, u32[]{:S(2)}) collective-permute-start(bf16[896,512]{1,0:T(8,128)(2,1)} %shard_map.91.refs_3_), channel_id=1, source_target_pairs={{0,16},{16,0},{1,17},{17,1},{2,18},{18,2},{3,19},{19,3},{4,20},{20... | collective-permute-start | bytes 2752520 | tf_op jit(solution)/shard_map/ppermute | solution.py:263
  82.1 8.1 %all-to-all-done.2.refs_0_.refs_2_ = bf16[8,240,128]{2,1,0:T(8,128)(2,1)S(1)} async-done(((bf16[8,240,128]{2,1,0:T(8,128)(2,1)}), bf16[8,240,128]{2,1,0:T(8,128)(2,1)S(1)}, u32[]{:S(2)}, u32[]{:S(2)}) %all-to-all-start.2) | async-done | bytes 491552 | tf_op jit(solution)/shard_map/all_to_all | solution.py:329
  90.2 3.2 %collective-permute-start.8 = (bf16[8,240,128]{2,1,0:T(8,128)(2,1)S(1)}, bf16[8,240,128]{2,1,0:T(8,128)(2,1)S(1)}, u32[]{:S(2)}, u32[]{:S(2)}) collective-permute-start(bf16[8,240,128]{2,1,0:T(8,128)(2,1)S(1)} %all-to-all-done.2.refs_0_.refs_2_), channel_id=1, source_target_pairs={{0,32},{32,0},{1,33},{33,1},{2,34},{34,2},{3,35},{35,3},{4,36},{36... | collective-permute-start | bytes 1474568 | tf_op jit(solution)/shard_map/ppermute | solution.py:263
  93.4 3.2 %shard_map.92 = bf16[16,48,128]{2,1,0:T(8,128)(2,1)} custom-call(bf16[8,240,128]{2,1,0:T(8,128)(2,1)S(1)} %all-to-all-done.2.refs_0_.refs_2_, bf16[512,896]{1,0:T(8,128)(2,1)S(1)} %shard_map.86.refs_1_.refs_0_, bf16[512,896]{1,0:T(8,128)(2,1)S(1)} %collective-permute-done.1.refs_2_, bf16[896,512]{1,0:T(8,128)(2,1)} %shard_map.91.refs_3_, ...), custom_call_target="tpu_custom_call" | custom-call | bytes 4358144 | tf_op jit(solution)/shard_map/pallas_call | solution.py:37
  96.6 5.4 %all-to-all-start.3 = ((bf16[16,48,128]{2,1,0:T(8,128)(2,1)}), bf16[16,48,128]{2,1,0:T(8,128)(2,1)S(1)}, u32[]{:S(2)}, u32[]{:S(2)}) async-start(bf16[16,48,128]{2,1,0:T(8,128)(2,1)} %shard_map.92), calls=%async_computation.3 | async-start | bytes 393216 | tf_op jit(solution)/shard_map/all_to_all | solution.py:346
  102.0 2.1 %collective-permute-start.7 = (bf16[8,240,128]{2,1,0:T(8,128)(2,1)S(1)}, bf16[8,240,128]{2,1,0:T(8,128)(2,1)S(1)}, u32[]{:S(2)}, u32[]{:S(2)}) collective-permute-start(bf16[8,240,128]{2,1,0:T(8,128)(2,1)S(1)} %all-to-all-done.2.refs_0_.refs_2_), channel_id=1, source_target_pairs={{0,16},{16,0},{1,17},{17,1},{2,18},{18,2},{3,19},{19,3},{4,20},{20... | collective-permute-start | bytes 1474568 | tf_op jit(solution)/shard_map/ppermute | solution.py:263
  104.1 2.4 %collective-permute-start.9 = (bf16[8,240,128]{2,1,0:T(8,128)(2,1)S(1)}, bf16[8,240,128]{2,1,0:T(8,128)(2,1)S(1)}, u32[]{:S(2)}, u32[]{:S(2)}) collective-permute-start(bf16[8,240,128]{2,1,0:T(8,128)(2,1)S(1)} %collective-permute-done.8.refs_4_), channel_id=1, source_target_pairs={{0,16},{16,0},{1,17},{17,1},{2,18},{18,2},{3,19},{19,3},{4,20},{20... | collective-permute-start | bytes 1474568 | tf_op jit(solution)/shard_map/ppermute | solution.py:263
  106.5 4.6 %all-to-all-done.3.refs_0_ = bf16[16,48,128]{2,1,0:T(8,128)(2,1)S(1)} async-done(((bf16[16,48,128]{2,1,0:T(8,128)(2,1)}), bf16[16,48,128]{2,1,0:T(8,128)(2,1)S(1)}, u32[]{:S(2)}, u32[]{:S(2)}) %all-to-all-start.3) | async-done | bytes 196640 | tf_op jit(solution)/shard_map/all_to_all | solution.py:346
  111.1 3.1 %collective-permute-start.6 = (bf16[11,512]{1,0:T(8,128)(2,1)S(1)}, bf16[11,512]{1,0:T(8,128)(2,1)S(1)}, u32[]{:S(2)}, u32[]{:S(2)}) collective-permute-start(bf16[11,512]{1,0:T(8,128)(2,1)S(1)} %shard_map.93), channel_id=1, source_target_pairs={{4,0},{13,1},{71,2},{72,3},{130,4},{139,5},{197,6},{206,7},{264,8}... | collective-permute-start | bytes 33800 | tf_op jit(solution)/shard_map/ppermute | solution.py:359
  114.3 1.9 %shard_map.94 = (bf16[256,896]{1,0:T(8,128)(2,1)}, bf16[256,896]{1,0:T(8,128)(2,1)}, bf16[896,256]{1,0:T(8,128)(2,1)}, f32[8,128]{1,0:T(8,128)S(1)}) custom-call(bf16[192,512]{1,0:T(8,128)(2,1)S(1)} %copy-done.1, bf16[192,512]{1,0:T(8,128)(2,1)S(1)} %collective-permute-done.4.refs_2_.refs_1_, bf16[8,240,128]{2,1,0:T(8,128)(2,1)S(1)} %all-to-all-done.2.refs_0_.refs_2_, ...), custom_call_target="tpu_custom_call" | custom-call | bytes 3735552 | tf_op jit(solution)/shard_map/pallas_call | solution.py:37
  116.2 5.4 %collective-permute-done.6.refs_0_ = bf16[11,512]{1,0:T(8,128)(2,1)S(1)} collective-permute-done((bf16[11,512]{1,0:T(8,128)(2,1)S(1)}, bf16[11,512]{1,0:T(8,128)(2,1)S(1)}, u32[]{:S(2)}, u32[]{:S(2)}) %collective-permute-start.6) | collective-permute-done | bytes 11296 | tf_op jit(solution)/shard_map/ppermute | solution.py:359
  (26 shorter events, 6.3 us)
Async XLA Ops:
  0.6 0.7 copy-start.3
  1.3 0.7 copy-start.4
  2.1 14.0 %collective-permute-start = (bf16[88,128]{1,0:T(8,128)(2,1)S(1)}, bf16[88,128]{1,0:T(8,128)(2,1)S(1)}, u32[]{:S(2)}, u32[]{:S(2)}) collective-permute-start(bf16[88,128]{1,0:T(8,128)(2,1)S(1)} %get-tuple-element.16), channel_id=1, source_target_pairs={{0,4},{1,45},{2,71},{3,104},{4,130},{5,171},{6,197},{7,238},{8,264... | collective-permute-start | bytes 67592 | tf_op jit(solution)/shard_map/ppermute | solution.py:296
  14.1 25.4 %collective-permute-start.1 = (bf16[512,896]{1,0:T(8,128)(2,1)S(1)}, bf16[512,896]{1,0:T(8,128)(2,1)S(1)}, u32[]{:S(2)}, u32[]{:S(2)}) collective-permute-start(bf16[512,896]{1,0:T(8,128)(2,1)S(1)} %shard_map.86.refs_1_.refs_0_), channel_id=1, source_target_pairs={{0,16},{16,0},{1,17},{17,1},{2,18},{18,2},{3,19},{19,3},{4,20},{20... | collective-permute-start | bytes 2752520 | tf_op jit(solution)/shard_map/ppermute | solution.py:263
  16.8 9.0 %copy-start = (bf16[896,256]{1,0:T(8,128)(2,1)S(1)}, bf16[896,256]{1,0:T(8,128)(2,1)}, u32[]{:S(2)}) copy-start(bf16[896,256]{1,0:T(8,128)(2,1)} %refs_3_.1) | copy-start | bytes 1376260
  16.8 22.7 %all-to-all-start = ((bf16[16,88,128]{2,1,0:T(8,128)(2,1)}), bf16[16,88,128]{2,1,0:T(8,128)(2,1)S(1)}, u32[]{:S(2)}, u32[]{:S(2)}) async-start(bf16[16,88,128]{2,1,0:T(8,128)(2,1)} %shard_map.85), calls=%async_computation | async-start | bytes 720896 | tf_op jit(solution)/shard_map/all_to_all | solution.py:298
  25.8 3.7 %collective-permute-start.2 = (bf16[896,256]{1,0:T(8,128)(2,1)S(1)}, bf16[896,256]{1,0:T(8,128)(2,1)S(1)}, u32[]{:S(2)}, u32[]{:S(2)}) collective-permute-start(bf16[896,256]{1,0:T(8,128)(2,1)S(1)} %copy-done), channel_id=1, source_target_pairs={{0,16},{16,0},{1,17},{17,1},{2,18},{18,2},{3,19},{19,3},{4,20},{20... | collective-permute-start | bytes 1376264 | tf_op jit(solution)/shard_map/ppermute | solution.py:263
  41.3 28.5 %all-to-all-start.1 = ((bf16[16,240,128]{2,1,0:T(8,128)(2,1)}), bf16[16,240,128]{2,1,0:T(8,128)(2,1)S(1)}, u32[]{:S(2)}, u32[]{:S(2)}) async-start(bf16[16,240,128]{2,1,0:T(8,128)(2,1)} %get-tuple-element.18), calls=%async_computation.1 | async-start | bytes 1966080 | tf_op jit(solution)/shard_map/all_to_all | solution.py:323
  49.3 3.3 %copy-start.2 = (bf16[192,512]{1,0:T(8,128)(2,1)S(1)}, bf16[192,512]{1,0:T(8,128)(2,1)}, u32[]{:S(2)}) copy-start(bf16[192,512]{1,0:T(8,128)(2,1)} %get-tuple-element.22.refs_0_) | copy-start | bytes 589828
  50.5 29.6 %collective-permute-start.3 = (bf16[896,512]{1,0:T(8,128)(2,1)}, bf16[896,512]{1,0:T(8,128)(2,1)}, u32[]{:S(2)}, u32[]{:S(2)}) collective-permute-start(bf16[896,512]{1,0:T(8,128)(2,1)} %shard_map.89), channel_id=1, source_target_pairs={{0,32},{32,0},{1,33},{33,1},{2,34},{34,2},{3,35},{35,3},{4,36},{36... | collective-permute-start | bytes 2752520 | tf_op jit(solution)/shard_map/ppermute | solution.py:263
  52.6 23.1 %collective-permute-start.4 = (bf16[192,512]{1,0:T(8,128)(2,1)S(1)}, bf16[192,512]{1,0:T(8,128)(2,1)S(1)}, u32[]{:S(2)}, u32[]{:S(2)}) collective-permute-start(bf16[192,512]{1,0:T(8,128)(2,1)S(1)} %shard_map.90), channel_id=1, source_target_pairs={{0,16},{16,0},{1,17},{17,1},{2,18},{18,2},{3,19},{19,3},{4,20},{20... | collective-permute-start | bytes 589832 | tf_op jit(solution)/shard_map/ppermute | solution.py:263
  70.8 19.4 %all-to-all-start.2 = ((bf16[8,240,128]{2,1,0:T(8,128)(2,1)}), bf16[8,240,128]{2,1,0:T(8,128)(2,1)S(1)}, u32[]{:S(2)}, u32[]{:S(2)}) async-start(bf16[8,240,128]{2,1,0:T(8,128)(2,1)} %get-tuple-element.19), calls=%async_computation.2 | async-start | bytes 983040 | tf_op jit(solution)/shard_map/all_to_all | solution.py:329
  80.1 13.3 %collective-permute-start.5 = (bf16[896,512]{1,0:T(8,128)(2,1)}, bf16[896,512]{1,0:T(8,128)(2,1)}, u32[]{:S(2)}, u32[]{:S(2)}) collective-permute-start(bf16[896,512]{1,0:T(8,128)(2,1)} %shard_map.91.refs_3_), channel_id=1, source_target_pairs={{0,16},{16,0},{1,17},{17,1},{2,18},{18,2},{3,19},{19,3},{4,20},{20... | collective-permute-start | bytes 2752520 | tf_op jit(solution)/shard_map/ppermute | solution.py:263
  90.2 13.9 %collective-permute-start.8 = (bf16[8,240,128]{2,1,0:T(8,128)(2,1)S(1)}, bf16[8,240,128]{2,1,0:T(8,128)(2,1)S(1)}, u32[]{:S(2)}, u32[]{:S(2)}) collective-permute-start(bf16[8,240,128]{2,1,0:T(8,128)(2,1)S(1)} %all-to-all-done.2.refs_0_.refs_2_), channel_id=1, source_target_pairs={{0,32},{32,0},{1,33},{33,1},{2,34},{34,2},{3,35},{35,3},{4,36},{36... | collective-permute-start | bytes 1474568 | tf_op jit(solution)/shard_map/ppermute | solution.py:263
  96.6 14.5 %all-to-all-start.3 = ((bf16[16,48,128]{2,1,0:T(8,128)(2,1)}), bf16[16,48,128]{2,1,0:T(8,128)(2,1)S(1)}, u32[]{:S(2)}, u32[]{:S(2)}) async-start(bf16[16,48,128]{2,1,0:T(8,128)(2,1)} %shard_map.92), calls=%async_computation.3 | async-start | bytes 393216 | tf_op jit(solution)/shard_map/all_to_all | solution.py:346
  102.0 12.3 %copy-start.1 = (bf16[192,512]{1,0:T(8,128)(2,1)S(1)}, bf16[192,512]{1,0:T(8,128)(2,1)}, u32[]{:S(2)}) copy-start(bf16[192,512]{1,0:T(8,128)(2,1)} %get-tuple-element.23.refs_0_) | copy-start | bytes 589828
  102.0 12.2 %collective-permute-start.7 = (bf16[8,240,128]{2,1,0:T(8,128)(2,1)S(1)}, bf16[8,240,128]{2,1,0:T(8,128)(2,1)S(1)}, u32[]{:S(2)}, u32[]{:S(2)}) collective-permute-start(bf16[8,240,128]{2,1,0:T(8,128)(2,1)S(1)} %all-to-all-done.2.refs_0_.refs_2_), channel_id=1, source_target_pairs={{0,16},{16,0},{1,17},{17,1},{2,18},{18,2},{3,19},{19,3},{4,20},{20... | collective-permute-start | bytes 1474568 | tf_op jit(solution)/shard_map/ppermute | solution.py:263
  104.1 10.2 %collective-permute-start.9 = (bf16[8,240,128]{2,1,0:T(8,128)(2,1)S(1)}, bf16[8,240,128]{2,1,0:T(8,128)(2,1)S(1)}, u32[]{:S(2)}, u32[]{:S(2)}) collective-permute-start(bf16[8,240,128]{2,1,0:T(8,128)(2,1)S(1)} %collective-permute-done.8.refs_4_), channel_id=1, source_target_pairs={{0,16},{16,0},{1,17},{17,1},{2,18},{18,2},{3,19},{19,3},{4,20},{20... | collective-permute-start | bytes 1474568 | tf_op jit(solution)/shard_map/ppermute | solution.py:263
  111.1 10.4 %collective-permute-start.6 = (bf16[11,512]{1,0:T(8,128)(2,1)S(1)}, bf16[11,512]{1,0:T(8,128)(2,1)S(1)}, u32[]{:S(2)}, u32[]{:S(2)}) collective-permute-start(bf16[11,512]{1,0:T(8,128)(2,1)S(1)} %shard_map.93), channel_id=1, source_target_pairs={{4,0},{13,1},{71,2},{72,3},{130,4},{139,5},{197,6},{206,7},{264,8}... | collective-permute-start | bytes 33800 | tf_op jit(solution)/shard_map/ppermute | solution.py:359

commit v10 on v9

--- a/solution.py
+++ b/solution.py
@@ -67,10 +67,10 @@
     return core, xh, lax.rem(base + xh, 8), lax.rem(base + 1 - xh, 8), z // 4
 
 
-def pack_kernel(tok, cot, out, wide):
+def pack_kernel(both, out, wide):
     odd = here()[0] == 1
-    for base, ref in ((0, tok), (4, cot)):
-        rows = ref[...].astype(F32)
+    for base in (0, 4):
+        rows = both[:, base * 128 : (base + 4) * 128].astype(F32)
         for j in range(4):
             piece = jnp.where(odd, tile(rows, (j + 2) % 4), tile(rows, j))
             wide[pl.ds(base + j, ROWS, stride=8), :] = piece
@@ -290,7 +290,7 @@
     packed, ready0 = call(
         pack_kernel,
         (shape(88, 128),),
-        (tokens, cotangent),
+        (jnp.concatenate([tokens, cotangent], axis=1),),
         [pltpu.VMEM((96, 128), F32)],
     )
     packed = lax.ppermute(packed, ALL, there)

time: 125 us -> 124 us (level)
  local copies, waits for them, and re-layouts: 1.44 us -> 0.01 us
    unnamed x10 -> x6, local copies, waits for them, and re-layouts: 1.44 us -> 0.01 us
where the time goes in v10:
time: 124 us; the launch traced here: 122 us
  starting transfers between devices  58.5 us (47%)
  waiting for transfers between devices  49.8 us (40%)
  Pallas kernels  11.7 us (9%)
    ppermute x8, starting transfers between devices, swap(): return lax.ppermute(x, axis, [(0, 1), (1, 0)])  17.3 us
    all_to_all x1, waiting for transfers between devices, per_device(): parts = lax.all_to_all(parts, ('xh', 'z'), 0, 0, tiled=True)  15.4 us
    pallas_call x11, Pallas kernels, call(): pl.pallas_call(body, out_shape=(*out_shape, *[shape(8, 128, dtype=F32)] *...  11.7 us
    ppermute x1, starting transfers between devices, per_device(): packed = lax.ppermute(packed, ALL, there)  10.8 us
    all_to_all x1, waiting for transfers between devices, per_device(): rows = lax.all_to_all(spread, AROUND, 0, 0, tiled=True)  10 us
    all_to_all x1, starting transfers between devices, per_device(): rows = lax.all_to_all(spread, AROUND, 0, 0, tiled=True)  8.95 us
    all_to_all x1, waiting for transfers between devices, per_device(): acts0 = lax.all_to_all(acts0, 'z', 0, 0, tiled=True)  8.17 us
    all_to_all x1, starting transfers between devices, per_device(): parts = lax.all_to_all(parts, ('xh', 'z'), 0, 0, tiled=True)  7.96 us
  transfers between devices with their start and end apart: 14, of which 7 were waited for; matrix products, arithmetic and copies ran while one was open for 0% of the time, Pallas kernels for 8%

profile of v10, /device:TPU:6, one launch (start us, length us, event | category | flops | bytes accessed | tf_op | source)
XLA Modules:
  0.0 121.5 jit_solution(5644807559054035963)
XLA Ops:
  1.4 10.8 %collective-permute-start = (bf16[88,128]{1,0:T(8,128)(2,1)S(1)}, bf16[88,128]{1,0:T(8,128)(2,1)S(1)}, u32[]{:S(2)}, u32[]{:S(2)}) collective-permute-start(bf16[88,128]{1,0:T(8,128)(2,1)S(1)} %get-tuple-element.16), channel_id=1, source_target_pairs={{0,4},{1,45},{2,71},{3,104},{4,130},{5,171},{6,197},{7,238},{8,264... | collective-permute-start | bytes 67592 | tf_op jit(solution)/shard_map/ppermute | solution.py:296
  13.4 1.9 %collective-permute-start.1 = (bf16[512,896]{1,0:T(8,128)(2,1)S(1)}, bf16[512,896]{1,0:T(8,128)(2,1)S(1)}, u32[]{:S(2)}, u32[]{:S(2)}) collective-permute-start(bf16[512,896]{1,0:T(8,128)(2,1)S(1)} %shard_map.86.refs_1_.refs_0_), channel_id=1, source_target_pairs={{0,16},{16,0},{1,17},{17,1},{2,18},{18,2},{3,19},{19,3},{4,20},{20... | collective-permute-start | bytes 2752520 | tf_op jit(solution)/shard_map/ppermute | solution.py:263
  16.2 9.0 %all-to-all-start = ((bf16[16,88,128]{2,1,0:T(8,128)(2,1)}), bf16[16,88,128]{2,1,0:T(8,128)(2,1)S(1)}, u32[]{:S(2)}, u32[]{:S(2)}) async-start(bf16[16,88,128]{2,1,0:T(8,128)(2,1)} %shard_map.85), calls=%async_computation | async-start | bytes 720896 | tf_op jit(solution)/shard_map/all_to_all | solution.py:298
  25.1 1.9 %collective-permute-start.2 = (bf16[896,256]{1,0:T(8,128)(2,1)S(1)}, bf16[896,256]{1,0:T(8,128)(2,1)S(1)}, u32[]{:S(2)}, u32[]{:S(2)}) collective-permute-start(bf16[896,256]{1,0:T(8,128)(2,1)S(1)} %copy-done), channel_id=1, source_target_pairs={{0,16},{16,0},{1,17},{17,1},{2,18},{18,2},{3,19},{19,3},{4,20},{20... | collective-permute-start | bytes 1376264 | tf_op jit(solution)/shard_map/ppermute | solution.py:263
  27.0 1.8 %collective-permute-done.2.refs_4_ = bf16[896,256]{1,0:T(8,128)(2,1)S(1)} collective-permute-done((bf16[896,256]{1,0:T(8,128)(2,1)S(1)}, bf16[896,256]{1,0:T(8,128)(2,1)S(1)}, u32[]{:S(2)}, u32[]{:S(2)}) %collective-permute-start.2) | collective-permute-done | bytes 458784 | tf_op jit(solution)/shard_map/ppermute | solution.py:263
  28.8 10.0 %all-to-all-done.refs_0_ = bf16[16,88,128]{2,1,0:T(8,128)(2,1)S(1)} async-done(((bf16[16,88,128]{2,1,0:T(8,128)(2,1)}), bf16[16,88,128]{2,1,0:T(8,128)(2,1)S(1)}, u32[]{:S(2)}, u32[]{:S(2)}) %all-to-all-start) | async-done | bytes 360480 | tf_op jit(solution)/shard_map/all_to_all | solution.py:298
  38.8 1.8 %shard_map.87 = (bf16[16,240,128]{2,1,0:T(8,128)(2,1)}, bf16[192,512]{1,0:T(8,128)(2,1)}, bf16[192,512]{1,0:T(8,128)(2,1)}, f32[8,128]{1,0:T(8,128)S(1)}) custom-call(bf16[16,88,128]{2,1,0:T(8,128)(2,1)S(1)} %all-to-all-done.refs_0_, bf16[512,896]{1,0:T(8,128)(2,1)S(1)} %shard_map.86.refs_1_.refs_0_, bf16[512,896]{1,0:T(8,128)(2,1)S(1)} %collective-permute-done.1.refs_2_, ...), custom_call_target="tpu_custom_call" | custom-call | bytes 4489216 | tf_op jit(solution)/shard_map/pallas_call | solution.py:37
  40.7 8.0 %all-to-all-start.1 = ((bf16[16,240,128]{2,1,0:T(8,128)(2,1)}), bf16[16,240,128]{2,1,0:T(8,128)(2,1)S(1)}, u32[]{:S(2)}, u32[]{:S(2)}) async-start(bf16[16,240,128]{2,1,0:T(8,128)(2,1)} %get-tuple-element.18), calls=%async_computation.1 | async-start | bytes 1966080 | tf_op jit(solution)/shard_map/all_to_all | solution.py:323
  49.9 2.0 %collective-permute-start.3 = (bf16[896,512]{1,0:T(8,128)(2,1)}, bf16[896,512]{1,0:T(8,128)(2,1)}, u32[]{:S(2)}, u32[]{:S(2)}) collective-permute-start(bf16[896,512]{1,0:T(8,128)(2,1)} %shard_map.89), channel_id=1, source_target_pairs={{0,32},{32,0},{1,33},{33,1},{2,34},{34,2},{3,35},{35,3},{4,36},{36... | collective-permute-start | bytes 2752520 | tf_op jit(solution)/shard_map/ppermute | solution.py:263
  51.9 1.9 %collective-permute-start.4 = (bf16[192,512]{1,0:T(8,128)(2,1)S(1)}, bf16[192,512]{1,0:T(8,128)(2,1)S(1)}, u32[]{:S(2)}, u32[]{:S(2)}) collective-permute-start(bf16[192,512]{1,0:T(8,128)(2,1)S(1)} %shard_map.90), channel_id=1, source_target_pairs={{0,16},{16,0},{1,17},{17,1},{2,18},{18,2},{3,19},{19,3},{4,20},{20... | collective-permute-start | bytes 589832 | tf_op jit(solution)/shard_map/ppermute | solution.py:263
  53.8 15.4 %all-to-all-done.1.refs_0_ = bf16[16,240,128]{2,1,0:T(8,128)(2,1)S(1)} async-done(((bf16[16,240,128]{2,1,0:T(8,128)(2,1)}), bf16[16,240,128]{2,1,0:T(8,128)(2,1)S(1)}, u32[]{:S(2)}, u32[]{:S(2)}) %all-to-all-start.1) | async-done | bytes 983072 | tf_op jit(solution)/shard_map/all_to_all | solution.py:323
  70.1 4.9 %all-to-all-start.2 = ((bf16[8,240,128]{2,1,0:T(8,128)(2,1)}), bf16[8,240,128]{2,1,0:T(8,128)(2,1)S(1)}, u32[]{:S(2)}, u32[]{:S(2)}) async-start(bf16[8,240,128]{2,1,0:T(8,128)(2,1)} %get-tuple-element.19), calls=%async_computation.2 | async-start | bytes 983040 | tf_op jit(solution)/shard_map/all_to_all | solution.py:329
  75.0 4.4 %collective-permute-done.3.refs_0_ = bf16[896,512]{1,0:T(8,128)(2,1)} collective-permute-done((bf16[896,512]{1,0:T(8,128)(2,1)}, bf16[896,512]{1,0:T(8,128)(2,1)}, u32[]{:S(2)}, u32[]{:S(2)}) %collective-permute-start.3) | collective-permute-done | bytes 917536 | tf_op jit(solution)/shard_map/ppermute | solution.py:263
  79.5 1.9 %collective-permute-start.5 = (bf16[896,512]{1,0:T(8,128)(2,1)}, bf16[896,512]{1,0:T(8,128)(2,1)}, u32[]{:S(2)}, u32[]{:S(2)}) collective-permute-start(bf16[896,512]{1,0:T(8,128)(2,1)} %shard_map.91.refs_3_), channel_id=1, source_target_pairs={{0,16},{16,0},{1,17},{17,1},{2,18},{18,2},{3,19},{19,3},{4,20},{20... | collective-permute-start | bytes 2752520 | tf_op jit(solution)/shard_map/ppermute | solution.py:263
  81.4 8.2 %all-to-all-done.2.refs_0_.refs_2_ = bf16[8,240,128]{2,1,0:T(8,128)(2,1)S(1)} async-done(((bf16[8,240,128]{2,1,0:T(8,128)(2,1)}), bf16[8,240,128]{2,1,0:T(8,128)(2,1)S(1)}, u32[]{:S(2)}, u32[]{:S(2)}) %all-to-all-start.2) | async-done | bytes 491552 | tf_op jit(solution)/shard_map/all_to_all | solution.py:329
  89.5 3.2 %collective-permute-start.8 = (bf16[8,240,128]{2,1,0:T(8,128)(2,1)S(1)}, bf16[8,240,128]{2,1,0:T(8,128)(2,1)S(1)}, u32[]{:S(2)}, u32[]{:S(2)}) collective-permute-start(bf16[8,240,128]{2,1,0:T(8,128)(2,1)S(1)} %all-to-all-done.2.refs_0_.refs_2_), channel_id=1, source_target_pairs={{0,32},{32,0},{1,33},{33,1},{2,34},{34,2},{3,35},{35,3},{4,36},{36... | collective-permute-start | bytes 1474568 | tf_op jit(solution)/shard_map/ppermute | solution.py:263
  92.8 3.2 %shard_map.92 = bf16[16,48,128]{2,1,0:T(8,128)(2,1)} custom-call(bf16[8,240,128]{2,1,0:T(8,128)(2,1)S(1)} %all-to-all-done.2.refs_0_.refs_2_, bf16[512,896]{1,0:T(8,128)(2,1)S(1)} %shard_map.86.refs_1_.refs_0_, bf16[512,896]{1,0:T(8,128)(2,1)S(1)} %collective-permute-done.1.refs_2_, bf16[896,512]{1,0:T(8,128)(2,1)} %shard_map.91.refs_3_, ...), custom_call_target="tpu_custom_call" | custom-call | bytes 4358144 | tf_op jit(solution)/shard_map/pallas_call | solution.py:37
  95.9 5.4 %all-to-all-start.3 = ((bf16[16,48,128]{2,1,0:T(8,128)(2,1)}), bf16[16,48,128]{2,1,0:T(8,128)(2,1)S(1)}, u32[]{:S(2)}, u32[]{:S(2)}) async-start(bf16[16,48,128]{2,1,0:T(8,128)(2,1)} %shard_map.92), calls=%async_computation.3 | async-start | bytes 393216 | tf_op jit(solution)/shard_map/all_to_all | solution.py:346
  101.3 2.1 %collective-permute-start.7 = (bf16[8,240,128]{2,1,0:T(8,128)(2,1)S(1)}, bf16[8,240,128]{2,1,0:T(8,128)(2,1)S(1)}, u32[]{:S(2)}, u32[]{:S(2)}) collective-permute-start(bf16[8,240,128]{2,1,0:T(8,128)(2,1)S(1)} %all-to-all-done.2.refs_0_.refs_2_), channel_id=1, source_target_pairs={{0,16},{16,0},{1,17},{17,1},{2,18},{18,2},{3,19},{19,3},{4,20},{20... | collective-permute-start | bytes 1474568 | tf_op jit(solution)/shard_map/ppermute | solution.py:263
  103.4 2.4 %collective-permute-start.9 = (bf16[8,240,128]{2,1,0:T(8,128)(2,1)S(1)}, bf16[8,240,128]{2,1,0:T(8,128)(2,1)S(1)}, u32[]{:S(2)}, u32[]{:S(2)}) collective-permute-start(bf16[8,240,128]{2,1,0:T(8,128)(2,1)S(1)} %collective-permute-done.8.refs_4_), channel_id=1, source_target_pairs={{0,16},{16,0},{1,17},{17,1},{2,18},{18,2},{3,19},{19,3},{4,20},{20... | collective-permute-start | bytes 1474568 | tf_op jit(solution)/shard_map/ppermute | solution.py:263
  105.8 4.6 %all-to-all-done.3.refs_0_ = bf16[16,48,128]{2,1,0:T(8,128)(2,1)S(1)} async-done(((bf16[16,48,128]{2,1,0:T(8,128)(2,1)}), bf16[16,48,128]{2,1,0:T(8,128)(2,1)S(1)}, u32[]{:S(2)}, u32[]{:S(2)}) %all-to-all-start.3) | async-done | bytes 196640 | tf_op jit(solution)/shard_map/all_to_all | solution.py:346
  110.5 3.1 %collective-permute-start.6 = (bf16[11,512]{1,0:T(8,128)(2,1)S(1)}, bf16[11,512]{1,0:T(8,128)(2,1)S(1)}, u32[]{:S(2)}, u32[]{:S(2)}) collective-permute-start(bf16[11,512]{1,0:T(8,128)(2,1)S(1)} %shard_map.93), channel_id=1, source_target_pairs={{4,0},{13,1},{71,2},{72,3},{130,4},{139,5},{197,6},{206,7},{264,8}... | collective-permute-start | bytes 33800 | tf_op jit(solution)/shard_map/ppermute | solution.py:359
  113.6 1.9 %shard_map.94 = (bf16[256,896]{1,0:T(8,128)(2,1)}, bf16[256,896]{1,0:T(8,128)(2,1)}, bf16[896,256]{1,0:T(8,128)(2,1)}, f32[8,128]{1,0:T(8,128)S(1)}) custom-call(bf16[192,512]{1,0:T(8,128)(2,1)S(1)} %copy-done.1, bf16[192,512]{1,0:T(8,128)(2,1)S(1)} %collective-permute-done.4.refs_2_.refs_1_, bf16[8,240,128]{2,1,0:T(8,128)(2,1)S(1)} %all-to-all-done.2.refs_0_.refs_2_, ...), custom_call_target="tpu_custom_call" | custom-call | bytes 3735552 | tf_op jit(solution)/shard_map/pallas_call | solution.py:37
  115.5 5.4 %collective-permute-done.6.refs_0_ = bf16[11,512]{1,0:T(8,128)(2,1)S(1)} collective-permute-done((bf16[11,512]{1,0:T(8,128)(2,1)S(1)}, bf16[11,512]{1,0:T(8,128)(2,1)S(1)}, u32[]{:S(2)}, u32[]{:S(2)}) %collective-permute-start.6) | collective-permute-done | bytes 11296 | tf_op jit(solution)/shard_map/ppermute | solution.py:359
  (23 shorter events, 5.6 us)
Async XLA Ops:
  1.4 14.0 %collective-permute-start = (bf16[88,128]{1,0:T(8,128)(2,1)S(1)}, bf16[88,128]{1,0:T(8,128)(2,1)S(1)}, u32[]{:S(2)}, u32[]{:S(2)}) collective-permute-start(bf16[88,128]{1,0:T(8,128)(2,1)S(1)} %get-tuple-element.16), channel_id=1, source_target_pairs={{0,4},{1,45},{2,71},{3,104},{4,130},{5,171},{6,197},{7,238},{8,264... | collective-permute-start | bytes 67592 | tf_op jit(solution)/shard_map/ppermute | solution.py:296
  13.4 25.4 %collective-permute-start.1 = (bf16[512,896]{1,0:T(8,128)(2,1)S(1)}, bf16[512,896]{1,0:T(8,128)(2,1)S(1)}, u32[]{:S(2)}, u32[]{:S(2)}) collective-permute-start(bf16[512,896]{1,0:T(8,128)(2,1)S(1)} %shard_map.86.refs_1_.refs_0_), channel_id=1, source_target_pairs={{0,16},{16,0},{1,17},{17,1},{2,18},{18,2},{3,19},{19,3},{4,20},{20... | collective-permute-start | bytes 2752520 | tf_op jit(solution)/shard_map/ppermute | solution.py:263
  16.1 9.0 %copy-start = (bf16[896,256]{1,0:T(8,128)(2,1)S(1)}, bf16[896,256]{1,0:T(8,128)(2,1)}, u32[]{:S(2)}) copy-start(bf16[896,256]{1,0:T(8,128)(2,1)} %refs_3_.1) | copy-start | bytes 1376260
  16.2 22.7 %all-to-all-start = ((bf16[16,88,128]{2,1,0:T(8,128)(2,1)}), bf16[16,88,128]{2,1,0:T(8,128)(2,1)S(1)}, u32[]{:S(2)}, u32[]{:S(2)}) async-start(bf16[16,88,128]{2,1,0:T(8,128)(2,1)} %shard_map.85), calls=%async_computation | async-start | bytes 720896 | tf_op jit(solution)/shard_map/all_to_all | solution.py:298
  25.1 3.7 %collective-permute-start.2 = (bf16[896,256]{1,0:T(8,128)(2,1)S(1)}, bf16[896,256]{1,0:T(8,128)(2,1)S(1)}, u32[]{:S(2)}, u32[]{:S(2)}) collective-permute-start(bf16[896,256]{1,0:T(8,128)(2,1)S(1)} %copy-done), channel_id=1, source_target_pairs={{0,16},{16,0},{1,17},{17,1},{2,18},{18,2},{3,19},{19,3},{4,20},{20... | collective-permute-start | bytes 1376264 | tf_op jit(solution)/shard_map/ppermute | solution.py:263
  40.7 28.5 %all-to-all-start.1 = ((bf16[16,240,128]{2,1,0:T(8,128)(2,1)}), bf16[16,240,128]{2,1,0:T(8,128)(2,1)S(1)}, u32[]{:S(2)}, u32[]{:S(2)}) async-start(bf16[16,240,128]{2,1,0:T(8,128)(2,1)} %get-tuple-element.18), calls=%async_computation.1 | async-start | bytes 1966080 | tf_op jit(solution)/shard_map/all_to_all | solution.py:323
  48.6 3.2 %copy-start.2 = (bf16[192,512]{1,0:T(8,128)(2,1)S(1)}, bf16[192,512]{1,0:T(8,128)(2,1)}, u32[]{:S(2)}) copy-start(bf16[192,512]{1,0:T(8,128)(2,1)} %get-tuple-element.22.refs_0_) | copy-start | bytes 589828
  49.9 29.6 %collective-permute-start.3 = (bf16[896,512]{1,0:T(8,128)(2,1)}, bf16[896,512]{1,0:T(8,128)(2,1)}, u32[]{:S(2)}, u32[]{:S(2)}) collective-permute-start(bf16[896,512]{1,0:T(8,128)(2,1)} %shard_map.89), channel_id=1, source_target_pairs={{0,32},{32,0},{1,33},{33,1},{2,34},{34,2},{3,35},{35,3},{4,36},{36... | collective-permute-start | bytes 2752520 | tf_op jit(solution)/shard_map/ppermute | solution.py:263
  51.9 23.1 %collective-permute-start.4 = (bf16[192,512]{1,0:T(8,128)(2,1)S(1)}, bf16[192,512]{1,0:T(8,128)(2,1)S(1)}, u32[]{:S(2)}, u32[]{:S(2)}) collective-permute-start(bf16[192,512]{1,0:T(8,128)(2,1)S(1)} %shard_map.90), channel_id=1, source_target_pairs={{0,16},{16,0},{1,17},{17,1},{2,18},{18,2},{3,19},{19,3},{4,20},{20... | collective-permute-start | bytes 589832 | tf_op jit(solution)/shard_map/ppermute | solution.py:263
  70.1 19.4 %all-to-all-start.2 = ((bf16[8,240,128]{2,1,0:T(8,128)(2,1)}), bf16[8,240,128]{2,1,0:T(8,128)(2,1)S(1)}, u32[]{:S(2)}, u32[]{:S(2)}) async-start(bf16[8,240,128]{2,1,0:T(8,128)(2,1)} %get-tuple-element.19), calls=%async_computation.2 | async-start | bytes 983040 | tf_op jit(solution)/shard_map/all_to_all | solution.py:329
  79.5 13.3 %collective-permute-start.5 = (bf16[896,512]{1,0:T(8,128)(2,1)}, bf16[896,512]{1,0:T(8,128)(2,1)}, u32[]{:S(2)}, u32[]{:S(2)}) collective-permute-start(bf16[896,512]{1,0:T(8,128)(2,1)} %shard_map.91.refs_3_), channel_id=1, source_target_pairs={{0,16},{16,0},{1,17},{17,1},{2,18},{18,2},{3,19},{19,3},{4,20},{20... | collective-permute-start | bytes 2752520 | tf_op jit(solution)/shard_map/ppermute | solution.py:263
  89.5 13.9 %collective-permute-start.8 = (bf16[8,240,128]{2,1,0:T(8,128)(2,1)S(1)}, bf16[8,240,128]{2,1,0:T(8,128)(2,1)S(1)}, u32[]{:S(2)}, u32[]{:S(2)}) collective-permute-start(bf16[8,240,128]{2,1,0:T(8,128)(2,1)S(1)} %all-to-all-done.2.refs_0_.refs_2_), channel_id=1, source_target_pairs={{0,32},{32,0},{1,33},{33,1},{2,34},{34,2},{3,35},{35,3},{4,36},{36... | collective-permute-start | bytes 1474568 | tf_op jit(solution)/shard_map/ppermute | solution.py:263
  95.9 14.5 %all-to-all-start.3 = ((bf16[16,48,128]{2,1,0:T(8,128)(2,1)}), bf16[16,48,128]{2,1,0:T(8,128)(2,1)S(1)}, u32[]{:S(2)}, u32[]{:S(2)}) async-start(bf16[16,48,128]{2,1,0:T(8,128)(2,1)} %shard_map.92), calls=%async_computation.3 | async-start | bytes 393216 | tf_op jit(solution)/shard_map/all_to_all | solution.py:346
  101.3 12.3 %copy-start.1 = (bf16[192,512]{1,0:T(8,128)(2,1)S(1)}, bf16[192,512]{1,0:T(8,128)(2,1)}, u32[]{:S(2)}) copy-start(bf16[192,512]{1,0:T(8,128)(2,1)} %get-tuple-element.23.refs_0_) | copy-start | bytes 589828
  101.3 12.2 %collective-permute-start.7 = (bf16[8,240,128]{2,1,0:T(8,128)(2,1)S(1)}, bf16[8,240,128]{2,1,0:T(8,128)(2,1)S(1)}, u32[]{:S(2)}, u32[]{:S(2)}) collective-permute-start(bf16[8,240,128]{2,1,0:T(8,128)(2,1)S(1)} %all-to-all-done.2.refs_0_.refs_2_), channel_id=1, source_target_pairs={{0,16},{16,0},{1,17},{17,1},{2,18},{18,2},{3,19},{19,3},{4,20},{20... | collective-permute-start | bytes 1474568 | tf_op jit(solution)/shard_map/ppermute | solution.py:263
  103.4 10.2 %collective-permute-start.9 = (bf16[8,240,128]{2,1,0:T(8,128)(2,1)S(1)}, bf16[8,240,128]{2,1,0:T(8,128)(2,1)S(1)}, u32[]{:S(2)}, u32[]{:S(2)}) collective-permute-start(bf16[8,240,128]{2,1,0:T(8,128)(2,1)S(1)} %collective-permute-done.8.refs_4_), channel_id=1, source_target_pairs={{0,16},{16,0},{1,17},{17,1},{2,18},{18,2},{3,19},{19,3},{4,20},{20... | collective-permute-start | bytes 1474568 | tf_op jit(solution)/shard_map/ppermute | solution.py:263
  110.5 10.4 %collective-permute-start.6 = (bf16[11,512]{1,0:T(8,128)(2,1)S(1)}, bf16[11,512]{1,0:T(8,128)(2,1)S(1)}, u32[]{:S(2)}, u32[]{:S(2)}) collective-permute-start(bf16[11,512]{1,0:T(8,128)(2,1)S(1)} %shard_map.93), channel_id=1, source_target_pairs={{4,0},{13,1},{71,2},{72,3},{130,4},{139,5},{197,6},{206,7},{264,8}... | collective-permute-start | bytes 33800 | tf_op jit(solution)/shard_map/ppermute | solution.py:359
